TPU v7x, 32 devices: a whole 2x2x4 slice. The times are simulated.
32 devices in a mesh: group: 2 (over y), dom: 8 (over z, x), shot: 2 (over core).
Axes of the slice: x: 2, y: 2, z: 4, core: 2. Of those that a mesh axis runs over, the one named last changes fastest.
Arguments:
- checkpoint: float32 [4, 2, 64, 96, 256], P(('group', 'shot'), None, 'dom'), parts along dimension 0, may hold values from -6 to 6
- adjoint: float32 [4, 2, 64, 96, 256], P(('group', 'shot'), None, 'dom'), parts along dimension 0, may hold values from -6 to 6
- kappa: float32 [128, 128, 256], P(('group', 'dom')), parts along dimension 0, may hold values from 0.04 to 0.12
- buoyancy: float32 [128, 128, 256], P(('group', 'dom')), parts along dimension 0, may hold values from 0.5 to 2
- wavelet: float32 [1024], replicated, may hold values from 60 to 300
- src_cell: int32 [4], P(('group', 'shot')), parts along dimension 0, may hold values from 0 to 1572863
- rec_cell: int32 [4, 6400], P(('group', 'shot')), parts along dimension 0, may hold values from 0 to 1572863
- residuals: float32 [4, 2, 6400], P(('group', 'shot')), parts along dimension 0, may hold values from -64 to 64
- offsets: int32 [4], P(('group', 'shot')), parts along dimension 0, may hold values from 0 to 32
- ckpt_step: int32 [4], P(('group', 'shot')), parts along dimension 0, may hold values from 0 to 1023
Outputs:
- grad_kappa: float32 [128, 128, 256], P(('group', 'dom'), 'shot'), parts along dimension 0
- grad_buoy: float32 [128, 128, 256], P(('group', 'dom'), 'shot'), parts along dimension 0
- adjoint_next: float32 [4, 2, 64, 96, 256], P(('group', 'shot'), None, 'dom'), parts along dimension 0
There are 2 independent parts, one for each index of `group`. A program takes and returns all parts, laid end to end along the dimension named above; an argument that names none is the same for every part. Nothing has to cross between parts.
Inputs may be any that keep to these rules, and one draw needn't show every extreme that they name: `src_cell`: a flat cell of the shot's aperture. `rec_cell`: flat cells of the shot's aperture; several receivers may share a cell.
All inputs are finite; a program needn't handle non-finite values.
Results may differ from a plain program's by a relative error of at most 0.00011.
Values sent between devices are 32-bit elements; how exact they have to be, the bound alone decides.
No kernel may reach another device: no remote copies, remote signals or barrier semaphores. Data moves between devices by JAX's collectives and lax.ppermute only.
A program may use at most 64 MiB of HBM per device.

v0:
```python
import jax
import jax.numpy as jnp
from jax import lax
from jax.sharding import PartitionSpec as P


def extended(block, sides, width):
    for axis, dim in sides:
        count = lax.axis_size(axis)
        forward = [(i, i + 1) for i in range(count - 1)]
        backward = [(target, source) for source, target in forward]
        low = lax.ppermute(
            lax.slice_in_dim(block, block.shape[dim] - width, None, axis=dim), axis, forward
        )
        high = lax.ppermute(lax.slice_in_dim(block, 0, width, axis=dim), axis, backward)
        block = jnp.concatenate([low, block, high], axis=dim)
    return block


def view(padded, sx, sy, sz):
    rank = padded.ndim
    out = padded
    for axis, shift in ((rank - 3, sx), (rank - 2, sy), (rank - 1, sz)):
        count = padded.shape[axis] - 2
        out = lax.slice_in_dim(out, 1 + shift, 1 + shift + count, axis=axis)
    return out


def stencil(field_pad, buoy_pad):
    centre = view(field_pad, 0, 0, 0)
    bcentre = view(buoy_pad, 0, 0, 0)
    total = jnp.zeros_like(centre)
    for shifts in ((1, 0, 0), (-1, 0, 0), (0, 1, 0), (0, -1, 0), (0, 0, 1), (0, 0, -1)):
        face = 0.5 * (bcentre + view(buoy_pad, shifts[0], shifts[1], shifts[2]))
        total = total + face * (view(field_pad, shifts[0], shifts[1], shifts[2]) - centre)
    return total


def image_buoy(field_pad, adjoint_pad):
    pcentre = view(field_pad, 0, 0, 0)
    qcentre = view(adjoint_pad, 0, 0, 0)
    total = jnp.zeros_like(pcentre)
    for shifts in ((1, 0, 0), (0, 1, 0), (0, 0, 1)):
        total = total + (view(adjoint_pad, shifts[0], shifts[1], shifts[2]) - qcentre) * (
            view(field_pad, shifts[0], shifts[1], shifts[2]) - pcentre
        )
    return total


def pad_across(field):
    widths = [(0, 0)] * (field.ndim - 2) + [(1, 1), (1, 1)]
    return jnp.pad(field, widths)


def inject_source(field, cells, amps, dom_index):
    shots, width, ny, nz = field.shape
    local_cell = cells - dom_index * (width * ny * nz)
    cell_index = jnp.arange(width * ny * nz, dtype=jnp.int32).reshape(width, ny, nz)
    match = cell_index[None, :, :, :] == local_cell[:, None, None, None]
    return field + jnp.where(match, amps[:, None, None, None], 0.0)


def block_length(count):
    for size_try in range(min(count, 1600), 0, -1):
        if count % size_try == 0:
            return size_try
    return count


def inject_receivers(field, cells, values, dom_index):
    shots, width, ny, nz = field.shape
    plane = ny * nz
    count = cells.shape[1]
    length = block_length(count)
    blocks = count // length
    plane_rows = jnp.arange(width * ny, dtype=jnp.int32)
    depth_cols = jnp.arange(nz, dtype=jnp.int32)
    rows_x = cells[0] // plane
    local = rows_x - dom_index * width
    inside = (local >= 0) & (local < width)
    row_y = cells[0] // nz % ny
    depth = cells[0] % nz
    plane_row = jnp.where(inside, local * ny + row_y, -1)
    rows_blocks = plane_row.reshape(blocks, length)
    depth_blocks = depth.reshape(blocks, length)
    value_blocks = values[0].reshape(blocks, length)

    def add_block(total, pieces):
        rows_piece, depth_piece, value_piece = pieces
        left_hot = (plane_rows[:, None] == rows_piece[None, :]).astype(jnp.float32)
        right_val = jnp.where(
            depth_cols[None, :] == depth_piece[:, None], value_piece[:, None], 0.0
        )
        return (
            total
            + jnp.dot(
                left_hot,
                right_val,
                preferred_element_type=jnp.float32,
                precision=lax.Precision.HIGHEST,
            ),
            None,
        )

    start_total = jnp.zeros((width * ny, nz), jnp.float32)
    summed, unused = lax.scan(add_block, start_total, (rows_blocks, depth_blocks, value_blocks))
    results = [field[0] + summed.reshape(width, ny, nz)]
    return jnp.stack(results)


def shards(
    checkpoint, adjoint, kappa, buoyancy, wavelet, src_cell, rec_cell, residuals, offsets, ckpt_step
):
    width = checkpoint.shape[2]
    ny = checkpoint.shape[3]
    nz = checkpoint.shape[4]
    model_y = kappa.shape[1]
    dom_index = lax.axis_index("dom")
    buoy_rim = extended(buoyancy, (("dom", 0),), 1)
    kwin = jnp.stack(
        [lax.dynamic_slice(kappa, (jnp.int32(0), offsets[0], jnp.int32(0)), (width, ny, nz))]
    )
    bwin = jnp.stack(
        [lax.dynamic_slice(buoy_rim, (jnp.int32(0), offsets[0], jnp.int32(0)), (width + 2, ny, nz))]
    )
    buoy_pad = pad_across(bwin)
    p_old = checkpoint[:, 0]
    p_now = checkpoint[:, 1]
    q_late = adjoint[:, 0]
    q_now = adjoint[:, 1]
    kq_now = kwin * q_now
    p_rim = extended(p_now, (("dom", 1),), 1)
    kq_rim = extended(kq_now, (("dom", 1),), 1)
    p_pad = pad_across(p_rim)
    q_pad = pad_across(kq_rim)
    lap_now = stencil(p_pad, buoy_pad)
    samples = jnp.arange(wavelet.shape[0], dtype=jnp.int32)
    amp = jnp.sum(jnp.where(samples[None, :] == ckpt_step[:, None], wavelet[None, :], 0.0), axis=1)
    p_next = inject_source(2.0 * p_now - p_old + kwin * lap_now, src_cell, amp, dom_index)
    q_mid = inject_receivers(
        2.0 * q_now - q_late + stencil(q_pad, buoy_pad), rec_cell, residuals[:, 0], dom_index
    )
    kq_mid = kwin * q_mid
    pn_rim = extended(p_next, (("dom", 1),), 1)
    qm_rim = extended(kq_mid, (("dom", 1),), 1)
    pn_pad = pad_across(pn_rim)
    qm_pad = pad_across(qm_rim)
    lap_next = stencil(pn_pad, buoy_pad)
    q_last = inject_receivers(
        2.0 * q_mid - q_now + stencil(qm_pad, buoy_pad), rec_cell, residuals[:, 1], dom_index
    )
    part_k = q_mid * lap_now + q_now * lap_next
    part_b = -(image_buoy(p_pad, qm_pad) + image_buoy(pn_pad, q_pad))
    total_k = jnp.zeros((width, model_y, nz), jnp.float32)
    total_b = jnp.zeros((width, model_y, nz), jnp.float32)
    start = (jnp.int32(0), offsets[0], jnp.int32(0))
    total_k = lax.dynamic_update_slice(total_k, part_k[0], start)
    total_b = lax.dynamic_update_slice(total_b, part_b[0], start)
    summed_k, summed_b = lax.psum((total_k, total_b), "shot")
    share = model_y // lax.axis_size("shot")
    first = lax.axis_index("shot") * share
    grad_k = lax.dynamic_slice_in_dim(summed_k, first, share, 1)
    grad_b = lax.dynamic_slice_in_dim(summed_b, first, share, 1)
    return (grad_k, grad_b, jnp.stack([q_mid, q_last], axis=1))


def solution(mesh):
    in_specs = (
        P(("group", "shot"), None, "dom", None, None),
        P(("group", "shot"), None, "dom", None, None),
        P(("group", "dom"), None, None),
        P(("group", "dom"), None, None),
        P(),
        P(("group", "shot")),
        P(("group", "shot"), None),
        P(("group", "shot"), None, None),
        P(("group", "shot")),
        P(("group", "shot")),
    )
    out_specs = (
        P(("group", "dom"), "shot", None),
        P(("group", "dom"), "shot", None),
        P(("group", "shot"), None, "dom", None, None),
    )
    return jax.shard_map(shards, mesh=mesh, in_specs=in_specs, out_specs=out_specs, check_vma=False)
```

profile of v0, /device:TPU:12, one launch (start us, length us, event | category | flops | bytes accessed | tf_op | source)
XLA Modules:
  0.0 132.4 jit_solution(14146751852195065648)
XLA Ops:
  7.9 1.6 %fusion.95 = f32[1,8,96,256]{3,2,1,0:T(8,128)S(1)} fusion(f32[8,128,256]{2,1,0:T(8,128)} %param.16, s32[]{:T(128)S(6)} %select_n.69, f32[1,2,8,96,256]{4,3,2,1,0:T(8,128)} %param.15), kind=kLoop, calls=%fused_computation.148 | loop fusion | flops 196608 | bytes 2359300 | tf_op jit(solution)/shard_map/mul | solution.py:131
  9.6 3.3 %collective-permute-start.2 = (f32[1,1,96,256]{3,2,1,0:T(8,128)S(1)}, f32[1,1,96,256]{3,2,1,0:T(8,128)S(1)}, u32[]{:S(2)}, u32[]{:S(2)}) collective-permute-start(f32[1,1,96,256]{3,2,1,0:T(8,128)S(1)} %get-tuple-element.170), channel_id=1, source_target_pairs={{2,0},{4,2},{6,4},{8,6},{10,8},{12,10},{14,12},{3,1},{5,3},{7,5},{... | collective-permute-start | bytes 294920 | tf_op jit(solution)/shard_map/ppermute | solution.py:15
  12.8 2.6 %collective-permute-start.3 = (f32[1,1,96,256]{3,2,1,0:T(8,128)S(1)}, f32[1,1,96,256]{3,2,1,0:T(8,128)S(1)}, u32[]{:S(2)}, u32[]{:S(2)}) collective-permute-start(f32[1,1,96,256]{3,2,1,0:T(8,128)S(1)} %get-tuple-element.169), channel_id=1, source_target_pairs={{0,2},{2,4},{4,6},{6,8},{8,10},{10,12},{12,14},{1,3},{3,5},{5,7},{... | collective-permute-start | bytes 294920 | tf_op jit(solution)/shard_map/ppermute | solution.py:12
  15.4 1.0 fusion.109
  16.4 4.3 %collective-permute-start = (f32[1,128,256]{2,1,0:T(8,128)S(1)}, f32[1,128,256]{2,1,0:T(8,128)S(1)}, u32[]{:S(2)}, u32[]{:S(2)}) collective-permute-start(f32[1,128,256]{2,1,0:T(8,128)S(1)} %get-tuple-element.162), channel_id=1, source_target_pairs={{0,2},{2,4},{4,6},{6,8},{8,10},{10,12},{12,14},{1,3},{3,5},{5,7},{... | collective-permute-start | bytes 393224 | tf_op jit(solution)/shard_map/ppermute | solution.py:12
  20.7 2.4 %collective-permute-start.1 = (f32[1,128,256]{2,1,0:T(8,128)S(1)}, f32[1,128,256]{2,1,0:T(8,128)S(1)}, u32[]{:S(2)}, u32[]{:S(2)}) collective-permute-start(f32[1,128,256]{2,1,0:T(8,128)S(1)} %get-tuple-element.161), channel_id=1, source_target_pairs={{2,0},{4,2},{6,4},{8,6},{10,8},{12,10},{14,12},{3,1},{5,3},{7,5},{... | collective-permute-start | bytes 393224 | tf_op jit(solution)/shard_map/ppermute | solution.py:15
  23.2 0.7 fusion.112
  24.0 3.3 %collective-permute-start.4 = (f32[1,1,96,256]{3,2,1,0:T(8,128)}, f32[1,1,96,256]{3,2,1,0:T(8,128)S(1)}, u32[]{:S(2)}, u32[]{:S(2)}) collective-permute-start(f32[1,1,96,256]{3,2,1,0:T(8,128)} %get-tuple-element.168), channel_id=1, source_target_pairs={{2,0},{4,2},{6,4},{8,6},{10,8},{12,10},{14,12},{3,1},{5,3},{7,5},{... | collective-permute-start | bytes 294920 | tf_op jit(solution)/shard_map/ppermute | solution.py:15
  27.4 0.1 squeeze.53
  27.5 1.0 slice_reduce_fusion
  28.6 0.1 add_select_fusion
  28.7 12.6 %while.22 = (s32[]{:T(128)}, f32[768,256]{1,0:T(8,128)S(1)}, s32[4,1600]{1,0:T(4,128)S(1)}, s32[4,1600]{1,0:T(4,128)S(1)}, f32[4,1600]{1,0:T(4,128)S(1)}, /*index=5*/s32[]{:T(128)}, s32[]{:T(128)}) while((s32[]{:T(128)}, f32[768,256]{1,0:T(8,128)S(1)}, s32[4,1600]{1,0:T(4,128)S(1)}, s32[4,1600]{1,0:T(4,128)S(1)}, ...), condition=%wide.region_1.2_spmd.clone, body=%wide.region_0.1_spmd.clone.sunk | while | flops 3777314816 | bytes 1630559 | solution.py:106
  28.8 3.0 %fusion.119 = f32[768,256]{1,0:T(8,128)S(1)} fusion(s32[1600]{0:T(1024)S(1)} %get-tuple-element.236, f32[1600]{0:T(1024)S(1)} %dynamic-slice_reduce_fusion.11, s32[1600]{0:T(1024)S(1)} %get-tuple-element.237, f32[768,256]{1,0:T(8,128)S(1)} %get-tuple-element.253, pred[]{:T(512)S(6)} %compare.130), kind=kOutput, calls=%fused_computation.9.clone.1 | convolution fusion | flops 3777314816 | bytes 1592065 | tf_op jit(solution)/shard_map/while/body/eval_jaxpr/dot_general | solution.py:96
  32.0 3.0 %fusion.119 = f32[768,256]{1,0:T(8,128)S(1)} fusion(s32[1600]{0:T(1024)S(1)} %get-tuple-element.236, f32[1600]{0:T(1024)S(1)} %dynamic-slice_reduce_fusion.11, s32[1600]{0:T(1024)S(1)} %get-tuple-element.237, f32[768,256]{1,0:T(8,128)S(1)} %get-tuple-element.253, pred[]{:T(512)S(6)} %compare.130), kind=kOutput, calls=%fused_computation.9.clone.1 | convolution fusion | flops 3777314816 | bytes 1592065 | tf_op jit(solution)/shard_map/while/body/eval_jaxpr/dot_general | solution.py:96
  35.1 3.0 %fusion.119 = f32[768,256]{1,0:T(8,128)S(1)} fusion(s32[1600]{0:T(1024)S(1)} %get-tuple-element.236, f32[1600]{0:T(1024)S(1)} %dynamic-slice_reduce_fusion.11, s32[1600]{0:T(1024)S(1)} %get-tuple-element.237, f32[768,256]{1,0:T(8,128)S(1)} %get-tuple-element.253, pred[]{:T(512)S(6)} %compare.130), kind=kOutput, calls=%fused_computation.9.clone.1 | convolution fusion | flops 3777314816 | bytes 1592065 | tf_op jit(solution)/shard_map/while/body/eval_jaxpr/dot_general | solution.py:96
  38.2 3.0 %fusion.119 = f32[768,256]{1,0:T(8,128)S(1)} fusion(s32[1600]{0:T(1024)S(1)} %get-tuple-element.236, f32[1600]{0:T(1024)S(1)} %dynamic-slice_reduce_fusion.11, s32[1600]{0:T(1024)S(1)} %get-tuple-element.237, f32[768,256]{1,0:T(8,128)S(1)} %get-tuple-element.253, pred[]{:T(512)S(6)} %compare.130), kind=kOutput, calls=%fused_computation.9.clone.1 | convolution fusion | flops 3777314816 | bytes 1592065 | tf_op jit(solution)/shard_map/while/body/eval_jaxpr/dot_general | solution.py:96
  42.6 0.7 select_reduce_fusion
  43.3 2.5 %collective-permute-start.5 = (f32[1,1,96,256]{3,2,1,0:T(8,128)}, f32[1,1,96,256]{3,2,1,0:T(8,128)S(1)}, u32[]{:S(2)}, u32[]{:S(2)}) collective-permute-start(f32[1,1,96,256]{3,2,1,0:T(8,128)} %get-tuple-element.167), channel_id=1, source_target_pairs={{0,2},{2,4},{4,6},{6,8},{8,10},{10,12},{12,14},{1,3},{3,5},{5,7},{... | collective-permute-start | bytes 294920 | tf_op jit(solution)/shard_map/ppermute | solution.py:12
  45.8 0.5 select_maximum_fusion.6
  46.4 4.5 %collective-permute-done.5 = f32[1,1,96,256]{3,2,1,0:T(8,128)S(1)} collective-permute-done((f32[1,1,96,256]{3,2,1,0:T(8,128)}, f32[1,1,96,256]{3,2,1,0:T(8,128)S(1)}, u32[]{:S(2)}, u32[]{:S(2)}) %collective-permute-start.5) | collective-permute-done | bytes 98336 | tf_op jit(solution)/shard_map/ppermute | solution.py:12
  50.9 0.5 select_maximum_fusion.4
  51.4 0.1 fusion.33
  51.6 1.2 copy-done.14
  52.8 2.4 %bitcast_add_fusion = (f32[1,1,8,96,256]{4,3,2,1,0:T(8,128)}, f32[1,8,96,256]{3,2,1,0:T(8,128)S(1)}, f32[1,8,96,256]{3,2,1,0:T(8,128)S(1)}, f32[1,8,96,256]{3,2,...) fusion(f32[1,1,8,96,256]{4,3,2,1,0:T(8,128)S(1)} %bitcast.78, ...), kind=kLoop, calls=%fused_computation.139 | loop fusion | flops 6881280 | bytes 16121856 | tf_op jit(solution)/shard_map/add | solution.py:107
  55.2 0.2 fusion.92
  55.4 2.2 %collective-permute-start.8 = (f32[1,1,96,256]{3,2,1,0:T(8,128)S(1)}, f32[1,1,96,256]{3,2,1,0:T(8,128)S(1)}, u32[]{:S(2)}, u32[]{:S(2)}) collective-permute-start(f32[1,1,96,256]{3,2,1,0:T(8,128)S(1)} %get-tuple-element.164), channel_id=1, source_target_pairs={{2,0},{4,2},{6,4},{8,6},{10,8},{12,10},{14,12},{3,1},{5,3},{7,5},{... | collective-permute-start | bytes 294920 | tf_op jit(solution)/shard_map/ppermute | solution.py:15
  57.6 3.9 %collective-permute-start.9 = (f32[1,1,96,256]{3,2,1,0:T(8,128)S(1)}, f32[1,1,96,256]{3,2,1,0:T(8,128)S(1)}, u32[]{:S(2)}, u32[]{:S(2)}) collective-permute-start(f32[1,1,96,256]{3,2,1,0:T(8,128)S(1)} %get-tuple-element.163), channel_id=1, source_target_pairs={{0,2},{2,4},{4,6},{6,8},{8,10},{10,12},{12,14},{1,3},{3,5},{5,7},{... | collective-permute-start | bytes 294920 | tf_op jit(solution)/shard_map/ppermute | solution.py:12
  61.6 2.8 %fusion.94 = (f32[1,8,96,256]{3,2,1,0:T(8,128)S(1)}, f32[1,8,96,256]{3,2,1,0:T(8,128)}) fusion(f32[1,2,8,96,256]{4,3,2,1,0:T(8,128)S(1)} %copy-done.16, f32[8,128,256]{2,1,0:T(8,128)S(1)} %copy-done.1, s32[]{:T(128)S(6)} %select_n.69, f32[]{:T(128)} %select_reduce_fusion, s32[]{:T(128)} %bitcast.11, f32[1,8,96,256]{3,2,1,0:T(8,128)S(1)} %get-tuple-element.154, ...), kind=kLoop, calls=%fused_computation.145 | loop fusion | flops 5898240 | bytes 12779532 | tf_op jit(solution)/shard_map/add | solution.py:60
  64.4 2.8 %collective-permute-start.6 = (f32[1,1,96,256]{3,2,1,0:T(8,128)S(1)}, f32[1,1,96,256]{3,2,1,0:T(8,128)S(1)}, u32[]{:S(2)}, u32[]{:S(2)}) collective-permute-start(f32[1,1,96,256]{3,2,1,0:T(8,128)S(1)} %get-tuple-element.166), channel_id=1, source_target_pairs={{2,0},{4,2},{6,4},{8,6},{10,8},{12,10},{14,12},{3,1},{5,3},{7,5},{... | collective-permute-start | bytes 294920 | tf_op jit(solution)/shard_map/ppermute | solution.py:15
  67.2 3.2 %collective-permute-start.7 = (f32[1,1,96,256]{3,2,1,0:T(8,128)S(1)}, f32[1,1,96,256]{3,2,1,0:T(8,128)S(1)}, u32[]{:S(2)}, u32[]{:S(2)}) collective-permute-start(f32[1,1,96,256]{3,2,1,0:T(8,128)S(1)} %get-tuple-element.165), channel_id=1, source_target_pairs={{0,2},{2,4},{4,6},{6,8},{8,10},{10,12},{12,14},{1,3},{3,5},{5,7},{... | collective-permute-start | bytes 294920 | tf_op jit(solution)/shard_map/ppermute | solution.py:12
  70.5 0.6 copy-done.21
  71.1 0.5 select_maximum_fusion
  71.6 3.0 %collective-permute-done.7 = f32[1,1,96,256]{3,2,1,0:T(8,128)S(1)} collective-permute-done((f32[1,1,96,256]{3,2,1,0:T(8,128)S(1)}, f32[1,1,96,256]{3,2,1,0:T(8,128)S(1)}, u32[]{:S(2)}, u32[]{:S(2)}) %collective-permute-start.7) | collective-permute-done | bytes 98336 | tf_op jit(solution)/shard_map/ppermute | solution.py:12
  74.6 0.5 select_maximum_fusion.2
  75.2 3.0 %negate_bitcast_fusion = f32[8,96,256]{2,1,0:T(8,128)} fusion(f32[1,8,96,256]{3,2,1,0:T(8,128)S(1)} %copy-done.3, f32[1,1,96,256]{3,2,1,0:T(8,128)S(1)} %collective-permute-done.2, f32[1,8,96,256]{3,2,1,0:T(8,128)S(1)} %copy-done.7, f32[1,1,96,256]{3,2,1,0:T(8,128)S(1)} %copy-done.20, f32[1,8,96,256]{3,2,1,0:T(8,128)S(1)} %get-tuple-element.155, ...), kind=kLoop, calls=%fused_computation.152 | loop fusion | flops 5898240 | bytes 12976132 | tf_op jit(solution)/shard_map/squeeze | solution.py:158
  78.1 1.1 broadcast.137.clone.1
  79.2 4.7 %dynamic_update_slice.7 = f32[8,128,256]{2,1,0:T(8,128)} dynamic-update-slice(f32[8,128,256]{2,1,0:T(8,128)} %broadcast.137.clone.1, f32[8,96,256]{2,1,0:T(8,128)} %negate_bitcast_fusion, s32[]{:T(128)} %constant.91.clone.1, s32[]{:T(128)S(6)} %select_n.69, s32[]{:T(128)} %constant.91.clone.1) | dynamic-update-slice | bytes 1572868 | tf_op jit(solution)/shard_map/dynamic_update_slice | solution.py:158
  83.9 7.5 %fusion.59 = f32[8,96,256]{2,1,0:T(8,128)} fusion(f32[1,8,96,256]{3,2,1,0:T(8,128)} %copy-done.13, f32[1,8,96,256]{3,2,1,0:T(8,128)} %copy-done.5, f32[1,10,98,258]{3,2,1,0:T(8,128)} %copy-done, f32[1,8,96,256]{3,2,1,0:T(8,128)} %copy-done.12, f32[1,8,96,256]{3,2,1,0:T(8,128)} %copy-done.11, f32[1,1,96,256]{3,2,1,0:T(8,128)S(1)} %copy-done.24, ...), kind=kLoop, calls=%fused_computation.88 | loop fusion | flops 4521984 | bytes 12779520 | tf_op jit(solution)/shard_map/squeeze | solution.py:157
  91.4 1.1 broadcast.137.clone
  92.5 4.7 %dynamic_update_slice.6 = f32[8,128,256]{2,1,0:T(8,128)} dynamic-update-slice(f32[8,128,256]{2,1,0:T(8,128)} %broadcast.137.clone, f32[8,96,256]{2,1,0:T(8,128)} %fusion.59, s32[]{:T(128)} %constant.91.clone.1, s32[]{:T(128)S(6)} %select_n.69, s32[]{:T(128)} %constant.91.clone.1) | dynamic-update-slice | bytes 1572868 | tf_op jit(solution)/shard_map/dynamic_update_slice | solution.py:157
  97.3 19.2 %while.23 = (s32[]{:T(128)}, f32[768,256]{1,0:T(8,128)}, s32[4,1600]{1,0:T(4,128)S(1)}, s32[4,1600]{1,0:T(4,128)S(1)}, f32[4,1600]{1,0:T(4,128)S(1)}, /*index=5*/s32[]{:T(128)}, s32[]{:T(128)}) while((s32[]{:T(128)}, f32[768,256]{1,0:T(8,128)}, s32[4,1600]{1,0:T(4,128)S(1)}, s32[4,1600]{1,0:T(4,128)S(1)}, f32[4,1600]{1,0:T(4,128)S(1)}, ...), condition=%wide.region_6.7_spmd.clone, body=%wide.region_5.6_spmd.clone.sunk | while | flops 3777314816 | bytes 1630559 | solution.py:106
  97.4 3.8 %fusion.121 = f32[768,256]{1,0:T(8,128)} fusion(s32[1600]{0:T(1024)S(1)} %get-tuple-element.243, f32[1600]{0:T(1024)S(1)} %dynamic-slice_reduce_fusion.13, s32[1600]{0:T(1024)S(1)} %get-tuple-element.244, f32[768,256]{1,0:T(8,128)} %get-tuple-element.274, pred[]{:T(512)S(6)} %compare.131), kind=kOutput, calls=%fused_computation.22.clone.1 | convolution fusion | flops 3777314816 | bytes 1592065 | tf_op jit(solution)/shard_map/while/body/eval_jaxpr/dot_general | solution.py:96
  101.3 5.0 %fusion.121 = f32[768,256]{1,0:T(8,128)} fusion(s32[1600]{0:T(1024)S(1)} %get-tuple-element.243, f32[1600]{0:T(1024)S(1)} %dynamic-slice_reduce_fusion.13, s32[1600]{0:T(1024)S(1)} %get-tuple-element.244, f32[768,256]{1,0:T(8,128)} %get-tuple-element.274, pred[]{:T(512)S(6)} %compare.131), kind=kOutput, calls=%fused_computation.22.clone.1 | convolution fusion | flops 3777314816 | bytes 1592065 | tf_op jit(solution)/shard_map/while/body/eval_jaxpr/dot_general | solution.py:96
  106.4 5.0 %fusion.121 = f32[768,256]{1,0:T(8,128)} fusion(s32[1600]{0:T(1024)S(1)} %get-tuple-element.243, f32[1600]{0:T(1024)S(1)} %dynamic-slice_reduce_fusion.13, s32[1600]{0:T(1024)S(1)} %get-tuple-element.244, f32[768,256]{1,0:T(8,128)} %get-tuple-element.274, pred[]{:T(512)S(6)} %compare.131), kind=kOutput, calls=%fused_computation.22.clone.1 | convolution fusion | flops 3777314816 | bytes 1592065 | tf_op jit(solution)/shard_map/while/body/eval_jaxpr/dot_general | solution.py:96
  111.5 5.0 %fusion.121 = f32[768,256]{1,0:T(8,128)} fusion(s32[1600]{0:T(1024)S(1)} %get-tuple-element.243, f32[1600]{0:T(1024)S(1)} %dynamic-slice_reduce_fusion.13, s32[1600]{0:T(1024)S(1)} %get-tuple-element.244, f32[768,256]{1,0:T(8,128)} %get-tuple-element.274, pred[]{:T(512)S(6)} %compare.131), kind=kOutput, calls=%fused_computation.22.clone.1 | convolution fusion | flops 3777314816 | bytes 1592065 | tf_op jit(solution)/shard_map/while/body/eval_jaxpr/dot_general | solution.py:96
  116.5 5.6 %fusion.46 = f32[1,1,8,96,256]{4,3,2,1,0:T(8,128)S(1)} fusion(f32[1,1,8,96,256]{4,3,2,1,0:T(8,128)} %bitcast.84, f32[1,8,96,256]{3,2,1,0:T(8,128)} %copy-done.13, f32[1,8,96,256]{3,2,1,0:T(8,128)} %copy-done.4, f32[1,10,98,258]{3,2,1,0:T(8,128)S(1)} %select_maximum_fusion, f32[1,8,96,256]{3,2,1,0:T(8,128)} %copy-done.12, f32[1,8,96,256]{3,2,1,0:T(8,128)} %copy-done.11, ...), kind=kLoop, calls=%fused_computation.69 | loop fusion | flops 5111808 | bytes 14352388 | tf_op jit(solution)/shard_map/add | solution.py:107
  122.1 1.2 pad_maximum_fusion
  123.3 2.3 %constant_dynamic-slice_fusion = (f32[8,64,256]{2,1,0:T(8,128)}, f32[8,64,256]{2,1,0:T(8,128)}) fusion(f32[8,128,256]{2,1,0:T(8,128)} %get-tuple-element.146, s32[]{:T(128)S(6)} %select_n.77, f32[8,128,256]{2,1,0:T(8,128)} %get-tuple-element.145), kind=kLoop, calls=%fused_computation.174 | loop fusion | bytes 2097156 | tf_op jit(solution)/shard_map/dynamic_slice | solution.py:163
  (88 shorter events, 1.1 us)
Async XLA Ops:
  7.2 116.1 %all-reduce.8.cloned.1.call-start = ((), (), s32[]{:S(2)}) async-start(), calls=%async_computation | async-start | bytes 4194304 | tf_op jit(solution)/shard_map/psum | solution.py:159
  7.9 15.3 %copy-start.15 = (f32[1,2,8,96,256]{4,3,2,1,0:T(8,128)S(1)}, f32[1,2,8,96,256]{4,3,2,1,0:T(8,128)}, u32[]{:S(2)}) copy-start(f32[1,2,8,96,256]{4,3,2,1,0:T(8,128)} %param.14) | copy-start | bytes 4718596
  9.5 42.0 %copy-start.2 = (f32[1,8,96,256]{3,2,1,0:T(8,128)}, f32[1,8,96,256]{3,2,1,0:T(8,128)S(1)}, u32[]{:S(2)}) copy-start(f32[1,8,96,256]{3,2,1,0:T(8,128)S(1)} %fusion.95) | copy-start | bytes 2359300
  9.5 17.8 %copy-start.25 = (s32[1,6400]{1,0:T(1,128)S(1)}, s32[1,6400]{1,0:T(1,128)}, u32[]{:S(2)}) copy-start(s32[1,6400]{1,0:T(1,128)} %param.20) | copy-start | bytes 76804
  9.6 33.7 %collective-permute-start.2 = (f32[1,1,96,256]{3,2,1,0:T(8,128)S(1)}, f32[1,1,96,256]{3,2,1,0:T(8,128)S(1)}, u32[]{:S(2)}, u32[]{:S(2)}) collective-permute-start(f32[1,1,96,256]{3,2,1,0:T(8,128)S(1)} %get-tuple-element.170), channel_id=1, source_target_pairs={{2,0},{4,2},{6,4},{8,6},{10,8},{12,10},{14,12},{3,1},{5,3},{7,5},{... | collective-permute-start | bytes 294920 | tf_op jit(solution)/shard_map/ppermute | solution.py:15
  12.8 33.0 %collective-permute-start.3 = (f32[1,1,96,256]{3,2,1,0:T(8,128)S(1)}, f32[1,1,96,256]{3,2,1,0:T(8,128)S(1)}, u32[]{:S(2)}, u32[]{:S(2)}) collective-permute-start(f32[1,1,96,256]{3,2,1,0:T(8,128)S(1)} %get-tuple-element.169), channel_id=1, source_target_pairs={{0,2},{2,4},{4,6},{6,8},{8,10},{10,12},{12,14},{1,3},{3,5},{5,7},{... | collective-permute-start | bytes 294920 | tf_op jit(solution)/shard_map/ppermute | solution.py:12
  16.4 35.0 %collective-permute-start = (f32[1,128,256]{2,1,0:T(8,128)S(1)}, f32[1,128,256]{2,1,0:T(8,128)S(1)}, u32[]{:S(2)}, u32[]{:S(2)}) collective-permute-start(f32[1,128,256]{2,1,0:T(8,128)S(1)} %get-tuple-element.162), channel_id=1, source_target_pairs={{0,2},{2,4},{4,6},{6,8},{8,10},{10,12},{12,14},{1,3},{3,5},{5,7},{... | collective-permute-start | bytes 393224 | tf_op jit(solution)/shard_map/ppermute | solution.py:12
  20.7 30.7 %collective-permute-start.1 = (f32[1,128,256]{2,1,0:T(8,128)S(1)}, f32[1,128,256]{2,1,0:T(8,128)S(1)}, u32[]{:S(2)}, u32[]{:S(2)}) collective-permute-start(f32[1,128,256]{2,1,0:T(8,128)S(1)} %get-tuple-element.161), channel_id=1, source_target_pairs={{2,0},{4,2},{6,4},{8,6},{10,8},{12,10},{14,12},{3,1},{5,3},{7,5},{... | collective-permute-start | bytes 393224 | tf_op jit(solution)/shard_map/ppermute | solution.py:15
  23.2 38.3 %copy-start.6 = (f32[1,8,96,256]{3,2,1,0:T(8,128)}, f32[1,8,96,256]{3,2,1,0:T(8,128)S(1)}, u32[]{:S(2)}) copy-start(f32[1,8,96,256]{3,2,1,0:T(8,128)S(1)} %slice_bitcast_fusion) | copy-start | bytes 2359300
  24.0 22.4 %collective-permute-start.4 = (f32[1,1,96,256]{3,2,1,0:T(8,128)}, f32[1,1,96,256]{3,2,1,0:T(8,128)S(1)}, u32[]{:S(2)}, u32[]{:S(2)}) collective-permute-start(f32[1,1,96,256]{3,2,1,0:T(8,128)} %get-tuple-element.168), channel_id=1, source_target_pairs={{2,0},{4,2},{6,4},{8,6},{10,8},{12,10},{14,12},{3,1},{5,3},{7,5},{... | collective-permute-start | bytes 294920 | tf_op jit(solution)/shard_map/ppermute | solution.py:15
  28.7 13.9 %copy-start.26 = (f32[1024]{0:T(1024)S(1)}, f32[1024]{0:T(1024)}, u32[]{:S(2)}) copy-start(f32[1024]{0:T(1024)} %param.18) | copy-start | bytes 12292
  43.3 7.6 %collective-permute-start.5 = (f32[1,1,96,256]{3,2,1,0:T(8,128)}, f32[1,1,96,256]{3,2,1,0:T(8,128)S(1)}, u32[]{:S(2)}, u32[]{:S(2)}) collective-permute-start(f32[1,1,96,256]{3,2,1,0:T(8,128)} %get-tuple-element.167), channel_id=1, source_target_pairs={{0,2},{2,4},{4,6},{6,8},{8,10},{10,12},{12,14},{1,3},{3,5},{5,7},{... | collective-permute-start | bytes 294920 | tf_op jit(solution)/shard_map/ppermute | solution.py:12
  46.3 5.1 %copy-start.18 = (f32[8,128,256]{2,1,0:T(8,128)S(1)}, f32[8,128,256]{2,1,0:T(8,128)}, u32[]{:S(2)}) copy-start(f32[8,128,256]{2,1,0:T(8,128)} %param.17) | copy-start | bytes 3145732
  46.3 15.2 %copy-start.19 = (f32[1,1,96,256]{3,2,1,0:T(8,128)}, f32[1,1,96,256]{3,2,1,0:T(8,128)S(1)}, u32[]{:S(2)}) copy-start(f32[1,1,96,256]{3,2,1,0:T(8,128)S(1)} %collective-permute-done.4) | copy-start | bytes 294916
  51.4 1.4 %copy-start.14 = (f32[1,2,8,96,256]{4,3,2,1,0:T(8,128)S(1)}, f32[1,2,8,96,256]{4,3,2,1,0:T(8,128)}, u32[]{:S(2)}) copy-start(f32[1,2,8,96,256]{4,3,2,1,0:T(8,128)} %param.15) | copy-start | bytes 4718596
  52.8 2.4 %copy-start.1 = (f32[8,128,256]{2,1,0:T(8,128)S(1)}, f32[8,128,256]{2,1,0:T(8,128)}, u32[]{:S(2)}) copy-start(f32[8,128,256]{2,1,0:T(8,128)} %param.16) | copy-start | bytes 3145732
  55.1 6.4 %copy-start.8 = (f32[1,8,96,256]{3,2,1,0:T(8,128)}, f32[1,8,96,256]{3,2,1,0:T(8,128)S(1)}, u32[]{:S(2)}) copy-start(f32[1,8,96,256]{3,2,1,0:T(8,128)S(1)} %get-tuple-element.149) | copy-start | bytes 2359300
  55.1 6.4 %copy-start.9 = (f32[1,8,96,256]{3,2,1,0:T(8,128)}, f32[1,8,96,256]{3,2,1,0:T(8,128)S(1)}, u32[]{:S(2)}) copy-start(f32[1,8,96,256]{3,2,1,0:T(8,128)S(1)} %get-tuple-element.150) | copy-start | bytes 2359300
  55.1 6.4 %copy-start.10 = (f32[1,8,96,256]{3,2,1,0:T(8,128)}, f32[1,8,96,256]{3,2,1,0:T(8,128)S(1)}, u32[]{:S(2)}) copy-start(f32[1,8,96,256]{3,2,1,0:T(8,128)S(1)} %get-tuple-element.151) | copy-start | bytes 2359300
  55.1 6.4 %copy-start.11 = (f32[1,8,96,256]{3,2,1,0:T(8,128)}, f32[1,8,96,256]{3,2,1,0:T(8,128)S(1)}, u32[]{:S(2)}) copy-start(f32[1,8,96,256]{3,2,1,0:T(8,128)S(1)} %get-tuple-element.152) | copy-start | bytes 2359300
  55.1 9.2 %copy-start.12 = (f32[1,8,96,256]{3,2,1,0:T(8,128)}, f32[1,8,96,256]{3,2,1,0:T(8,128)S(1)}, u32[]{:S(2)}) copy-start(f32[1,8,96,256]{3,2,1,0:T(8,128)S(1)} %get-tuple-element.153) | copy-start | bytes 2359300
  55.2 9.2 %copy-start.13 = (f32[1,8,96,256]{3,2,1,0:T(8,128)}, f32[1,8,96,256]{3,2,1,0:T(8,128)S(1)}, u32[]{:S(2)}) copy-start(f32[1,8,96,256]{3,2,1,0:T(8,128)S(1)} %get-tuple-element.154) | copy-start | bytes 2359300
  55.2 6.4 %copy-start.16 = (f32[1,2,8,96,256]{4,3,2,1,0:T(8,128)S(1)}, f32[1,2,8,96,256]{4,3,2,1,0:T(8,128)}, u32[]{:S(2)}) copy-start(f32[1,2,8,96,256]{4,3,2,1,0:T(8,128)} %param.14) | copy-start | bytes 4718596
  55.4 19.8 %copy-start.4 = (f32[1,8,96,256]{3,2,1,0:T(8,128)}, f32[1,8,96,256]{3,2,1,0:T(8,128)S(1)}, u32[]{:S(2)}) copy-start(f32[1,8,96,256]{3,2,1,0:T(8,128)S(1)} %fusion.92) | copy-start | bytes 2359300
  55.4 15.0 %collective-permute-start.8 = (f32[1,1,96,256]{3,2,1,0:T(8,128)S(1)}, f32[1,1,96,256]{3,2,1,0:T(8,128)S(1)}, u32[]{:S(2)}, u32[]{:S(2)}) collective-permute-start(f32[1,1,96,256]{3,2,1,0:T(8,128)S(1)} %get-tuple-element.164), channel_id=1, source_target_pairs={{2,0},{4,2},{6,4},{8,6},{10,8},{12,10},{14,12},{3,1},{5,3},{7,5},{... | collective-permute-start | bytes 294920 | tf_op jit(solution)/shard_map/ppermute | solution.py:15
  57.6 12.8 %collective-permute-start.9 = (f32[1,1,96,256]{3,2,1,0:T(8,128)S(1)}, f32[1,1,96,256]{3,2,1,0:T(8,128)S(1)}, u32[]{:S(2)}, u32[]{:S(2)}) collective-permute-start(f32[1,1,96,256]{3,2,1,0:T(8,128)S(1)} %get-tuple-element.163), channel_id=1, source_target_pairs={{0,2},{2,4},{4,6},{6,8},{8,10},{10,12},{12,14},{1,3},{3,5},{5,7},{... | collective-permute-start | bytes 294920 | tf_op jit(solution)/shard_map/ppermute | solution.py:12
  64.4 10.8 %copy-start.5 = (f32[1,8,96,256]{3,2,1,0:T(8,128)}, f32[1,8,96,256]{3,2,1,0:T(8,128)S(1)}, u32[]{:S(2)}) copy-start(f32[1,8,96,256]{3,2,1,0:T(8,128)S(1)} %get-tuple-element.155) | copy-start | bytes 2359300
  64.4 7.2 %collective-permute-start.6 = (f32[1,1,96,256]{3,2,1,0:T(8,128)S(1)}, f32[1,1,96,256]{3,2,1,0:T(8,128)S(1)}, u32[]{:S(2)}, u32[]{:S(2)}) collective-permute-start(f32[1,1,96,256]{3,2,1,0:T(8,128)S(1)} %get-tuple-element.166), channel_id=1, source_target_pairs={{2,0},{4,2},{6,4},{8,6},{10,8},{12,10},{14,12},{3,1},{5,3},{7,5},{... | collective-permute-start | bytes 294920 | tf_op jit(solution)/shard_map/ppermute | solution.py:15
  67.2 7.4 %collective-permute-start.7 = (f32[1,1,96,256]{3,2,1,0:T(8,128)S(1)}, f32[1,1,96,256]{3,2,1,0:T(8,128)S(1)}, u32[]{:S(2)}, u32[]{:S(2)}) collective-permute-start(f32[1,1,96,256]{3,2,1,0:T(8,128)S(1)} %get-tuple-element.165), channel_id=1, source_target_pairs={{0,2},{2,4},{4,6},{6,8},{8,10},{10,12},{12,14},{1,3},{3,5},{5,7},{... | collective-permute-start | bytes 294920 | tf_op jit(solution)/shard_map/ppermute | solution.py:12
  70.4 0.6 copy-start.21
  71.6 3.6 %copy-start.3 = (f32[1,8,96,256]{3,2,1,0:T(8,128)S(1)}, f32[1,8,96,256]{3,2,1,0:T(8,128)}, u32[]{:S(2)}) copy-start(f32[1,8,96,256]{3,2,1,0:T(8,128)} %copy-done.2) | copy-start | bytes 2359300
  71.6 3.6 %copy-start.7 = (f32[1,8,96,256]{3,2,1,0:T(8,128)S(1)}, f32[1,8,96,256]{3,2,1,0:T(8,128)}, u32[]{:S(2)}) copy-start(f32[1,8,96,256]{3,2,1,0:T(8,128)} %copy-done.6) | copy-start | bytes 2359300
  71.6 3.6 %copy-start.20 = (f32[1,1,96,256]{3,2,1,0:T(8,128)S(1)}, f32[1,1,96,256]{3,2,1,0:T(8,128)}, u32[]{:S(2)}) copy-start(f32[1,1,96,256]{3,2,1,0:T(8,128)} %copy-done.19) | copy-start | bytes 294916
  74.6 3.5 %copy-start.23 = (f32[1,1,96,256]{3,2,1,0:T(8,128)}, f32[1,1,96,256]{3,2,1,0:T(8,128)S(1)}, u32[]{:S(2)}) copy-start(f32[1,1,96,256]{3,2,1,0:T(8,128)S(1)} %collective-permute-done.7) | copy-start | bytes 294916
  75.2 3.0 %copy-start = (f32[1,10,98,258]{3,2,1,0:T(8,128)}, f32[1,10,98,258]{3,2,1,0:T(8,128)S(1)}, u32[]{:S(2)}) copy-start(f32[1,10,98,258]{3,2,1,0:T(8,128)S(1)} %select_maximum_fusion.2) | copy-start | bytes 3034084
  79.2 4.7 %copy-start.24 = (f32[1,1,96,256]{3,2,1,0:T(8,128)S(1)}, f32[1,1,96,256]{3,2,1,0:T(8,128)}, u32[]{:S(2)}) copy-start(f32[1,1,96,256]{3,2,1,0:T(8,128)} %copy-done.23) | copy-start | bytes 294916
  97.3 19.2 %copy-start.22 = (f32[1,1,96,256]{3,2,1,0:T(8,128)S(1)}, f32[1,1,96,256]{3,2,1,0:T(8,128)}, u32[]{:S(2)}) copy-start(f32[1,1,96,256]{3,2,1,0:T(8,128)} %copy-done.21) | copy-start | bytes 294916
  116.5 5.6 %copy-start.17 = (f32[1,1,8,96,256]{4,3,2,1,0:T(8,128)S(1)}, f32[1,1,8,96,256]{4,3,2,1,0:T(8,128)}, u32[]{:S(2)}) copy-start(f32[1,1,8,96,256]{4,3,2,1,0:T(8,128)} %get-tuple-element.147) | copy-start | bytes 2359300
Sparse Core Ops, SparseCore 0:
  97.3 21.7 all-reduce.7
where the time goes:
time: 133 us; the launch traced here: 132 us
  matrix products  30.9 us (23%)
  starting transfers between devices  30.6 us (23%)
  other arithmetic  27.2 us (20%)
  local copies, waits for them, and re-layouts  19.5 us (15%)
  between operations  16.6 us (12%)
  waiting for transfers between devices  7.53 us (6%)
    dot_general x8, matrix products, add_block(): jnp.dot(left_hot, right_val, preferred_element_type=jnp.float32, precisio...  30.9 us
    ppermute x5, starting transfers between devices, extended(): lax.ppermute(lax.slice_in_dim(block, block.shape[dim] - width, None, axis...  16.5 us
    ppermute x5, starting transfers between devices, extended(): lax.ppermute(lax.slice_in_dim(block, 0, width, axis=dim), axis, backward)  14 us
    add x2, other arithmetic, inject_receivers(): results = [field[0] + summed.reshape(width, ny, nz)]  7.92 us
    ppermute x5, waiting for transfers between devices, extended(): lax.ppermute(lax.slice_in_dim(block, block.shape[dim] - width, None, axis...  7.5 us
    squeeze x1, other arithmetic, shards(): total_k = lax.dynamic_update_slice(total_k, part_k[0], start)  7.49 us
    dynamic_update_slice x1, local copies, waits for them, and re-layouts, shards(): total_k = lax.dynamic_update_slice(total_k, part_k[0], start)  4.71 us
    dynamic_update_slice x1, local copies, waits for them, and re-layouts, shards(): total_b = lax.dynamic_update_slice(total_b, part_b[0], start)  4.7 us
  transfers between devices with their start and end apart: 11, of which 2 were waited for; matrix products, arithmetic and copies ran while one was open for 35% of the time, Pallas kernels for 0%

commit v1 on v0

v1 whole, which is shorter than its diff:
```python
import functools

import jax
import jax.numpy as jnp
from jax import lax
from jax.experimental import pallas as pl
from jax.experimental.pallas import tpu as pltpu
from jax.sharding import PartitionSpec as P

F32 = jnp.float32
BF16 = jnp.bfloat16
LANES = 128
GROUP_ROWS = 5

VM = pl.BlockSpec(memory_space=pltpu.VMEM)
SM = pl.BlockSpec(memory_space=pltpu.SMEM)
ANY = pl.BlockSpec(memory_space=pl.ANY)


def vmem(*shape):
    return pltpu.VMEM(shape, F32)


def keep(x):
    return pltpu.with_memory_space_constraint(x, pltpu.VMEM)


def params():
    return pltpu.CompilerParams(vmem_limit_bytes=24 * 1024 * 1024)


def edges(width):
    even = lax.rem(lax.axis_index("dom"), 2) == 0
    last = jnp.int32(width - 1)
    first = jnp.int32(0)
    return jnp.where(even, last, first), jnp.where(even, first, last)


def window(block, off, ny):
    rows = block.shape[0]
    return pltpu.roll(block, lax.rem(rows - off, rows), 0)[:ny]


def placed(plane, off, rows):
    fill = jnp.zeros((rows - plane.shape[0], plane.shape[1]), plane.dtype)
    return pltpu.roll(jnp.concatenate([plane, fill], axis=0), off, 0)


def up(v, axis):
    return pltpu.roll(v, v.shape[axis] - 1, axis)


def down(v, axis):
    return pltpu.roll(v, 1, axis)


def first_send(off, ckpt, adj, kappa, buoy, send_b, send_a, q_e, k_e, b_e, sem):
    width, ny, nz = ckpt.shape[2:]
    edge_a, edge_b = edges(width)
    copies = []
    for n, (edge, send) in enumerate(((edge_b, send_b), (edge_a, send_a))):
        copies.append(
            (
                pltpu.make_async_copy(ckpt.at[0, 1, edge], send.at[0], sem.at[n, 0]),
                pltpu.make_async_copy(adj.at[0, 1, edge], q_e.at[n], sem.at[n, 1]),
                pltpu.make_async_copy(kappa.at[edge], k_e.at[n], sem.at[n, 2]),
                pltpu.make_async_copy(buoy.at[edge], b_e.at[n], sem.at[n, 3]),
            )
        )
    for group in copies:
        for copy in group:
            copy.start()
    for n, send in enumerate((send_b, send_a)):
        for copy in copies[n]:
            copy.wait()
        send[1] = window(k_e[n], off[0], ny) * q_e[n]
        send[2] = window(b_e[n], off[0], ny)


def receivers(rec, res, total, cells0, nz, rank_s, row_a_s, row_b_s, z_s, val_s, left, right_hi, right_lo):
    rows, lanes = rec.shape
    cells = left.shape[0] * nz
    shift = nz.bit_length() - 1
    local = rec[...] - cells0
    inside = (local >= 0) & (local < cells)
    row = lax.shift_right_logical(local, jnp.int32(shift))
    row_a_s[...] = lax.shift_right_logical(row, jnp.int32(2)).astype(F32)
    row_b_s[...] = (row & 3).astype(F32)
    z_s[...] = (local & (nz - 1)).astype(F32)
    for step in range(2):
        value = res[step]
        high = value.astype(BF16).astype(F32)
        val_s[2 * step] = high
        val_s[2 * step + 1] = value - high
    mask = jnp.where(inside, 1.0, 0.0).astype(BF16)
    before = lax.broadcasted_iota(jnp.int32, (lanes, lanes), 0) < lax.broadcasted_iota(
        jnp.int32, (lanes, lanes), 1
    )
    in_row = jnp.dot(mask, jnp.where(before, 1.0, 0.0).astype(BF16), preferred_element_type=F32)
    row_sum = jnp.dot(mask, jnp.ones((lanes, lanes), BF16), preferred_element_type=F32)
    r = lax.broadcasted_iota(jnp.int32, (rows, rows), 0)
    c = lax.broadcasted_iota(jnp.int32, (rows, rows), 1)
    group_r = lax.shift_right_logical(r * 3277, jnp.int32(14))
    group_c = lax.shift_right_logical(c * 3277, jnp.int32(14))
    earlier = jnp.where((group_r == group_c) & (c < r), 1.0, 0.0).astype(BF16)
    row_start = jnp.dot(earlier, row_sum.astype(BF16), preferred_element_type=F32)
    rank = jnp.where(inside, in_row + row_start, -1.0)
    rank_s[...] = rank
    passes = lax.shift_right_logical(jnp.max(rank).astype(jnp.int32), jnp.int32(7)) + 1
    passes = jnp.maximum(passes, 1)
    groups = rows // GROUP_ROWS
    slot = lax.broadcasted_iota(jnp.int32, (LANES, lanes), 0).astype(F32)
    sub8 = lax.broadcasted_iota(jnp.int32, (8, lanes), 0)
    row_iota = lax.broadcasted_iota(jnp.int32, (left.shape[0], LANES), 0).astype(F32)
    depth_iota = lax.broadcasted_iota(jnp.int32, (LANES, nz), 1).astype(F32)

    def one_pass(number, first):
        base = (number * LANES).astype(F32) if not isinstance(number, int) else float(number * LANES)
        for g in range(groups):
            picks = []
            fields = []
            for n in range(GROUP_ROWS):
                at = pl.ds(g * GROUP_ROWS + n, 1)
                want = jnp.broadcast_to(rank_s[at, :] - base, (LANES, lanes))
                picks.append(jnp.where(want == slot, 1.0, 0.0).astype(BF16))
                data = jnp.zeros((8, lanes), F32)
                sources = [row_a_s, row_b_s, z_s] + [val_s.at[m] for m in range(4)]
                for m, source in enumerate(sources):
                    data = jnp.where(sub8 == m, jnp.broadcast_to(source[at, :], (8, lanes)), data)
                fields.append(data.astype(BF16))
            pick = jnp.concatenate(picks, axis=1)
            data = jnp.concatenate(fields, axis=1)
            dims = (((1,), (1,)), ((), ()))
            by_slot = lax.dot_general(pick, data, dims, preferred_element_type=F32)
            by_field = lax.dot_general(data, pick, dims, preferred_element_type=F32)
            where_row = by_field[0:1, :] * 4.0 + by_field[1:2, :]
            here = pl.ds(g * LANES, LANES)
            left[:, here] = jnp.where(row_iota == where_row, 1.0, 0.0).astype(BF16)
            same = by_slot[:, 2:3] == depth_iota
            for step in range(2):
                cols = pl.ds(step * nz, nz)
                right_hi[here, cols] = jnp.where(same, by_slot[:, 3 + 2 * step : 4 + 2 * step], 0.0).astype(BF16)
                right_lo[here, cols] = jnp.where(same, by_slot[:, 4 + 2 * step : 5 + 2 * step], 0.0).astype(BF16)
        out = jnp.dot(left[...], right_hi[...], preferred_element_type=F32) + jnp.dot(
            left[...], right_lo[...], preferred_element_type=F32
        )
        if first:
            total[...] = out
        else:
            total[...] += out

    one_pass(0, True)

    @pl.when(passes > 1)
    def _():
        def body(number, carry):
            one_pass(number, False)
            return carry

        lax.fori_loop(1, passes, body, 0)


def lap_plane(f, f_next, gx_last, hx, fy, fz, dg):
    gx = hx * (f_next - f)
    gy = fy * (up(f, 0) - f)
    gz = fz * (up(f, 1) - f)
    out = (gx - gx_last) + (gy - down(gy, 0)) + (gz - down(gz, 1)) - dg * f
    return out, gx


def step_one(
    off, step, src, wav, rec, res, ckpt, adj, kappa, buoy, after,
    p, q, kq, kw, hb, fy_o, fz_o, dg_o, lap, pn, qm, total,
    p_old, q_late, k_full, b_full, count, gx_p, gx_q,
    rank_s, row_a_s, row_b_s, z_s, val_s, left, right_hi, right_lo, sem,
):
    width, ny, nz = p.shape
    copies = [
        pltpu.make_async_copy(source, target, sem.at[n])
        for n, (source, target) in enumerate(
            (
                (kappa, k_full), (buoy, b_full), (adj.at[0, 1], q), (ckpt.at[0, 1], p),
                (ckpt.at[0, 0], p_old), (adj.at[0, 0], q_late),
            )
        )
    ]
    for copy in copies:
        copy.start()
    cells0 = lax.axis_index("dom") * (width * ny * nz)
    receivers(rec, res, total, cells0, nz, rank_s, row_a_s, row_b_s, z_s, val_s, left, right_hi, right_lo)
    ys = lax.broadcasted_iota(jnp.int32, (ny, nz), 0)
    zs = lax.broadcasted_iota(jnp.int32, (ny, nz), 1)
    end_y = (ys == 0) | (ys == ny - 1)
    end_z = (zs == 0) | (zs == nz - 1)
    count[...] = jnp.where(end_y, 1.0, 0.0) + jnp.where(end_z, 1.0, 0.0)
    gx_p[...] = jnp.zeros((ny, nz), F32)
    gx_q[...] = jnp.zeros((ny, nz), F32)
    for copy in copies:
        copy.wait()

    def windows(x, carry):
        k = window(k_full[x], off[0], ny)
        kw[x] = k
        kq[x] = k * q[x]
        hb[x] = 0.5 * window(b_full[x], off[0], ny)
        return carry

    lax.fori_loop(0, width, windows, 0)

    def plane(x, carry):
        xn = jnp.minimum(x + 1, width - 1)
        h = hb[x]
        hx = h + hb[xn]
        fy = jnp.where(ys == ny - 1, 0.0, h + up(h, 0))
        fz = jnp.where(zs == nz - 1, 0.0, h + up(h, 1))
        dg = h * count[...]
        fy_o[x] = fy
        fz_o[x] = fz
        dg_o[x] = dg
        here = p[x]
        lap_p, gx = lap_plane(here, p[xn], gx_p[...], hx, fy, fz, dg)
        gx_p[...] = gx
        lap[x] = lap_p
        pn[x] = 2.0 * here - p_old[x] + kw[x] * lap_p
        lap_q, gx = lap_plane(kq[x], kq[xn], gx_q[...], hx, fy, fz, dg)
        gx_q[...] = gx
        at = pl.ds(pl.multiple_of(x * ny, 8), ny)
        qm[x] = 2.0 * q[x] - q_late[x] + lap_q + total[at, 0:nz]
        return carry

    lax.fori_loop(0, width, plane, 0)
    cell = src[0] - cells0

    @pl.when((cell >= 0) & (cell < width * ny * nz))
    def _():
        shift = nz.bit_length() - 1
        row = lax.shift_right_logical(cell, jnp.int32(shift))
        x = lax.div(row, jnp.int32(ny))
        y = row - x * ny
        spot = lax.broadcasted_iota(jnp.int32, (1, nz), 1) == (cell & (nz - 1))
        pn[x, pl.ds(y, 1), :] += jnp.where(spot, wav[step[0]], 0.0)


def edge_one(which, recv, p, kq, kw, hb, lap, pn, qm, send, kept):
    edge = edges(p.shape[0])[which]
    face = hb[edge] + 0.5 * recv[2]
    flux = face * (recv[0] - p[edge])
    kept[0] = lap[edge] + flux
    k = kw[edge]
    send[0] = pn[edge] + k * flux
    mid = qm[edge] + face * (recv[1] - kq[edge])
    kept[1] = mid
    send[1] = k * mid


def step_two(
    off, send_a, kept_a, send_b, kept_b, p, q, kq, kw, hb, fy_i, fz_i, dg_i, lap_i, pn_i, qm_i, total,
    adj_out, last_e, mine, other,
    pn, qm, kqm, last, g_full, gx_s, sem,
):
    width, ny, nz = p.shape
    half = mine.shape[2]
    edge_a, edge_b = edges(width)
    ys = lax.broadcasted_iota(jnp.int32, (ny, nz), 0)
    zs = lax.broadcasted_iota(jnp.int32, (ny, nz), 1)
    gx_s[...] = jnp.zeros(gx_s.shape, F32)

    def gather(x, carry):
        pn[x] = pn_i[x]
        mid = qm_i[x]
        qm[x] = mid
        kqm[x] = kw[x] * mid
        return carry

    lax.fori_loop(0, width, gather, 0)
    for edge, send, kept in ((edge_a, send_a, kept_a), (edge_b, send_b, kept_b)):
        pn[edge] = send[0]
        kqm[edge] = send[1]
        qm[edge] = kept[1]
    mid_copy = pltpu.make_async_copy(qm, adj_out.at[0, 0], sem.at[0])
    mid_copy.start()
    model_y = g_full.shape[2]

    def plane(x, carry):
        xn = jnp.minimum(x + 1, width - 1)
        hx = hb[x] + hb[xn]
        fy = fy_i[x]
        fz = fz_i[x]
        dg = dg_i[x]

        def diffs(ref):
            f = ref[x]
            return f, ref[xn] - f, up(f, 0) - f, up(f, 1) - f

        def lap(d, slot):
            f, dx, dy, dz = d
            gx = hx * dx
            gy = fy * dy
            gz = fz * dz
            out = (gx - gx_s[slot]) + (gy - down(gy, 0)) + (gz - down(gz, 1)) - dg * f
            gx_s[slot] = gx
            return out

        dpn = diffs(pn)
        lap2 = lap(dpn, 0)
        dqm = diffs(kqm)
        at = pl.ds(pl.multiple_of(x * ny, 8), ny)
        last[x] = 2.0 * qm[x] - q[x] + lap(dqm, 1) + total[at, nz : 2 * nz]
        lap1 = jnp.where(x == edge_a, kept_a[0], jnp.where(x == edge_b, kept_b[0], lap_i[x]))
        g_full[0, x] = placed(qm[x] * lap1 + q[x] * lap2, off[0], model_y)
        dp = diffs(p)
        dq = diffs(kq)
        prod = [a * b + c * d for a, b, c, d in zip(dp, dqm, dpn, dq)]
        gb = prod[1]
        gb += jnp.where(ys == ny - 1, prod[0], prod[2])
        gb += jnp.where(zs == nz - 1, prod[0], prod[3])
        g_full[1, x] = placed(-gb, off[0], model_y)
        return carry

    lax.fori_loop(0, width, plane, 0)
    last_copy = pltpu.make_async_copy(last, adj_out.at[0, 1], sem.at[1])
    last_copy.start()
    last_e[0] = last[edge_a]
    last_e[1] = last[edge_b]
    shot = lax.axis_index("shot")
    own = pl.ds(pl.multiple_of(shot * half, 8), half)
    far = pl.ds(pl.multiple_of((1 - shot) * half, 8), half)
    for g in range(2):
        mine[g] = g_full[g, :, own, :]
        other[g] = g_full[g, :, far, :]
    mid_copy.wait()
    last_copy.wait()


def edge_two(
    off, recv_a, recv_b, recv2_a, recv2_b, send_a, send_b, p, q, kq, hb, last_e, adj_in,
    adj_out, mine, other, full, ql, sem,
):
    width, ny, nz = p.shape
    half = mine.shape[1]
    which = edges(width)
    model_y = full.shape[1]
    full[2] = jnp.zeros(full.shape[1:], F32)
    copies = []
    for n, (recv, recv2, send) in enumerate(((recv_a, recv2_a, send_a), (recv_b, recv2_b, send_b))):
        edge = which[n]
        face = hb[edge] + 0.5 * recv[2]
        dpn = recv2[0] - send[0]
        dqm = recv2[1] - send[1]
        ql[n] = last_e[n] + face * dqm
        copy = pltpu.make_async_copy(ql.at[n], adj_out.at[0, 1, edge], sem.at[n])
        copy.start()
        copies.append(copy)
        slot = jnp.where(edge == width - 1, 1, 0)
        full[slot] = placed(q[edge] * (face * dpn), off[0], model_y)

        @pl.when(edge == width - 1)
        def _():
            full[2] = placed(-(dqm * (recv[0] - p[edge]) + dpn * (recv[1] - kq[edge])), off[0], model_y)

    shot = lax.axis_index("shot")
    mine[...] = full[:, pl.ds(pl.multiple_of(shot * half, 8), half), :]
    other[...] = full[:, pl.ds(pl.multiple_of((1 - shot) * half, 8), half), :]
    for copy in copies:
        copy.wait()


def combine(mine, recv, mine_e, recv_e, grad_k, grad_b):
    width = grad_k.shape[0]
    grad_k[...] = mine[0] + recv[0]
    grad_b[...] = mine[1] + recv[1]
    grad_k[0] += mine_e[0] + recv_e[0]
    grad_k[width - 1] += mine_e[1] + recv_e[1]
    grad_b[width - 1] += mine_e[2] + recv_e[2]


def pairs(count, first):
    out = []
    for low in range(first, count - 1, 2):
        out += [(low, low + 1), (low + 1, low)]
    return out


def shards(
    checkpoint, adjoint, kappa, buoyancy, wavelet, src_cell, rec_cell, residuals, offsets, ckpt_step
):
    width, ny, nz = checkpoint.shape[2:]
    model_y = kappa.shape[1]
    half = model_y // 2
    count = lax.axis_size("dom")
    pairs_a = pairs(count, 0)
    pairs_b = pairs(count, 1)
    nrec = rec_cell.shape[1]
    rrows = nrec // LANES
    groups = rrows // GROUP_ROWS
    slots = groups * LANES
    layer = (ny, nz)
    field = (width, ny, nz)
    dma = pltpu.SemaphoreType.DMA

    send_b, send_a = pl.pallas_call(
        first_send,
        in_specs=[SM, ANY, ANY, ANY, ANY],
        out_specs=[VM, VM],
        out_shape=[vmem(3, *layer)] * 2,
        scratch_shapes=[vmem(2, *layer), vmem(2, model_y, nz), vmem(2, model_y, nz), dma((2, 4))],
        compiler_params=params(),
    )(offsets, checkpoint, adjoint, kappa, buoyancy)
    recv_b = lax.ppermute(send_b, "dom", pairs_b)
    recv_a = lax.ppermute(send_a, "dom", pairs_a)

    p, q, kq, kw, hb, fy, fz, dg, lap, pn, qm, total = pl.pallas_call(
        step_one,
        in_specs=[SM, SM, SM, SM, VM, VM, ANY, ANY, ANY, ANY, ANY],
        out_specs=[VM] * 12,
        out_shape=[vmem(*field)] * 11 + [vmem(width * ny, 2 * nz)],
        scratch_shapes=[
            vmem(*field), vmem(*field), vmem(width, model_y, nz), vmem(width, model_y, nz),
            vmem(*layer), vmem(*layer), vmem(*layer),
            vmem(rrows, LANES), vmem(rrows, LANES), vmem(rrows, LANES), vmem(rrows, LANES),
            vmem(4, rrows, LANES),
            pltpu.VMEM((width * ny, slots), BF16),
            pltpu.VMEM((slots, 2 * nz), BF16),
            pltpu.VMEM((slots, 2 * nz), BF16),
            dma((6,)),
        ],
        compiler_params=params(),
        cost_estimate=pl.CostEstimate(flops=10_000_000_000, bytes_accessed=6_000_000, transcendentals=0),
    )(
        offsets, ckpt_step, src_cell, wavelet,
        rec_cell.reshape(rrows, LANES), residuals.reshape(2, rrows, LANES),
        checkpoint, adjoint, kappa, buoyancy, send_a,
    )

    def first_edge(which, recv):
        return pl.pallas_call(
            functools.partial(edge_one, which),
            in_specs=[VM] * 8,
            out_specs=[VM, VM],
            out_shape=[vmem(2, *layer)] * 2,
            compiler_params=params(),
        )(keep(recv), keep(p), keep(kq), keep(kw), keep(hb), keep(lap), keep(pn), keep(qm))

    send2_b, kept_b = first_edge(1, recv_b)
    recv2_b = lax.ppermute(send2_b, "dom", pairs_b)
    send2_a, kept_a = first_edge(0, recv_a)
    recv2_a = lax.ppermute(send2_a, "dom", pairs_a)

    adj_part, last_e, mine, other = pl.pallas_call(
        step_two,
        in_specs=[SM] + [VM] * 16,
        out_specs=[ANY, VM, VM, VM],
        out_shape=[
            jax.ShapeDtypeStruct((1, 2, *field), F32),
            vmem(2, *layer),
            vmem(2, width, half, nz),
            vmem(2, width, half, nz),
        ],
        scratch_shapes=[
            vmem(*field), vmem(*field), vmem(*field), vmem(*field),
            vmem(2, width, model_y, nz), vmem(2, *layer), dma((2,)),
        ],
        compiler_params=params(),
        cost_estimate=pl.CostEstimate(flops=6_000_000_000, bytes_accessed=2_000_000, transcendentals=0),
    )(
        offsets,
        *[keep(v) for v in (send2_a, kept_a, send2_b, kept_b, p, q, kq, kw, hb, fy, fz, dg, lap, pn, qm, total)],
    )
    swap = [(0, 1), (1, 0)]
    recv_g = lax.ppermute(other, "shot", swap)

    adj_next, mine_e, other_e = pl.pallas_call(
        edge_two,
        in_specs=[SM] + [VM] * 11 + [ANY],
        out_specs=[ANY, VM, VM],
        out_shape=[
            jax.ShapeDtypeStruct((1, 2, *field), F32),
            vmem(3, half, nz),
            vmem(3, half, nz),
        ],
        scratch_shapes=[vmem(3, model_y, nz), vmem(2, *layer), dma((2,))],
        input_output_aliases={12: 0},
        compiler_params=params(),
    )(
        offsets,
        *[keep(v) for v in (recv_a, recv_b, recv2_a, recv2_b, send2_a, send2_b, p, q, kq, hb, last_e)],
        adj_part,
    )
    recv_e = lax.ppermute(other_e, "shot", swap)
    grad_k, grad_b = pl.pallas_call(
        combine,
        in_specs=[VM] * 4,
        out_specs=[VM, VM],
        out_shape=[jax.ShapeDtypeStruct((width, half, nz), F32)] * 2,
        compiler_params=params(),
    )(keep(mine), keep(recv_g), keep(mine_e), keep(recv_e))
    return grad_k, grad_b, adj_next


def solution(mesh):
    in_specs = (
        P(("group", "shot"), None, "dom", None, None),
        P(("group", "shot"), None, "dom", None, None),
        P(("group", "dom"), None, None),
        P(("group", "dom"), None, None),
        P(),
        P(("group", "shot")),
        P(("group", "shot"), None),
        P(("group", "shot"), None, None),
        P(("group", "shot")),
        P(("group", "shot")),
    )
    out_specs = (
        P(("group", "dom"), "shot", None),
        P(("group", "dom"), "shot", None),
        P(("group", "shot"), None, "dom", None, None),
    )
    return jax.shard_map(shards, mesh=mesh, in_specs=in_specs, out_specs=out_specs, check_vma=False)
```

time: 133 us -> 52.8 us (0.40)
  the two profiles are of different devices: /device:TPU:12 before, /device:TPU:9 now
where the time goes in v1:
time: 52.8 us; the launch traced here: 52.2 us
  Pallas kernels  18.9 us (36%)
  waiting for transfers between devices  11.1 us (21%)
  starting transfers between devices  10.1 us (19%)
  local copies, waits for them, and re-layouts  8.56 us (16%)
  between operations  2.69 us (5%)
  other arithmetic  0.81 us (2%)
    pallas_call x1, Pallas kernels, shards(): pl.pallas_call(step_one, in_specs=[SM, SM, SM, SM, VM, VM, ANY, ANY, ANY,...  7.76 us
    unnamed x18, local copies, waits for them, and re-layouts  7.71 us
    pallas_call x1, Pallas kernels, shards(): pl.pallas_call(step_two, in_specs=[SM] + [VM] * 16, out_specs=[ANY, VM, V...  5.03 us
    ppermute x1, waiting for transfers between devices, shards(): recv2_b = lax.ppermute(send2_b, 'dom', pairs_b)  4.89 us
    ppermute x1, waiting for transfers between devices, shards(): recv2_a = lax.ppermute(send2_a, 'dom', pairs_a)  4.52 us
    ppermute x1, starting transfers between devices, shards(): recv_b = lax.ppermute(send_b, 'dom', pairs_b)  3 us
    ppermute x1, starting transfers between devices, shards(): recv2_b = lax.ppermute(send2_b, 'dom', pairs_b)  2.84 us
    pallas_call x1, Pallas kernels, shards(): pl.pallas_call(first_send, in_specs=[SM, ANY, ANY, ANY, ANY], out_specs=[...  2.14 us
  transfers between devices with their start and end apart: 6, of which 4 were waited for; matrix products, arithmetic and copies ran while one was open for 3% of the time, Pallas kernels for 18%

profile of v1, /device:TPU:9, one launch (start us, length us, event | category | flops | bytes accessed | tf_op | source)
XLA Modules:
  0.0 52.2 jit_solution(7871777922585641179)
XLA Ops:
  1.3 0.0 copy-start
  1.3 1.4 %copy-done = f32[1,2,8,96,256]{4,3,2,1,0:T(8,128)S(1)} copy-done((f32[1,2,8,96,256]{4,3,2,1,0:T(8,128)S(1)}, f32[1,2,8,96,256]{4,3,2,1,0:T(8,128)}, u32[]{:S(2)}) %copy-start) | copy-done | bytes 1572888
  2.7 0.0 copy-start.2
  2.7 1.4 %copy-done.2 = f32[1,2,8,96,256]{4,3,2,1,0:T(8,128)S(1)} copy-done((f32[1,2,8,96,256]{4,3,2,1,0:T(8,128)S(1)}, f32[1,2,8,96,256]{4,3,2,1,0:T(8,128)}, u32[]{:S(2)}) %copy-start.2) | copy-done | bytes 1572888
  4.1 0.0 copy-start.4
  4.1 1.2 %copy-done.4 = f32[8,128,256]{2,1,0:T(8,128)S(1)} copy-done((f32[8,128,256]{2,1,0:T(8,128)S(1)}, f32[8,128,256]{2,1,0:T(8,128)}, u32[]{:S(2)}) %copy-start.4) | copy-done | bytes 1048600
  5.3 0.0 copy-start.6
  5.3 1.2 %copy-done.6 = f32[8,128,256]{2,1,0:T(8,128)S(1)} copy-done((f32[8,128,256]{2,1,0:T(8,128)S(1)}, f32[8,128,256]{2,1,0:T(8,128)}, u32[]{:S(2)}) %copy-start.6) | copy-done | bytes 1048600
  6.5 0.0 copy-start.1
  6.5 0.0 copy-start.3
  6.5 0.0 copy-start.8
  6.6 2.1 %shard_map.121 = (f32[3,96,256]{2,1,0:T(8,128)}, f32[3,96,256]{2,1,0:T(8,128)}) custom-call(s32[1]{0:T(128)S(6)} %copy.16.off, f32[1,2,8,96,256]{4,3,2,1,0:T(8,128)S(1)} %copy-done, f32[1,2,8,96,256]{4,3,2,1,0:T(8,128)S(1)} %copy-done.2, f32[8,128,256]{2,1,0:T(8,128)S(1)} %copy-done.4, f32[8,128,256]{2,1,0:T(8,128)S(1)} %copy-done.6), custom_call_target="tpu_custom_call" | custom-call | tf_op jit(solution)/shard_map/pallas_call | solution.py:401
  8.7 3.0 %collective-permute-start.1 = (f32[3,96,256]{2,1,0:T(8,128)}, f32[3,96,256]{2,1,0:T(8,128)S(1)}, u32[]{:S(2)}, u32[]{:S(2)}) collective-permute-start(f32[3,96,256]{2,1,0:T(8,128)} %get-tuple-element.40), channel_id=1, source_target_pairs={{2,4},{4,2},{6,8},{8,6},{10,12},{12,10},{3,5},{5,3},{7,9},{9,7},{1... | collective-permute-start | bytes 884744 | tf_op jit(solution)/shard_map/ppermute | solution.py:409
  11.7 1.4 %collective-permute-start = (f32[3,96,256]{2,1,0:T(8,128)}, f32[3,96,256]{2,1,0:T(8,128)}, u32[]{:S(2)}, u32[]{:S(2)}) collective-permute-start(f32[3,96,256]{2,1,0:T(8,128)} %get-tuple-element.30.after), channel_id=1, source_target_pairs={{0,2},{2,0},{4,6},{6,4},{8,10},{10,8},{12,14},{14,12},{1,3},{3,1},... | collective-permute-start | bytes 884744 | tf_op jit(solution)/shard_map/ppermute | solution.py:410
  13.2 0.8 %reshape.13.res = f32[2,50,128]{2,1,0:T(8,128)S(1)} reshape(f32[1,2,6400]{2,1,0:T(2,128)} %param.17) | data formatting | bytes 102400 | tf_op jit(solution)/shard_map/reshape | solution.py:431
  15.3 0.8 %reduce = s32[6400]{0:T(1024)S(1)} reduce(s32[1,6400]{1,0:T(1,128)} %param.16, s32[]{:T(128)} %constant.9), dimensions={0}, to_apply=%param.16.reduce_sub_computation | reduce | bytes 51204 | tf_op args[6]
  16.1 0.0 copy-done.1
  16.1 0.0 copy-done.3
  16.1 0.0 copy-done.8
  16.1 0.0 copy-start.5
  16.2 1.2 %copy-done.5 = f32[8,128,256]{2,1,0:T(8,128)S(1)} copy-done((f32[8,128,256]{2,1,0:T(8,128)S(1)}, f32[8,128,256]{2,1,0:T(8,128)}, u32[]{:S(2)}) %copy-start.5) | copy-done | bytes 1048600
  17.4 0.0 copy-start.7
  17.4 1.2 %copy-done.7 = f32[8,128,256]{2,1,0:T(8,128)S(1)} copy-done((f32[8,128,256]{2,1,0:T(8,128)S(1)}, f32[8,128,256]{2,1,0:T(8,128)}, u32[]{:S(2)}) %copy-start.7) | copy-done | bytes 1048600
  18.6 7.8 %shard_map.122 = (f32[8,96,256]{2,1,0:T(8,128)S(1)}, f32[8,96,256]{2,1,0:T(8,128)S(1)}, f32[8,96,256]{2,1,0:T(8,128)S(1)}, f32[8,96,256]{2,1,0:T(8,128)S(1)}, f3...) custom-call(s32[1]{0:T(128)S(6)} %copy.16.off, ...), custom_call_target="tpu_custom_call" | custom-call | flops 10000000000 | bytes 6000000 | tf_op jit(solution)/shard_map/pallas_call | solution.py:412
  26.4 0.0 collective-permute-done.1.recv.recv_b
  26.4 0.1 shard_map.124
  26.4 0.6 %collective-permute-done.recv.recv_a = f32[3,96,256]{2,1,0:T(8,128)} collective-permute-done((f32[3,96,256]{2,1,0:T(8,128)}, f32[3,96,256]{2,1,0:T(8,128)}, u32[]{:S(2)}, u32[]{:S(2)}) %collective-permute-start) | collective-permute-done | bytes 294944 | tf_op jit(solution)/shard_map/ppermute | solution.py:410
  27.1 1.0 %shard_map.123 = (f32[2,96,256]{2,1,0:T(8,128)S(1)}, f32[2,96,256]{2,1,0:T(8,128)S(1)}) custom-call(f32[3,96,256]{2,1,0:T(8,128)} %collective-permute-done.recv.recv_a, f32[8,96,256]{2,1,0:T(8,128)S(1)} %get-tuple-element.31.p, f32[8,96,256]{2,1,0:T(8,128)S(1)} %get-tuple-element.32.kq, f32[8,96,256]{2,1,0:T(8,128)S(1)} %get-tuple-element.33.kw, ...), custom_call_target="tpu_custom_call" | custom-call | tf_op jit(solution)/shard_map/pallas_call | solution.py:436
  28.1 5.0 %shard_map.125 = (f32[1,2,8,96,256]{4,3,2,1,0:T(8,128)}, f32[2,96,256]{2,1,0:T(8,128)S(1)}, f32[2,8,64,256]{3,2,1,0:T(8,128)S(1)}, f32[2,8,64,256]{3,2,1,0:T(8,128)S(1)}) custom-call(s32[1]{0:T(128)S(6)} %copy.16.off, f32[2,96,256]{2,1,0:T(8,128)S(1)} %get-tuple-element.38.send_a, f32[2,96,256]{2,1,0:T(8,128)S(1)} %get-tuple-element.39.kept_a, ...), custom_call_target="tpu_custom_call" | custom-call | flops 6000000000 | bytes 2000000 | tf_op jit(solution)/shard_map/pallas_call | solution.py:449
  33.1 0.7 %collective-permute-start.2 = (f32[2,8,64,256]{3,2,1,0:T(8,128)S(1)}, f32[2,8,64,256]{3,2,1,0:T(8,128)S(1)}, u32[]{:S(2)}, u32[]{:S(2)}) collective-permute-start(f32[2,8,64,256]{3,2,1,0:T(8,128)S(1)} %get-tuple-element.49), channel_id=1, source_target_pairs={{0,1},{1,0},{2,3},{3,2},{4,5},{5,4},{6,7},{7,6},{8,9},{9,8},{10,11... | collective-permute-start | bytes 3145736 | tf_op jit(solution)/shard_map/ppermute | solution.py:470
  33.8 2.8 %collective-permute-start.4 = (f32[2,96,256]{2,1,0:T(8,128)S(1)}, f32[2,96,256]{2,1,0:T(8,128)S(1)}, u32[]{:S(2)}, u32[]{:S(2)}) collective-permute-start(f32[2,96,256]{2,1,0:T(8,128)S(1)} %get-tuple-element.41.send_b), channel_id=1, source_target_pairs={{2,4},{4,2},{6,8},{8,6},{10,12},{12,10},{3,5},{5,3},{7,9},{9,7},{1... | collective-permute-start | bytes 589832 | tf_op jit(solution)/shard_map/ppermute | solution.py:445
  36.7 1.6 %collective-permute-start.3 = (f32[2,96,256]{2,1,0:T(8,128)S(1)}, f32[2,96,256]{2,1,0:T(8,128)S(1)}, u32[]{:S(2)}, u32[]{:S(2)}) collective-permute-start(f32[2,96,256]{2,1,0:T(8,128)S(1)} %get-tuple-element.38.send_a), channel_id=1, source_target_pairs={{0,2},{2,0},{4,6},{6,4},{8,10},{10,8},{12,14},{14,12},{1,3},{3,1},... | collective-permute-start | bytes 589832 | tf_op jit(solution)/shard_map/ppermute | solution.py:447
  38.3 4.9 %collective-permute-done.4.recv2_b = f32[2,96,256]{2,1,0:T(8,128)S(1)} collective-permute-done((f32[2,96,256]{2,1,0:T(8,128)S(1)}, f32[2,96,256]{2,1,0:T(8,128)S(1)}, u32[]{:S(2)}, u32[]{:S(2)}) %collective-permute-start.4) | collective-permute-done | bytes 196640 | tf_op jit(solution)/shard_map/ppermute | solution.py:445
  43.2 4.5 %collective-permute-done.3.recv2_a = f32[2,96,256]{2,1,0:T(8,128)S(1)} collective-permute-done((f32[2,96,256]{2,1,0:T(8,128)S(1)}, f32[2,96,256]{2,1,0:T(8,128)S(1)}, u32[]{:S(2)}, u32[]{:S(2)}) %collective-permute-start.3) | collective-permute-done | bytes 196640 | tf_op jit(solution)/shard_map/ppermute | solution.py:447
  47.7 1.8 %shard_map.126 = (f32[1,2,8,96,256]{4,3,2,1,0:T(8,128)}, f32[3,64,256]{2,1,0:T(8,128)S(1)}, f32[3,64,256]{2,1,0:T(8,128)S(1)}) custom-call(s32[1]{0:T(128)S(6)} %copy.16.off, f32[3,96,256]{2,1,0:T(8,128)} %collective-permute-done.recv.recv_a, f32[3,96,256]{2,1,0:T(8,128)S(1)} %collective-permute-done.1.recv.recv_b, ...), custom_call_target="tpu_custom_call", output_to_operand_aliasing={{0}: (12, {})} | custom-call | tf_op jit(solution)/shard_map/pallas_call | solution.py:472
  49.5 0.5 %collective-permute-start.5 = (f32[3,64,256]{2,1,0:T(8,128)S(1)}, f32[3,64,256]{2,1,0:T(8,128)S(1)}, u32[]{:S(2)}, u32[]{:S(2)}) collective-permute-start(f32[3,64,256]{2,1,0:T(8,128)S(1)} %get-tuple-element.53), channel_id=1, source_target_pairs={{0,1},{1,0},{2,3},{3,2},{4,5},{5,4},{6,7},{7,6},{8,9},{9,8},{10,11... | collective-permute-start | bytes 589832 | tf_op jit(solution)/shard_map/ppermute | solution.py:489
  50.0 1.1 %collective-permute-done.5.recv_e = f32[3,64,256]{2,1,0:T(8,128)S(1)} collective-permute-done((f32[3,64,256]{2,1,0:T(8,128)S(1)}, f32[3,64,256]{2,1,0:T(8,128)S(1)}, u32[]{:S(2)}, u32[]{:S(2)}) %collective-permute-start.5) | collective-permute-done | bytes 196640 | tf_op jit(solution)/shard_map/ppermute | solution.py:489
  51.1 0.0 collective-permute-done.2.recv
  51.1 1.1 %shard_map.127 = (f32[8,64,256]{2,1,0:T(8,128)}, f32[8,64,256]{2,1,0:T(8,128)}) custom-call(f32[2,8,64,256]{3,2,1,0:T(8,128)S(1)} %get-tuple-element.48.mine, f32[2,8,64,256]{3,2,1,0:T(8,128)S(1)} %collective-permute-done.2.recv, f32[3,64,256]{2,1,0:T(8,128)S(1)} %get-tuple-element.52.mine_e, f32[3,64,256]{2,1,0:T(8,128)S(1)} %collective-permute-done.5.recv_e), custom_call_target="tpu_custom_call" | custom-call | tf_op jit(solution)/shard_map/pallas_call | solution.py:490
Async XLA Ops:
  1.3 1.4 %copy-start = (f32[1,2,8,96,256]{4,3,2,1,0:T(8,128)S(1)}, f32[1,2,8,96,256]{4,3,2,1,0:T(8,128)}, u32[]{:S(2)}) copy-start(f32[1,2,8,96,256]{4,3,2,1,0:T(8,128)} %ckpt.3) | copy-start | bytes 4718596
  2.7 1.4 %copy-start.2 = (f32[1,2,8,96,256]{4,3,2,1,0:T(8,128)S(1)}, f32[1,2,8,96,256]{4,3,2,1,0:T(8,128)}, u32[]{:S(2)}) copy-start(f32[1,2,8,96,256]{4,3,2,1,0:T(8,128)} %adj.3) | copy-start | bytes 4718596
  4.1 1.2 %copy-start.4 = (f32[8,128,256]{2,1,0:T(8,128)S(1)}, f32[8,128,256]{2,1,0:T(8,128)}, u32[]{:S(2)}) copy-start(f32[8,128,256]{2,1,0:T(8,128)} %kappa.3) | copy-start | bytes 3145732
  5.3 1.2 %copy-start.6 = (f32[8,128,256]{2,1,0:T(8,128)S(1)}, f32[8,128,256]{2,1,0:T(8,128)}, u32[]{:S(2)}) copy-start(f32[8,128,256]{2,1,0:T(8,128)} %buoy.3) | copy-start | bytes 3145732
  6.5 9.6 %copy-start.1 = (f32[1,2,8,96,256]{4,3,2,1,0:T(8,128)S(1)}, f32[1,2,8,96,256]{4,3,2,1,0:T(8,128)}, u32[]{:S(2)}) copy-start(f32[1,2,8,96,256]{4,3,2,1,0:T(8,128)} %ckpt.3) | copy-start | bytes 4718596
  6.5 9.6 %copy-start.3 = (f32[1,2,8,96,256]{4,3,2,1,0:T(8,128)S(1)}, f32[1,2,8,96,256]{4,3,2,1,0:T(8,128)}, u32[]{:S(2)}) copy-start(f32[1,2,8,96,256]{4,3,2,1,0:T(8,128)} %adj.3) | copy-start | bytes 4718596
  6.5 9.6 %copy-start.8 = (f32[1024]{0:T(1024)S(1)}, f32[1024]{0:T(1024)}, u32[]{:S(2)}) copy-start(f32[1024]{0:T(1024)} %wav.1) | copy-start | bytes 12292
  8.7 17.7 %collective-permute-start.1 = (f32[3,96,256]{2,1,0:T(8,128)}, f32[3,96,256]{2,1,0:T(8,128)S(1)}, u32[]{:S(2)}, u32[]{:S(2)}) collective-permute-start(f32[3,96,256]{2,1,0:T(8,128)} %get-tuple-element.40), channel_id=1, source_target_pairs={{2,4},{4,2},{6,8},{8,6},{10,12},{12,10},{3,5},{5,3},{7,9},{9,7},{1... | collective-permute-start | bytes 884744 | tf_op jit(solution)/shard_map/ppermute | solution.py:409
  11.7 15.3 %collective-permute-start = (f32[3,96,256]{2,1,0:T(8,128)}, f32[3,96,256]{2,1,0:T(8,128)}, u32[]{:S(2)}, u32[]{:S(2)}) collective-permute-start(f32[3,96,256]{2,1,0:T(8,128)} %get-tuple-element.30.after), channel_id=1, source_target_pairs={{0,2},{2,0},{4,6},{6,4},{8,10},{10,8},{12,14},{14,12},{1,3},{3,1},... | collective-permute-start | bytes 884744 | tf_op jit(solution)/shard_map/ppermute | solution.py:410
  16.1 1.2 %copy-start.5 = (f32[8,128,256]{2,1,0:T(8,128)S(1)}, f32[8,128,256]{2,1,0:T(8,128)}, u32[]{:S(2)}) copy-start(f32[8,128,256]{2,1,0:T(8,128)} %kappa.3) | copy-start | bytes 3145732
  17.4 1.2 %copy-start.7 = (f32[8,128,256]{2,1,0:T(8,128)S(1)}, f32[8,128,256]{2,1,0:T(8,128)}, u32[]{:S(2)}) copy-start(f32[8,128,256]{2,1,0:T(8,128)} %buoy.3) | copy-start | bytes 3145732
  33.1 18.0 %collective-permute-start.2 = (f32[2,8,64,256]{3,2,1,0:T(8,128)S(1)}, f32[2,8,64,256]{3,2,1,0:T(8,128)S(1)}, u32[]{:S(2)}, u32[]{:S(2)}) collective-permute-start(f32[2,8,64,256]{3,2,1,0:T(8,128)S(1)} %get-tuple-element.49), channel_id=1, source_target_pairs={{0,1},{1,0},{2,3},{3,2},{4,5},{5,4},{6,7},{7,6},{8,9},{9,8},{10,11... | collective-permute-start | bytes 3145736 | tf_op jit(solution)/shard_map/ppermute | solution.py:470
  33.8 9.3 %collective-permute-start.4 = (f32[2,96,256]{2,1,0:T(8,128)S(1)}, f32[2,96,256]{2,1,0:T(8,128)S(1)}, u32[]{:S(2)}, u32[]{:S(2)}) collective-permute-start(f32[2,96,256]{2,1,0:T(8,128)S(1)} %get-tuple-element.41.send_b), channel_id=1, source_target_pairs={{2,4},{4,2},{6,8},{8,6},{10,12},{12,10},{3,5},{5,3},{7,9},{9,7},{1... | collective-permute-start | bytes 589832 | tf_op jit(solution)/shard_map/ppermute | solution.py:445
  36.7 11.0 %collective-permute-start.3 = (f32[2,96,256]{2,1,0:T(8,128)S(1)}, f32[2,96,256]{2,1,0:T(8,128)S(1)}, u32[]{:S(2)}, u32[]{:S(2)}) collective-permute-start(f32[2,96,256]{2,1,0:T(8,128)S(1)} %get-tuple-element.38.send_a), channel_id=1, source_target_pairs={{0,2},{2,0},{4,6},{6,4},{8,10},{10,8},{12,14},{14,12},{1,3},{3,1},... | collective-permute-start | bytes 589832 | tf_op jit(solution)/shard_map/ppermute | solution.py:447
  49.5 1.6 %collective-permute-start.5 = (f32[3,64,256]{2,1,0:T(8,128)S(1)}, f32[3,64,256]{2,1,0:T(8,128)S(1)}, u32[]{:S(2)}, u32[]{:S(2)}) collective-permute-start(f32[3,64,256]{2,1,0:T(8,128)S(1)} %get-tuple-element.53), channel_id=1, source_target_pairs={{0,1},{1,0},{2,3},{3,2},{4,5},{5,4},{6,7},{7,6},{8,9},{9,8},{10,11... | collective-permute-start | bytes 589832 | tf_op jit(solution)/shard_map/ppermute | solution.py:489

commit v2 on v1

--- a/solution.py
+++ b/solution.py
@@ -23,6 +23,14 @@
 
 def keep(x):
     return pltpu.with_memory_space_constraint(x, pltpu.VMEM)
+
+
+def far(x):
+    return pltpu.with_memory_space_constraint(x, pltpu.HBM)
+
+
+def cost(us):
+    return pl.CostEstimate(flops=int(us * 1_000_000_000), bytes_accessed=1024, transcendentals=0)
 
 
 def params():
@@ -255,11 +263,10 @@
 
 def step_two(
     off, send_a, kept_a, send_b, kept_b, p, q, kq, kw, hb, fy_i, fz_i, dg_i, lap_i, pn_i, qm_i, total,
-    adj_out, last_e, mine, other,
-    pn, qm, kqm, last, g_full, gx_s, sem,
+    adj_out, last_e, parts,
+    pn, qm, kqm, last, gx_s, sem,
 ):
     width, ny, nz = p.shape
-    half = mine.shape[2]
     edge_a, edge_b = edges(width)
     ys = lax.broadcasted_iota(jnp.int32, (ny, nz), 0)
     zs = lax.broadcasted_iota(jnp.int32, (ny, nz), 1)
@@ -279,7 +286,6 @@
         qm[edge] = kept[1]
     mid_copy = pltpu.make_async_copy(qm, adj_out.at[0, 0], sem.at[0])
     mid_copy.start()
-    model_y = g_full.shape[2]
 
     def plane(x, carry):
         xn = jnp.minimum(x + 1, width - 1)
@@ -307,14 +313,14 @@
         at = pl.ds(pl.multiple_of(x * ny, 8), ny)
         last[x] = 2.0 * qm[x] - q[x] + lap(dqm, 1) + total[at, nz : 2 * nz]
         lap1 = jnp.where(x == edge_a, kept_a[0], jnp.where(x == edge_b, kept_b[0], lap_i[x]))
-        g_full[0, x] = placed(qm[x] * lap1 + q[x] * lap2, off[0], model_y)
+        parts[0, x] = qm[x] * lap1 + q[x] * lap2
         dp = diffs(p)
         dq = diffs(kq)
         prod = [a * b + c * d for a, b, c, d in zip(dp, dqm, dpn, dq)]
         gb = prod[1]
         gb += jnp.where(ys == ny - 1, prod[0], prod[2])
         gb += jnp.where(zs == nz - 1, prod[0], prod[3])
-        g_full[1, x] = placed(-gb, off[0], model_y)
+        parts[1, x] = -gb
         return carry
 
     lax.fori_loop(0, width, plane, 0)
@@ -322,56 +328,73 @@
     last_copy.start()
     last_e[0] = last[edge_a]
     last_e[1] = last[edge_b]
-    shot = lax.axis_index("shot")
-    own = pl.ds(pl.multiple_of(shot * half, 8), half)
-    far = pl.ds(pl.multiple_of((1 - shot) * half, 8), half)
-    for g in range(2):
-        mine[g] = g_full[g, :, own, :]
-        other[g] = g_full[g, :, far, :]
     mid_copy.wait()
     last_copy.wait()
 
 
-def edge_two(
-    off, recv_a, recv_b, recv2_a, recv2_b, send_a, send_b, p, q, kq, hb, last_e, adj_in,
-    adj_out, mine, other, full, ql, sem,
+def edge_terms(edge, recv, recv2, send, p, q, kq, hb):
+    face = hb[edge] + 0.5 * recv[2]
+    dpn = recv2[0] - send[0]
+    dqm = recv2[1] - send[1]
+    add_k = q[edge] * (face * dpn)
+    add_b = -(dqm * (recv[0] - p[edge]) + dpn * (recv[1] - kq[edge]))
+    return face * dqm, add_k, jnp.where(edge == p.shape[0] - 1, add_b, 0.0)
+
+
+def split(plane, off, half):
+    whole = placed(plane, off, 2 * half)
+    shot = lax.axis_index("shot")
+    return (
+        jnp.where(shot == 0, whole[:half], whole[half:]),
+        jnp.where(shot == 0, whole[half:], whole[:half]),
+    )
+
+
+def edge_b_two(
+    off, recv, recv2, send, p, q, kq, hb, last_e, parts, adj_in,
+    adj_out, mine, other, add, ql, sem,
 ):
-    width, ny, nz = p.shape
+    width = p.shape[0]
+    half = mine.shape[2]
+    edge = edges(width)[1]
+    add_q, add[0], add[1] = edge_terms(edge, recv, recv2, send, p, q, kq, hb)
+    ql[...] = last_e[1] + add_q
+    copy = pltpu.make_async_copy(ql, adj_out.at[0, 1, edge], sem.at[0])
+    copy.start()
+
+    def plane(x, carry):
+        here = jnp.where(x == edge, 1.0, 0.0)
+        for g in range(2):
+            mine[g, x], other[g, x] = split(parts[g, x] + here * add[g], off[0], half)
+        return carry
+
+    lax.fori_loop(0, width, plane, 0)
+    copy.wait()
+
+
+def edge_a_two(
+    off, recv, recv2, send, p, q, kq, hb, last_e, adj_in,
+    adj_out, mine, other, ql, sem,
+):
+    width = p.shape[0]
     half = mine.shape[1]
-    which = edges(width)
-    model_y = full.shape[1]
-    full[2] = jnp.zeros(full.shape[1:], F32)
-    copies = []
-    for n, (recv, recv2, send) in enumerate(((recv_a, recv2_a, send_a), (recv_b, recv2_b, send_b))):
-        edge = which[n]
-        face = hb[edge] + 0.5 * recv[2]
-        dpn = recv2[0] - send[0]
-        dqm = recv2[1] - send[1]
-        ql[n] = last_e[n] + face * dqm
-        copy = pltpu.make_async_copy(ql.at[n], adj_out.at[0, 1, edge], sem.at[n])
-        copy.start()
-        copies.append(copy)
-        slot = jnp.where(edge == width - 1, 1, 0)
-        full[slot] = placed(q[edge] * (face * dpn), off[0], model_y)
-
-        @pl.when(edge == width - 1)
-        def _():
-            full[2] = placed(-(dqm * (recv[0] - p[edge]) + dpn * (recv[1] - kq[edge])), off[0], model_y)
-
-    shot = lax.axis_index("shot")
-    mine[...] = full[:, pl.ds(pl.multiple_of(shot * half, 8), half), :]
-    other[...] = full[:, pl.ds(pl.multiple_of((1 - shot) * half, 8), half), :]
-    for copy in copies:
-        copy.wait()
+    edge = edges(width)[0]
+    add_q, add_k, add_b = edge_terms(edge, recv, recv2, send, p, q, kq, hb)
+    ql[...] = last_e[0] + add_q
+    copy = pltpu.make_async_copy(ql, adj_out.at[0, 1, edge], sem.at[0])
+    copy.start()
+    mine[0], other[0] = split(add_k, off[0], half)
+    mine[1], other[1] = split(add_b, off[0], half)
+    copy.wait()
 
 
 def combine(mine, recv, mine_e, recv_e, grad_k, grad_b):
     width = grad_k.shape[0]
+    edge = edges(width)[0]
     grad_k[...] = mine[0] + recv[0]
     grad_b[...] = mine[1] + recv[1]
-    grad_k[0] += mine_e[0] + recv_e[0]
-    grad_k[width - 1] += mine_e[1] + recv_e[1]
-    grad_b[width - 1] += mine_e[2] + recv_e[2]
+    grad_k[edge] += mine_e[0] + recv_e[0]
+    grad_b[edge] += mine_e[1] + recv_e[1]
 
 
 def pairs(count, first):
@@ -398,6 +421,7 @@
     field = (width, ny, nz)
     dma = pltpu.SemaphoreType.DMA
 
+    inputs = [far(x) for x in (checkpoint, adjoint, kappa, buoyancy)]
     send_b, send_a = pl.pallas_call(
         first_send,
         in_specs=[SM, ANY, ANY, ANY, ANY],
@@ -405,13 +429,13 @@
         out_shape=[vmem(3, *layer)] * 2,
         scratch_shapes=[vmem(2, *layer), vmem(2, model_y, nz), vmem(2, model_y, nz), dma((2, 4))],
         compiler_params=params(),
-    )(offsets, checkpoint, adjoint, kappa, buoyancy)
+    )(offsets, *inputs)
     recv_b = lax.ppermute(send_b, "dom", pairs_b)
     recv_a = lax.ppermute(send_a, "dom", pairs_a)
 
     p, q, kq, kw, hb, fy, fz, dg, lap, pn, qm, total = pl.pallas_call(
         step_one,
-        in_specs=[SM, SM, SM, SM, VM, VM, ANY, ANY, ANY, ANY, ANY],
+        in_specs=[SM, SM, SM, SM, VM, VM, ANY, ANY, ANY, ANY, VM],
         out_specs=[VM] * 12,
         out_shape=[vmem(*field)] * 11 + [vmem(width * ny, 2 * nz)],
         scratch_shapes=[
@@ -425,11 +449,11 @@
             dma((6,)),
         ],
         compiler_params=params(),
-        cost_estimate=pl.CostEstimate(flops=10_000_000_000, bytes_accessed=6_000_000, transcendentals=0),
+        cost_estimate=cost(40),
     )(
         offsets, ckpt_step, src_cell, wavelet,
         rec_cell.reshape(rrows, LANES), residuals.reshape(2, rrows, LANES),
-        checkpoint, adjoint, kappa, buoyancy, send_a,
+        *inputs, keep(send_a),
     )
 
     def first_edge(which, recv):
@@ -446,45 +470,49 @@
     send2_a, kept_a = first_edge(0, recv_a)
     recv2_a = lax.ppermute(send2_a, "dom", pairs_a)
 
-    adj_part, last_e, mine, other = pl.pallas_call(
+    adj_part, last_e, parts = pl.pallas_call(
         step_two,
         in_specs=[SM] + [VM] * 16,
-        out_specs=[ANY, VM, VM, VM],
-        out_shape=[
-            jax.ShapeDtypeStruct((1, 2, *field), F32),
-            vmem(2, *layer),
-            vmem(2, width, half, nz),
-            vmem(2, width, half, nz),
-        ],
+        out_specs=[ANY, VM, VM],
+        out_shape=[pltpu.HBM((1, 2, *field), F32), vmem(2, *layer), vmem(2, *field)],
         scratch_shapes=[
-            vmem(*field), vmem(*field), vmem(*field), vmem(*field),
-            vmem(2, width, model_y, nz), vmem(2, *layer), dma((2,)),
+            vmem(*field), vmem(*field), vmem(*field), vmem(*field), vmem(2, *layer), dma((2,)),
         ],
         compiler_params=params(),
-        cost_estimate=pl.CostEstimate(flops=6_000_000_000, bytes_accessed=2_000_000, transcendentals=0),
+        cost_estimate=cost(40),
     )(
         offsets,
         *[keep(v) for v in (send2_a, kept_a, send2_b, kept_b, p, q, kq, kw, hb, fy, fz, dg, lap, pn, qm, total)],
     )
     swap = [(0, 1), (1, 0)]
-    recv_g = lax.ppermute(other, "shot", swap)
-
-    adj_next, mine_e, other_e = pl.pallas_call(
-        edge_two,
-        in_specs=[SM] + [VM] * 11 + [ANY],
+    adj_part, mine, other = pl.pallas_call(
+        edge_b_two,
+        in_specs=[SM] + [VM] * 9 + [ANY],
         out_specs=[ANY, VM, VM],
-        out_shape=[
-            jax.ShapeDtypeStruct((1, 2, *field), F32),
-            vmem(3, half, nz),
-            vmem(3, half, nz),
-        ],
-        scratch_shapes=[vmem(3, model_y, nz), vmem(2, *layer), dma((2,))],
-        input_output_aliases={12: 0},
+        out_shape=[pltpu.HBM((1, 2, *field), F32), vmem(2, width, half, nz), vmem(2, width, half, nz)],
+        scratch_shapes=[vmem(2, *layer), vmem(*layer), dma((1,))],
+        input_output_aliases={10: 0},
         compiler_params=params(),
+        cost_estimate=cost(1),
     )(
         offsets,
-        *[keep(v) for v in (recv_a, recv_b, recv2_a, recv2_b, send2_a, send2_b, p, q, kq, hb, last_e)],
-        adj_part,
+        *[keep(v) for v in (recv_b, recv2_b, send2_b, p, q, kq, hb, last_e, parts)],
+        far(adj_part),
+    )
+    recv_g = lax.ppermute(other, "shot", swap)
+    adj_next, mine_e, other_e = pl.pallas_call(
+        edge_a_two,
+        in_specs=[SM] + [VM] * 8 + [ANY],
+        out_specs=[ANY, VM, VM],
+        out_shape=[pltpu.HBM((1, 2, *field), F32), vmem(2, half, nz), vmem(2, half, nz)],
+        scratch_shapes=[vmem(*layer), dma((1,))],
+        input_output_aliases={9: 0},
+        compiler_params=params(),
+        cost_estimate=cost(40),
+    )(
+        offsets,
+        *[keep(v) for v in (recv_a, recv2_a, send2_a, p, q, kq, hb, last_e)],
+        far(adj_part),
     )
     recv_e = lax.ppermute(other_e, "shot", swap)
     grad_k, grad_b = pl.pallas_call(

time: 52.8 us -> 32.9 us (0.62)
  the two profiles are of different devices: /device:TPU:9 before, /device:TPU:0 now
where the time goes in v2:
time: 32.9 us; the launch traced here: 32.7 us
  Pallas kernels  15.7 us (48%)
  starting transfers between devices  8.37 us (25%)
  waiting for transfers between devices  5.75 us (17%)
  between operations  2.73 us (8%)
    pallas_call x1, Pallas kernels, shards(): pl.pallas_call(step_one, in_specs=[SM, SM, SM, SM, VM, VM, ANY, ANY, ANY,...  7.35 us
    pallas_call x1, Pallas kernels, shards(): pl.pallas_call(step_two, in_specs=[SM] + [VM] * 16, out_specs=[ANY, VM, V...  4.32 us
    ppermute x1, starting transfers between devices, shards(): recv2_a = lax.ppermute(send2_a, 'dom', pairs_a)  3.89 us
    ppermute x1, starting transfers between devices, shards(): recv_a = lax.ppermute(send_a, 'dom', pairs_a)  3 us
    ppermute x1, waiting for transfers between devices, shards(): recv_a = lax.ppermute(send_a, 'dom', pairs_a)  2.32 us
    ppermute x1, waiting for transfers between devices, shards(): recv2_a = lax.ppermute(send2_a, 'dom', pairs_a)  2.08 us
    pallas_call x1, Pallas kernels, shards(): pl.pallas_call(first_send, in_specs=[SM, ANY, ANY, ANY, ANY], out_specs=[...  1.4 us
    ppermute x1, waiting for transfers between devices, shards(): recv_e = lax.ppermute(other_e, 'shot', swap)  1.33 us
  transfers between devices with their start and end apart: 6, of which 3 were waited for; matrix products, arithmetic and copies ran while one was open for 0% of the time, Pallas kernels for 40%

profile of v2, /device:TPU:0, one launch (start us, length us, event | category | flops | bytes accessed | tf_op | source)
XLA Modules:
  0.0 32.7 jit_solution(10714488880754187013)
XLA Ops:
  1.3 0.0 copy-start.1
  1.3 0.0 copy-start.2
  1.3 0.0 copy-start
  1.3 1.4 %shard_map.121 = (f32[3,96,256]{2,1,0:T(8,128)S(1)}, f32[3,96,256]{2,1,0:T(8,128)S(1)}) custom-call(s32[1]{0:T(128)S(6)} %copy.18.off, f32[1,2,8,96,256]{4,3,2,1,0:T(8,128)} %ckpt.3, f32[1,2,8,96,256]{4,3,2,1,0:T(8,128)} %adj.3, f32[8,128,256]{2,1,0:T(8,128)} %kappa.3, f32[8,128,256]{2,1,0:T(8,128)} %buoy.3), custom_call_target="tpu_custom_call" | custom-call | tf_op jit(solution)/shard_map/pallas_call | solution.py:425
  2.7 3.0 %collective-permute-start.2 = (f32[3,96,256]{2,1,0:T(8,128)S(1)}, f32[3,96,256]{2,1,0:T(8,128)S(1)}, u32[]{:S(2)}, u32[]{:S(2)}) collective-permute-start(f32[3,96,256]{2,1,0:T(8,128)S(1)} %get-tuple-element.33.after), channel_id=1, source_target_pairs={{0,2},{2,0},{4,6},{6,4},{8,10},{10,8},{12,14},{14,12},{1,3},{3,1},... | collective-permute-start | bytes 884744 | tf_op jit(solution)/shard_map/ppermute | solution.py:434
  5.7 0.7 %collective-permute-start = (f32[3,96,256]{2,1,0:T(8,128)S(1)}, f32[3,96,256]{2,1,0:T(8,128)S(1)}, u32[]{:S(2)}, u32[]{:S(2)}) collective-permute-start(f32[3,96,256]{2,1,0:T(8,128)S(1)} %get-tuple-element.32), channel_id=1, source_target_pairs={{2,4},{4,2},{6,8},{8,6},{10,12},{12,10},{3,5},{5,3},{7,9},{9,7},{1... | collective-permute-start | bytes 884744 | tf_op jit(solution)/shard_map/ppermute | solution.py:433
  6.4 0.0 copy-done.1
  7.7 0.0 copy-done.2
  7.8 0.1 reduce
  7.8 0.0 copy-done
  7.8 7.4 %shard_map.122 = (f32[8,96,256]{2,1,0:T(8,128)S(1)}, f32[8,96,256]{2,1,0:T(8,128)S(1)}, f32[8,96,256]{2,1,0:T(8,128)S(1)}, f32[8,96,256]{2,1,0:T(8,128)S(1)}, f3...) custom-call(s32[1]{0:T(128)S(6)} %copy.18.off, ...), custom_call_target="tpu_custom_call" | custom-call | flops 40000000000 | bytes 1024 | tf_op jit(solution)/shard_map/pallas_call | solution.py:436
  15.2 0.0 collective-permute-done.recv
  15.2 0.1 shard_map.123
  15.3 0.7 %collective-permute-start.1 = (f32[2,96,256]{2,1,0:T(8,128)S(1)}, f32[2,96,256]{2,1,0:T(8,128)S(1)}, u32[]{:S(2)}, u32[]{:S(2)}) collective-permute-start(f32[2,96,256]{2,1,0:T(8,128)S(1)} %get-tuple-element.41.send_b.send), channel_id=1, source_target_pairs={{2,4},{4,2},{6,8},{8,6},{10,12},{12,10},{3,5},{5,3},{7,9},{9,7},{1... | collective-permute-start | bytes 589832 | tf_op jit(solution)/shard_map/ppermute | solution.py:469
  16.0 2.3 %collective-permute-done.2.recv = f32[3,96,256]{2,1,0:T(8,128)S(1)} collective-permute-done((f32[3,96,256]{2,1,0:T(8,128)S(1)}, f32[3,96,256]{2,1,0:T(8,128)S(1)}, u32[]{:S(2)}, u32[]{:S(2)}) %collective-permute-start.2) | collective-permute-done | bytes 294944 | tf_op jit(solution)/shard_map/ppermute | solution.py:434
  18.3 0.1 shard_map.124
  18.4 3.9 %collective-permute-start.4 = (f32[2,96,256]{2,1,0:T(8,128)S(1)}, f32[2,96,256]{2,1,0:T(8,128)S(1)}, u32[]{:S(2)}, u32[]{:S(2)}) collective-permute-start(f32[2,96,256]{2,1,0:T(8,128)S(1)} %get-tuple-element.43.send_a.send), channel_id=1, source_target_pairs={{0,2},{2,0},{4,6},{6,4},{8,10},{10,8},{12,14},{14,12},{1,3},{3,1},... | collective-permute-start | bytes 589832 | tf_op jit(solution)/shard_map/ppermute | solution.py:471
  22.3 4.3 %shard_map.125 = (f32[1,2,8,96,256]{4,3,2,1,0:T(8,128)}, f32[2,96,256]{2,1,0:T(8,128)S(1)}, f32[2,8,96,256]{3,2,1,0:T(8,128)S(1)}) custom-call(s32[1]{0:T(128)S(6)} %copy.18.off, f32[2,96,256]{2,1,0:T(8,128)S(1)} %get-tuple-element.43.send_a.send, f32[2,96,256]{2,1,0:T(8,128)S(1)} %get-tuple-element.44.kept_a, ...), custom_call_target="tpu_custom_call" | custom-call | flops 40000000000 | bytes 1024 | tf_op jit(solution)/shard_map/pallas_call | solution.py:473
  26.6 0.0 collective-permute-done.1.recv2
  26.6 0.7 %shard_map.126 = (f32[1,2,8,96,256]{4,3,2,1,0:T(8,128)}, f32[2,8,64,256]{3,2,1,0:T(8,128)S(1)}, f32[2,8,64,256]{3,2,1,0:T(8,128)S(1)}) custom-call(s32[1]{0:T(128)S(6)} %copy.18.off, f32[3,96,256]{2,1,0:T(8,128)S(1)} %collective-permute-done.recv, f32[2,96,256]{2,1,0:T(8,128)S(1)} %collective-permute-done.1.recv2, ...), custom_call_target="tpu_custom_call", output_to_operand_aliasing={{0}: (10, {})} | custom-call | flops 1000000000 | bytes 1024 | tf_op jit(solution)/shard_map/pallas_call | solution.py:488
  27.3 0.1 collective-permute-start.3
  27.4 2.1 %collective-permute-done.4.recv2 = f32[2,96,256]{2,1,0:T(8,128)S(1)} collective-permute-done((f32[2,96,256]{2,1,0:T(8,128)S(1)}, f32[2,96,256]{2,1,0:T(8,128)S(1)}, u32[]{:S(2)}, u32[]{:S(2)}) %collective-permute-start.4) | collective-permute-done | bytes 196640 | tf_op jit(solution)/shard_map/ppermute | solution.py:471
  29.5 0.7 %shard_map.127 = (f32[1,2,8,96,256]{4,3,2,1,0:T(8,128)}, f32[2,64,256]{2,1,0:T(8,128)S(1)}, f32[2,64,256]{2,1,0:T(8,128)S(1)}) custom-call(s32[1]{0:T(128)S(6)} %copy.18.off, f32[3,96,256]{2,1,0:T(8,128)S(1)} %collective-permute-done.2.recv, f32[2,96,256]{2,1,0:T(8,128)S(1)} %collective-permute-done.4.recv2, ...), custom_call_target="tpu_custom_call", output_to_operand_aliasing={{0}: (9, {})} | custom-call | flops 40000000000 | bytes 1024 | tf_op jit(solution)/shard_map/pallas_call | solution.py:503
  30.2 0.1 collective-permute-start.5
  30.3 1.3 %collective-permute-done.5.recv_e = f32[2,64,256]{2,1,0:T(8,128)S(1)} collective-permute-done((f32[2,64,256]{2,1,0:T(8,128)S(1)}, f32[2,64,256]{2,1,0:T(8,128)S(1)}, u32[]{:S(2)}, u32[]{:S(2)}) %collective-permute-start.5) | collective-permute-done | bytes 131104 | tf_op jit(solution)/shard_map/ppermute | solution.py:517
  31.6 0.0 collective-permute-done.3.recv
  31.6 1.1 %shard_map.128 = (f32[8,64,256]{2,1,0:T(8,128)}, f32[8,64,256]{2,1,0:T(8,128)}) custom-call(f32[2,8,64,256]{3,2,1,0:T(8,128)S(1)} %get-tuple-element.53.mine, f32[2,8,64,256]{3,2,1,0:T(8,128)S(1)} %collective-permute-done.3.recv, f32[2,64,256]{2,1,0:T(8,128)S(1)} %get-tuple-element.56.mine_e, f32[2,64,256]{2,1,0:T(8,128)S(1)} %collective-permute-done.5.recv_e), custom_call_target="tpu_custom_call" | custom-call | tf_op jit(solution)/shard_map/pallas_call | solution.py:518
  (1 shorter events, 0.0 us)
Async XLA Ops:
  1.3 5.1 %copy-start.1 = (f32[1,2,6400]{2,1,0:T(2,128)S(1)}, f32[1,2,6400]{2,1,0:T(2,128)}, u32[]{:S(2)}) copy-start(f32[1,2,6400]{2,1,0:T(2,128)} %param.17) | copy-start | bytes 153604
  1.3 6.5 %copy-start.2 = (s32[1,6400]{1,0:T(1,128)S(1)}, s32[1,6400]{1,0:T(1,128)}, u32[]{:S(2)}) copy-start(s32[1,6400]{1,0:T(1,128)} %param.16) | copy-start | bytes 76804
  1.3 6.5 %copy-start = (f32[1024]{0:T(1024)S(1)}, f32[1024]{0:T(1024)}, u32[]{:S(2)}) copy-start(f32[1024]{0:T(1024)} %wav.1) | copy-start | bytes 12292
  2.7 15.6 %collective-permute-start.2 = (f32[3,96,256]{2,1,0:T(8,128)S(1)}, f32[3,96,256]{2,1,0:T(8,128)S(1)}, u32[]{:S(2)}, u32[]{:S(2)}) collective-permute-start(f32[3,96,256]{2,1,0:T(8,128)S(1)} %get-tuple-element.33.after), channel_id=1, source_target_pairs={{0,2},{2,0},{4,6},{6,4},{8,10},{10,8},{12,14},{14,12},{1,3},{3,1},... | collective-permute-start | bytes 884744 | tf_op jit(solution)/shard_map/ppermute | solution.py:434
  5.7 9.5 %collective-permute-start = (f32[3,96,256]{2,1,0:T(8,128)S(1)}, f32[3,96,256]{2,1,0:T(8,128)S(1)}, u32[]{:S(2)}, u32[]{:S(2)}) collective-permute-start(f32[3,96,256]{2,1,0:T(8,128)S(1)} %get-tuple-element.32), channel_id=1, source_target_pairs={{2,4},{4,2},{6,8},{8,6},{10,12},{12,10},{3,5},{5,3},{7,9},{9,7},{1... | collective-permute-start | bytes 884744 | tf_op jit(solution)/shard_map/ppermute | solution.py:433
  15.3 11.3 %collective-permute-start.1 = (f32[2,96,256]{2,1,0:T(8,128)S(1)}, f32[2,96,256]{2,1,0:T(8,128)S(1)}, u32[]{:S(2)}, u32[]{:S(2)}) collective-permute-start(f32[2,96,256]{2,1,0:T(8,128)S(1)} %get-tuple-element.41.send_b.send), channel_id=1, source_target_pairs={{2,4},{4,2},{6,8},{8,6},{10,12},{12,10},{3,5},{5,3},{7,9},{9,7},{1... | collective-permute-start | bytes 589832 | tf_op jit(solution)/shard_map/ppermute | solution.py:469
  18.4 11.1 %collective-permute-start.4 = (f32[2,96,256]{2,1,0:T(8,128)S(1)}, f32[2,96,256]{2,1,0:T(8,128)S(1)}, u32[]{:S(2)}, u32[]{:S(2)}) collective-permute-start(f32[2,96,256]{2,1,0:T(8,128)S(1)} %get-tuple-element.43.send_a.send), channel_id=1, source_target_pairs={{0,2},{2,0},{4,6},{6,4},{8,10},{10,8},{12,14},{14,12},{1,3},{3,1},... | collective-permute-start | bytes 589832 | tf_op jit(solution)/shard_map/ppermute | solution.py:471
  27.3 4.3 %collective-permute-start.3 = (f32[2,8,64,256]{3,2,1,0:T(8,128)S(1)}, f32[2,8,64,256]{3,2,1,0:T(8,128)S(1)}, u32[]{:S(2)}, u32[]{:S(2)}) collective-permute-start(f32[2,8,64,256]{3,2,1,0:T(8,128)S(1)} %get-tuple-element.54), channel_id=1, source_target_pairs={{0,1},{1,0},{2,3},{3,2},{4,5},{5,4},{6,7},{7,6},{8,9},{9,8},{10,11... | collective-permute-start | bytes 3145736 | tf_op jit(solution)/shard_map/ppermute | solution.py:502
  30.2 1.4 %collective-permute-start.5 = (f32[2,64,256]{2,1,0:T(8,128)S(1)}, f32[2,64,256]{2,1,0:T(8,128)S(1)}, u32[]{:S(2)}, u32[]{:S(2)}) collective-permute-start(f32[2,64,256]{2,1,0:T(8,128)S(1)} %get-tuple-element.57), channel_id=1, source_target_pairs={{0,1},{1,0},{2,3},{3,2},{4,5},{5,4},{6,7},{7,6},{8,9},{9,8},{10,11... | collective-permute-start | bytes 393224 | tf_op jit(solution)/shard_map/ppermute | solution.py:517

commit v3 on v2

v3 whole, which is shorter than its diff:
```python
import functools

import jax
import jax.numpy as jnp
from jax import lax
from jax.experimental import pallas as pl
from jax.experimental.pallas import tpu as pltpu
from jax.sharding import PartitionSpec as P

F32 = jnp.float32
BF16 = jnp.bfloat16
LANES = 128
TILE = 8
GROUP_ROWS = 5
CHUNK = 16
LEAD = 0
RECV_COST = 40
ENDS_COST = 40
MIDDLE_COST = 40
EDGE_COST = 1
TWO_COST = (40, 2)
EDGE_B_COST = 2

VM = pl.BlockSpec(memory_space=pltpu.VMEM)
SM = pl.BlockSpec(memory_space=pltpu.SMEM)
ANY = pl.BlockSpec(memory_space=pl.ANY)


def vmem(*shape):
    return pltpu.VMEM(shape, F32)


def near(x):
    return pltpu.with_memory_space_constraint(x, pltpu.VMEM)


def far(x):
    return pltpu.with_memory_space_constraint(x, pltpu.HBM)


def cost(us):
    return pl.CostEstimate(flops=int(us * 1_000_000_000), bytes_accessed=1024, transcendentals=0)


def params():
    return pltpu.CompilerParams(vmem_limit_bytes=24 * 1024 * 1024)


def edges(width):
    even = lax.rem(lax.axis_index("dom"), 2) == 0
    last = jnp.int32(width - 1)
    first = jnp.int32(0)
    ends = jnp.where(even, last, first), jnp.where(even, first, last)
    return ends[LEAD], ends[1 - LEAD]


def window(block, off, ny):
    rows = block.shape[0]
    return pltpu.roll(block, lax.rem(rows - off, rows), 0)[:ny]


def placed(plane, off, rows):
    fill = jnp.zeros((rows - plane.shape[0], plane.shape[1]), plane.dtype)
    return pltpu.roll(jnp.concatenate([plane, fill], axis=0), off, 0)


def edge_copies(edge, ckpt, adj, kappa, buoy, send, q_e, k_e, b_e, sem):
    return [
        pltpu.make_async_copy(adj.at[0, 1, edge], q_e, sem.at[1]),
        pltpu.make_async_copy(kappa.at[edge], k_e, sem.at[2]),
        pltpu.make_async_copy(buoy.at[edge], b_e, sem.at[3]),
        pltpu.make_async_copy(ckpt.at[0, 1, edge], send.at[0], sem.at[0]),
    ]


def edge_fill(off, send, q_e, k_e, b_e):
    ny = q_e.shape[0]
    send[1] = window(k_e[...], off, ny) * q_e[...]
    send[2] = window(b_e[...], off, ny)


def first_send(off, ckpt, adj, kappa, buoy, send, q_e, k_e, b_e, sem):
    edge = edges(ckpt.shape[2])[0]
    copies = edge_copies(edge, ckpt, adj, kappa, buoy, send, q_e, k_e, b_e, sem)
    for copy in copies:
        copy.start()
    for copy in copies:
        copy.wait()
    edge_fill(off[0], send, q_e, k_e, b_e)


def receivers(
    off, rec, res, ckpt, adj, kappa, buoy, after, total, send,
    q_e, k_e, b_e, cell_s, rank_s, row_a_s, row_b_s, z_s, val_s, left, right_hi, right_lo, sem,
):
    nz = total.shape[1] // 2
    edge = edges(ckpt.shape[2])[1]
    copies = edge_copies(edge, ckpt, adj, kappa, buoy, send, q_e, k_e, b_e, sem)
    for copy in copies:
        copy.start()
    rows, lanes = cell_s.shape
    for r in range(rows):
        at = pl.ds(r * lanes, lanes)
        cell_s[r : r + 1, :] = rec[:, at]
        for step in range(2):
            val_s[2 * step, r : r + 1, :] = res[0, step : step + 1, at]
    cells = total.shape[0] * nz
    shift = nz.bit_length() - 1
    local = cell_s[...] - lax.axis_index("dom") * cells
    inside = (local >= 0) & (local < cells)
    row = lax.shift_right_logical(local, jnp.int32(shift))
    row_a_s[...] = lax.shift_right_logical(row, jnp.int32(2)).astype(F32)
    row_b_s[...] = (row & 3).astype(F32)
    z_s[...] = (local & (nz - 1)).astype(F32)
    for step in range(2):
        value = val_s[2 * step]
        high = value.astype(BF16).astype(F32)
        val_s[2 * step] = high
        val_s[2 * step + 1] = value - high
    mask = jnp.where(inside, 1.0, 0.0).astype(BF16)
    before = lax.broadcasted_iota(jnp.int32, (lanes, lanes), 0) < lax.broadcasted_iota(
        jnp.int32, (lanes, lanes), 1
    )
    in_row = jnp.dot(mask, jnp.where(before, 1.0, 0.0).astype(BF16), preferred_element_type=F32)
    row_sum = jnp.dot(mask, jnp.ones((lanes, lanes), BF16), preferred_element_type=F32)
    r = lax.broadcasted_iota(jnp.int32, (rows, rows), 0)
    c = lax.broadcasted_iota(jnp.int32, (rows, rows), 1)
    group_r = lax.shift_right_logical(r * 3277, jnp.int32(14))
    group_c = lax.shift_right_logical(c * 3277, jnp.int32(14))
    earlier = jnp.where((group_r == group_c) & (c < r), 1.0, 0.0).astype(BF16)
    row_start = jnp.dot(earlier, row_sum.astype(BF16), preferred_element_type=F32)
    rank = jnp.where(inside, in_row + row_start, -1.0)
    rank_s[...] = rank
    passes = lax.shift_right_logical(jnp.max(rank).astype(jnp.int32), jnp.int32(7)) + 1
    groups = rows // GROUP_ROWS
    slot = lax.broadcasted_iota(jnp.int32, (LANES, lanes), 0).astype(F32)
    sub8 = lax.broadcasted_iota(jnp.int32, (TILE, lanes), 0)
    row_iota = lax.broadcasted_iota(jnp.int32, (left.shape[0], LANES), 0).astype(F32)
    depth_iota = lax.broadcasted_iota(jnp.int32, (LANES, nz), 1).astype(F32)

    def one_pass(base, first):
        for g in range(groups):
            picks = []
            fields = []
            for n in range(GROUP_ROWS):
                at = pl.ds(g * GROUP_ROWS + n, 1)
                want = jnp.broadcast_to(rank_s[at, :] - base, (LANES, lanes))
                picks.append(jnp.where(want == slot, 1.0, 0.0).astype(BF16))
                data = jnp.zeros((TILE, lanes), F32)
                sources = [row_a_s, row_b_s, z_s] + [val_s.at[m] for m in range(4)]
                for m, source in enumerate(sources):
                    data = jnp.where(sub8 == m, jnp.broadcast_to(source[at, :], (TILE, lanes)), data)
                fields.append(data.astype(BF16))
            pick = jnp.concatenate(picks, axis=1)
            data = jnp.concatenate(fields, axis=1)
            dims = (((1,), (1,)), ((), ()))
            by_slot = lax.dot_general(pick, data, dims, preferred_element_type=F32)
            by_field = lax.dot_general(data, pick, dims, preferred_element_type=F32)
            where_row = by_field[0:1, :] * 4.0 + by_field[1:2, :]
            here = pl.ds(g * LANES, LANES)
            left[:, here] = jnp.where(row_iota == where_row, 1.0, 0.0).astype(BF16)
            same = by_slot[:, 2:3] == depth_iota
            for step in range(2):
                cols = pl.ds(step * nz, nz)
                high = by_slot[:, 3 + 2 * step : 4 + 2 * step]
                low = by_slot[:, 4 + 2 * step : 5 + 2 * step]
                right_hi[here, cols] = jnp.where(same, high, 0.0).astype(BF16)
                right_lo[here, cols] = jnp.where(same, low, 0.0).astype(BF16)
        out = jnp.dot(left[...], right_hi[...], preferred_element_type=F32) + jnp.dot(
            left[...], right_lo[...], preferred_element_type=F32
        )
        if first:
            total[...] = out
        else:
            total[...] += out

    one_pass(0.0, True)

    @pl.when(passes > 1)
    def _():
        def body(number, carry):
            one_pass((number * LANES).astype(F32), False)
            return carry

        lax.fori_loop(1, passes, body, 0)

    for copy in copies:
        copy.wait()
    edge_fill(off[0], send, q_e, k_e, b_e)


def next_row(f, tile):
    rows = f.shape[0]
    return pltpu.roll(jnp.concatenate([f, tile], axis=0), rows + TILE - 1, 0)[:rows]


def last_row(f, tile):
    return pltpu.roll(jnp.concatenate([tile, f], axis=0), 1, 0)[TILE:]


def next_depth(blocks, end):
    moved = [pltpu.roll(f, LANES - 1, 1) for f in blocks]
    return [jnp.where(end, behind, here) for here, behind in zip(moved, moved[1:] + [0.0])]


def last_depth(blocks, start, first):
    moved = [pltpu.roll(g, 1, 1) for g in blocks]
    return [jnp.where(start, ahead, here) for here, ahead in zip(moved, [first] + moved[:-1])]


class Chunks:
    def __init__(self, ny, nz):
        self.starts = list(range(0, ny, CHUNK))
        self.ny = ny
        self.blocks = nz // LANES
        lane = lax.broadcasted_iota(jnp.int32, (CHUNK, LANES), 1)
        row = lax.broadcasted_iota(jnp.int32, (CHUNK, LANES), 0)
        self.end = lane == LANES - 1
        self.start = lane == 0
        self.top = row == 0

    def load(self, ref, lead, y):
        return [ref[(*lead, pl.ds(y, CHUNK), pl.ds(n * LANES, LANES))] for n in range(self.blocks)]

    def store(self, ref, lead, y, values):
        for n, value in enumerate(values):
            ref[(*lead, pl.ds(y, CHUNK), pl.ds(n * LANES, LANES))] = value

    def behind(self, ref, lead, y):
        if y + CHUNK == self.ny:
            return [jnp.zeros((TILE, LANES), F32)] * self.blocks
        return [
            ref[(*lead, pl.ds(y + CHUNK, TILE), pl.ds(n * LANES, LANES))] for n in range(self.blocks)
        ]

    def rows_up(self, ref, lead, y, f):
        return [next_row(a, b) for a, b in zip(f, self.behind(ref, lead, y))]

    def diffs(self, ref, x, xn, y):
        f = self.load(ref, (x,), y)
        dx = [a - b for a, b in zip(self.load(ref, (xn,), y), f)]
        dy = [a - b for a, b in zip(self.rows_up(ref, (x,), y, f), f)]
        dz = [a - b for a, b in zip(next_depth(f, self.end), f)]
        return f, dx, dy, dz

    def lap(self, d, faces, h, gx_ref, slot, y, carry):
        f, dx, dy, dz = d
        gx, gy, gz = ([a * b for a, b in zip(face, diff)] for face, diff in zip(faces, (dx, dy, dz)))
        old = self.load(gx_ref, (slot,), y)
        self.store(gx_ref, (slot,), y, gx)
        if y == 0:
            ahead = [jnp.where(self.top, a * b, pltpu.roll(g, 1, 0)) for a, b, g in zip(h, f, gy)]
        else:
            ahead = [last_row(g, t) for g, t in zip(gy, carry)]
        back = last_depth(gz, self.start, h[0] * f[0])
        out = [
            (a - b) + (c - e) + (m - n) for a, b, c, e, m, n in zip(gx, old, gy, ahead, gz, back)
        ]
        return out, [g[CHUNK - TILE :] for g in gy]


def one_plane(ch, x, xn, p, q, kq, kw, hb, p_old, q_late, total, fy_o, fz_o, lap_o, pn, qm, kqm, gx_s):
    ny = ch.ny
    tail_p = tail_q = None
    for y in ch.starts:
        h = ch.load(hb, (x,), y)
        fx = [a + b for a, b in zip(h, ch.load(hb, (xn,), y))]
        fy = [a + b for a, b in zip(h, ch.rows_up(hb, (x,), y, h))]
        fz = [a + b for a, b in zip(h, next_depth(h, ch.end))]
        ch.store(fy_o, (x,), y, fy)
        ch.store(fz_o, (x,), y, fz)
        faces = (fx, fy, fz)
        k = ch.load(kw, (x,), y)
        d = ch.diffs(p, x, xn, y)
        lap_p, tail_p = ch.lap(d, faces, h, gx_s, 0, y, tail_p)
        ch.store(lap_o, (x,), y, lap_p)
        old = ch.load(p_old, (x,), y)
        ch.store(pn, (x,), y, [2.0 * a - b + c * e for a, b, c, e in zip(d[0], old, k, lap_p)])
        d = ch.diffs(kq, x, xn, y)
        lap_q, tail_q = ch.lap(d, faces, h, gx_s, 1, y, tail_q)
        now = ch.load(q, (x,), y)
        late = ch.load(q_late, (x,), y)
        at = pl.ds(pl.multiple_of(x * ny + y, TILE), CHUNK)
        add = [total[at, pl.ds(n * LANES, LANES)] for n in range(ch.blocks)]
        mid = [2.0 * a - b + c + e for a, b, c, e in zip(now, late, lap_q, add)]
        ch.store(qm, (x,), y, mid)
        ch.store(kqm, (x,), y, [a * b for a, b in zip(k, mid)])


def add_source(step, src, wav, pn, low, high):
    width, ny, nz = pn.shape
    cell = src[0] - lax.axis_index("dom") * (width * ny * nz)
    plane = ny * nz

    @pl.when((cell >= low * plane) & (cell < high * plane))
    def _():
        shift = nz.bit_length() - 1
        row = lax.shift_right_logical(cell, jnp.int32(shift))
        x = lax.div(row, jnp.int32(ny))
        y = row - x * ny
        spot = lax.broadcasted_iota(jnp.int32, (1, nz), 1) == (cell & (nz - 1))
        pn[x, pl.ds(y, 1), :] += jnp.where(spot, wav[step[0]], 0.0)


def step_one_ends(
    off, step, src, wav_in, ckpt, adj, k_full, b_full, total, after,
    kq, kw, hb, fy, fz, lap, pn, qm, kqm,
    gx_s, wav, sem,
):
    width, ny, nz = kq.shape
    copy = pltpu.make_async_copy(wav_in, wav, sem.at[0])
    copy.start()
    p_old, p, q_late, q = ckpt.at[0, 0], ckpt.at[0, 1], adj.at[0, 0], adj.at[0, 1]

    def windows(x, carry):
        k = window(k_full[x], off[0], ny)
        kw[x] = k
        kq[x] = k * q[x]
        hb[x] = 0.5 * window(b_full[x], off[0], ny)
        return carry

    lax.fori_loop(0, width, windows, 0)
    ch = Chunks(ny, nz)
    end = width - 1
    rest = (p, q, kq, kw, hb, p_old, q_late, total, fy, fz, lap, pn, qm, kqm, gx_s)

    def ends(n, carry):
        x = n * end
        before = jnp.maximum(x - 1, 0)
        face = hb[before] + hb[x]
        gx_s[0] = face * (p[x] - p[before])
        gx_s[1] = face * (kq[x] - kq[before])
        one_plane(ch, x, jnp.minimum(x + 1, end), *rest)
        return carry

    lax.fori_loop(0, 2, ends, 0)
    copy.wait()
    add_source(step, src, wav, pn, 0, 1)
    add_source(step, src, wav, pn, end, width)


def step_one_middle(
    step, src, wav_in, ckpt, adj, kq, kw, hb, total, fy_i, fz_i, lap_i, pn_i, qm_i, kqm_i,
    fy, fz, lap, pn, qm, kqm,
    gx_s, wav, sem,
):
    width, ny, nz = kq.shape
    copy = pltpu.make_async_copy(wav_in, wav, sem.at[0])
    copy.start()
    p_old, p, q_late, q = ckpt.at[0, 0], ckpt.at[0, 1], adj.at[0, 0], adj.at[0, 1]
    ch = Chunks(ny, nz)
    face = hb[0] + hb[1]
    gx_s[0] = face * (p[1] - p[0])
    gx_s[1] = face * (kq[1] - kq[0])

    def plane(x, carry):
        one_plane(ch, x, x + 1, p, q, kq, kw, hb, p_old, q_late, total, fy, fz, lap, pn, qm, kqm, gx_s)
        return carry

    lax.fori_loop(1, width - 1, plane, 0)
    copy.wait()
    add_source(step, src, wav, pn, 1, width - 1)


def edge_one(which, recv, ckpt, kq, kw, hb, lap_i, pn_i, qm_i, kqm_i, send, lap, pn, qm, kqm):
    edge = edges(kq.shape[0])[which]
    p = ckpt.at[0, 1]
    face = hb[edge] + 0.5 * recv[2]
    flux = face * (recv[0] - p[edge])
    lap[edge] = lap_i[edge] + flux
    k = kw[edge]
    new = pn_i[edge] + k * flux
    send[0] = new
    pn[edge] = new
    mid = qm_i[edge] + face * (recv[1] - kq[edge])
    qm[edge] = mid
    mid = k * mid
    send[1] = mid
    kqm[edge] = mid


def step_two(part, ckpt, adj, kq, hb, fy_i, fz_i, lap_i, pn, qm, kqm, total, *refs):
    last, parts, gx_s = refs[-3:]
    width, ny, nz = kq.shape
    p, q = ckpt.at[0, 1], adj.at[0, 1]
    at_end = edges(width)[1] == width - 1
    if part == 0:
        low = jnp.where(at_end, 0, 2)
        high = low + width - 2
    else:
        low = jnp.where(at_end, width - 2, 0)
        high = low + 2
    before = jnp.maximum(low - 1, 0)
    face = hb[before] + hb[low]
    gx_s[0] = face * (pn[low] - pn[before])
    gx_s[1] = face * (kqm[low] - kqm[before])
    ch = Chunks(ny, nz)

    def plane(x, carry):
        xn = jnp.minimum(x + 1, width - 1)
        tail_p = tail_q = None
        for y in ch.starts:
            h = ch.load(hb, (x,), y)
            fx = [a + b for a, b in zip(h, ch.load(hb, (xn,), y))]
            faces = (fx, ch.load(fy_i, (x,), y), ch.load(fz_i, (x,), y))
            dpn = ch.diffs(pn, x, xn, y)
            lap_p, tail_p = ch.lap(dpn, faces, h, gx_s, 0, y, tail_p)
            mid = ch.load(qm, (x,), y)
            now = ch.load(q, (x,), y)
            lap_1 = ch.load(lap_i, (x,), y)
            ch.store(parts, (0, x), y, [a * b + c * e for a, b, c, e in zip(mid, lap_1, now, lap_p)])
            dqm = ch.diffs(kqm, x, xn, y)
            lap_q, tail_q = ch.lap(dqm, faces, h, gx_s, 1, y, tail_q)
            add = [
                total[pl.ds(pl.multiple_of(x * ny + y, TILE), CHUNK), pl.ds(nz + n * LANES, LANES)]
                for n in range(ch.blocks)
            ]
            ch.store(last, (x,), y, [2.0 * a - b + c + e for a, b, c, e in zip(mid, now, lap_q, add)])
            dp = ch.diffs(p, x, xn, y)
            sums = [
                sum(a * b for a, b in zip(u, v))
                for u, v in zip(zip(*dp[1:]), zip(*dqm[1:]))
            ]
            dq = ch.diffs(kq, x, xn, y)
            sums = [
                s + sum(a * b for a, b in zip(u, v))
                for s, u, v in zip(sums, zip(*dpn[1:]), zip(*dq[1:]))
            ]
            ch.store(parts, (1, x), y, [-s for s in sums])
        return carry

    lax.fori_loop(low, high, plane, 0)


def edge_terms(edge, recv, recv2, send, ckpt, adj, kq, hb):
    p, q = ckpt.at[0, 1], adj.at[0, 1]
    face = hb[edge] + 0.5 * recv[2]
    dpn = recv2[0] - send[0]
    dqm = recv2[1] - send[1]
    add_k = q[edge] * (face * dpn)
    add_b = -(dqm * (recv[0] - p[edge]) + dpn * (recv[1] - kq[edge]))
    return face * dqm, add_k, jnp.where(edge == kq.shape[0] - 1, add_b, 0.0)


def split(plane, off, half):
    whole = placed(plane, off, 2 * half)
    shot = lax.axis_index("shot")
    return (
        jnp.where(shot == 0, whole[:half], whole[half:]),
        jnp.where(shot == 0, whole[half:], whole[:half]),
    )


def first_edge_two(
    off, recv, recv2, send, ckpt, adj, kq, hb, last_i, parts, qm,
    adj_out, last, mine, other, add, sem,
):
    width = kq.shape[0]
    mid_copy = pltpu.make_async_copy(qm, adj_out.at[0, 0], sem.at[1])
    mid_copy.start()
    half = mine.shape[2]
    edge = edges(width)[0]
    add_q, add[0], add[1] = edge_terms(edge, recv, recv2, send, ckpt, adj, kq, hb)
    last[edge] = last_i[edge] + add_q
    copy = pltpu.make_async_copy(last, adj_out.at[0, 1], sem.at[0])
    copy.start()

    def plane(x, carry):
        here = jnp.where(x == edge, 1.0, 0.0)
        for g in range(2):
            mine[g, x], other[g, x] = split(parts[g, x] + here * add[g], off[0], half)
        return carry

    lax.fori_loop(0, width, plane, 0)
    copy.wait()
    mid_copy.wait()


def second_edge_two(off, recv, recv2, send, ckpt, adj, kq, hb, last, mine, other, last_e):
    half = mine.shape[1]
    edge = edges(kq.shape[0])[1]
    add_q, add_k, add_b = edge_terms(edge, recv, recv2, send, ckpt, adj, kq, hb)
    last_e[...] = last[edge] + add_q
    mine[0], other[0] = split(add_k, off[0], half)
    mine[1], other[1] = split(add_b, off[0], half)


def combine(mine, recv, mine_e, grad_k, grad_b, sums_e, sums, sem):
    edge = edges(sums.shape[1])[1]
    copies = []
    for g, grad in enumerate((grad_k, grad_b)):
        sums[g] = mine[g] + recv[g]
        copy = pltpu.make_async_copy(sums.at[g], grad, sem.at[g])
        copy.start()
        copies.append(copy)
    for g in range(2):
        sums_e[g] = sums[g, edge] + mine_e[g]
    for copy in copies:
        copy.wait()


def finish(sums_e, recv_e, last_e, grad_k_in, grad_b_in, adj_in, grad_k, grad_b, adj_out, sums, sem):
    edge = edges(grad_k.shape[0])[1]
    copies = [pltpu.make_async_copy(last_e, adj_out.at[0, 1, edge], sem.at[2])]
    copies[0].start()
    for g, grad in enumerate((grad_k, grad_b)):
        sums[g] = sums_e[g] + recv_e[g]
        copy = pltpu.make_async_copy(sums.at[g], grad.at[edge], sem.at[g])
        copy.start()
        copies.append(copy)
    for copy in copies:
        copy.wait()


def pairs(count, first):
    out = []
    for low in range(first, count - 1, 2):
        out += [(low, low + 1), (low + 1, low)]
    return out


def shards(
    checkpoint, adjoint, kappa, buoyancy, wavelet, src_cell, rec_cell, residuals, offsets, ckpt_step
):
    width, ny, nz = checkpoint.shape[2:]
    model_y = kappa.shape[1]
    half = model_y // 2
    count = lax.axis_size("dom")
    swaps = pairs(count, LEAD), pairs(count, 1 - LEAD)
    rrows = rec_cell.shape[1] // LANES
    slots = rrows // GROUP_ROWS * LANES
    layer = (ny, nz)
    field = (width, ny, nz)
    dma = pltpu.SemaphoreType.DMA
    adj_shape = pltpu.HBM((1, 2, *field), F32)
    grad_shape = pltpu.HBM((width, half, nz), F32)

    inputs = [far(x) for x in (checkpoint, adjoint, kappa, buoyancy)]
    edge_scratch = [vmem(*layer), vmem(model_y, nz), vmem(model_y, nz)]
    send_1 = pl.pallas_call(
        first_send,
        in_specs=[SM] + [ANY] * 4,
        out_specs=VM,
        out_shape=vmem(3, *layer),
        scratch_shapes=edge_scratch + [dma((4,))],
        compiler_params=params(),
    )(offsets, *inputs)
    recv_1 = lax.ppermute(send_1, "dom", swaps[0])

    total, send_2 = pl.pallas_call(
        receivers,
        in_specs=[SM, VM, VM] + [ANY] * 4 + [VM],
        out_specs=[VM, VM],
        out_shape=[vmem(width * ny, 2 * nz), vmem(3, *layer)],
        scratch_shapes=edge_scratch + [
            pltpu.VMEM((rrows, LANES), jnp.int32),
            vmem(rrows, LANES), vmem(rrows, LANES), vmem(rrows, LANES), vmem(rrows, LANES),
            vmem(4, rrows, LANES),
            pltpu.VMEM((width * ny, slots), BF16),
            pltpu.VMEM((slots, 2 * nz), BF16),
            pltpu.VMEM((slots, 2 * nz), BF16),
            dma((4,)),
        ],
        compiler_params=params(),
        cost_estimate=cost(RECV_COST),
    )(offsets, near(rec_cell), near(residuals), *inputs, near(send_1))
    recv_2 = lax.ppermute(send_2, "dom", swaps[1])

    kq, kw, hb, *state = pl.pallas_call(
        step_one_ends,
        in_specs=[SM] * 3 + [ANY] + [VM] * 6,
        out_specs=[VM] * 9,
        out_shape=[vmem(*field)] * 9,
        scratch_shapes=[vmem(2, *layer), pltpu.SMEM(wavelet.shape, F32), dma((1,))],
        compiler_params=params(),
        cost_estimate=cost(ENDS_COST),
    )(
        offsets, ckpt_step, src_cell, far(wavelet),
        *[near(v) for v in (checkpoint, adjoint, kappa, buoyancy, total, send_2)],
    )

    def first_edge(which, recv, state):
        send, *new = pl.pallas_call(
            functools.partial(edge_one, which),
            in_specs=[VM] * 9,
            out_specs=[VM] * 5,
            out_shape=[vmem(2, *layer)] + [vmem(*field)] * 4,
            input_output_aliases={5: 1, 6: 2, 7: 3, 8: 4},
            compiler_params=params(),
            cost_estimate=cost(EDGE_COST),
        )(*[near(v) for v in (recv, checkpoint, kq, kw, hb, *state[2:])])
        return send, list(state[:2]) + list(new)

    send2_1, state = first_edge(0, recv_1, state)
    recv2_1 = lax.ppermute(send2_1, "dom", swaps[0])
    state = pl.pallas_call(
        step_one_middle,
        in_specs=[SM] * 2 + [ANY] + [VM] * 12,
        out_specs=[VM] * 6,
        out_shape=[vmem(*field)] * 6,
        scratch_shapes=[vmem(2, *layer), pltpu.SMEM(wavelet.shape, F32), dma((1,))],
        input_output_aliases={9 + n: n for n in range(6)},
        compiler_params=params(),
        cost_estimate=cost(MIDDLE_COST),
    )(
        ckpt_step, src_cell, far(wavelet),
        *[near(v) for v in (checkpoint, adjoint, kq, kw, hb, total, *state)],
    )
    def second_step(part, state, *partial):
        out_shape = [vmem(*field), vmem(2, *field)]
        return pl.pallas_call(
            functools.partial(step_two, part),
            in_specs=[VM] * (11 + len(partial)),
            out_specs=[VM, VM],
            out_shape=out_shape,
            scratch_shapes=[vmem(2, *layer)],
            input_output_aliases={11 + n: n for n in range(len(partial))},
            compiler_params=params(),
            cost_estimate=cost(TWO_COST[part]),
        )(*[near(v) for v in (checkpoint, adjoint, kq, hb, *state, total, *partial)])

    partial = second_step(0, state)
    send2_2, state = first_edge(1, recv_2, state)
    recv2_2 = lax.ppermute(send2_2, "dom", swaps[1])
    last, parts = second_step(1, state, *partial)
    swap = [(0, 1), (1, 0)]
    adj_part, last, mine, other = pl.pallas_call(
        first_edge_two,
        in_specs=[SM] + [VM] * 10,
        out_specs=[ANY, VM, VM, VM],
        out_shape=[adj_shape, vmem(*field), vmem(2, width, half, nz), vmem(2, width, half, nz)],
        scratch_shapes=[vmem(2, *layer), dma((2,))],
        input_output_aliases={8: 1},
        compiler_params=params(),
        cost_estimate=cost(EDGE_B_COST),
    )(
        offsets,
        *[near(v) for v in (recv_1, recv2_1, send2_1, checkpoint, adjoint, kq, hb, last, parts, state[4])],
    )
    recv_g = lax.ppermute(other, "shot", swap)
    mine_e, other_e, last_e = pl.pallas_call(
        second_edge_two,
        in_specs=[SM] + [VM] * 8,
        out_specs=[VM, VM, VM],
        out_shape=[vmem(2, half, nz), vmem(2, half, nz), vmem(*layer)],
        compiler_params=params(),
        cost_estimate=cost(40),
    )(offsets, *[near(v) for v in (recv_2, recv2_2, send2_2, checkpoint, adjoint, kq, hb, last)])
    recv_e = lax.ppermute(other_e, "shot", swap)
    grad_k, grad_b, sums_e = pl.pallas_call(
        combine,
        in_specs=[VM] * 3,
        out_specs=[ANY, ANY, VM],
        out_shape=[grad_shape, grad_shape, vmem(2, half, nz)],
        scratch_shapes=[vmem(2, width, half, nz), dma((2,))],
        compiler_params=params(),
        cost_estimate=cost(40),
    )(near(mine), near(recv_g), near(mine_e))
    return pl.pallas_call(
        finish,
        in_specs=[VM] * 3 + [ANY] * 3,
        out_specs=[ANY] * 3,
        out_shape=[grad_shape, grad_shape, adj_shape],
        scratch_shapes=[vmem(2, half, nz), dma((3,))],
        input_output_aliases={3: 0, 4: 1, 5: 2},
        compiler_params=params(),
    )(near(sums_e), near(recv_e), near(last_e), far(grad_k), far(grad_b), far(adj_part))


def solution(mesh):
    in_specs = (
        P(("group", "shot"), None, "dom", None, None),
        P(("group", "shot"), None, "dom", None, None),
        P(("group", "dom"), None, None),
        P(("group", "dom"), None, None),
        P(),
        P(("group", "shot")),
        P(("group", "shot"), None),
        P(("group", "shot"), None, None),
        P(("group", "shot")),
        P(("group", "shot")),
    )
    out_specs = (
        P(("group", "dom"), "shot", None),
        P(("group", "dom"), "shot", None),
        P(("group", "shot"), None, "dom", None, None),
    )
    return jax.shard_map(shards, mesh=mesh, in_specs=in_specs, out_specs=out_specs, check_vma=False)
```

time: 32.9 us -> 30.9 us (0.939)
  the two profiles are of different devices: /device:TPU:0 before, /device:TPU:9 now
where the time goes in v3:
time: 30.9 us; the launch traced here: 30.7 us
  Pallas kernels  13.8 us (45%)
  starting transfers between devices  10.7 us (35%)
  waiting for transfers between devices  3.32 us (11%)
  between operations  2.77 us (9%)
    pallas_call x1, Pallas kernels, shards(): pl.pallas_call(receivers, in_specs=[SM, VM, VM] + [ANY] * 4 + [VM], out_s...  3.76 us
    pallas_call x2, Pallas kernels, second_step(): pl.pallas_call(functools.partial(step_two, part), in_specs=[VM] * (11 + l...  2.74 us
    ppermute x1, starting transfers between devices, shards(): recv2_1 = lax.ppermute(send2_1, 'dom', swaps[0])  2.53 us
    ppermute x1, starting transfers between devices, shards(): recv_e = lax.ppermute(other_e, 'shot', swap)  2.5 us
    ppermute x1, waiting for transfers between devices, shards(): recv2_1 = lax.ppermute(send2_1, 'dom', swaps[0])  2.28 us
    ppermute x1, starting transfers between devices, shards(): recv_2 = lax.ppermute(send_2, 'dom', swaps[1])  1.92 us
    ppermute x1, starting transfers between devices, shards(): recv2_2 = lax.ppermute(send2_2, 'dom', swaps[1])  1.92 us
    pallas_call x1, Pallas kernels, shards(): pl.pallas_call(step_one_middle, in_specs=[SM] * 2 + [ANY] + [VM] * 12, ou...  1.7 us
  transfers between devices with their start and end apart: 6, of which 2 were waited for; matrix products, arithmetic and copies ran while one was open for 0% of the time, Pallas kernels for 39%

profile of v3, /device:TPU:9, one launch (start us, length us, event | category | flops | bytes accessed | tf_op | source)
XLA Modules:
  0.0 30.7 jit_solution(1889707476742129829)
XLA Ops:
  1.3 0.0 copy-start.4
  1.3 0.0 copy-start.5
  1.3 1.2 %shard_map.121.after = f32[3,96,256]{2,1,0:T(8,128)S(1)} custom-call(s32[1]{0:T(128)S(6)} %copy.54.off, f32[1,2,8,96,256]{4,3,2,1,0:T(8,128)} %ckpt.19, f32[1,2,8,96,256]{4,3,2,1,0:T(8,128)} %adj.15, f32[8,128,256]{2,1,0:T(8,128)} %k_full.1, f32[8,128,256]{2,1,0:T(8,128)} %b_full.1), custom_call_target="tpu_custom_call" | custom-call | tf_op jit(solution)/shard_map/pallas_call | solution.py:540
  2.5 0.0 copy-start
  2.5 0.0 copy-start.1
  2.5 0.0 copy-start.2
  2.5 0.0 copy-start.3
  2.5 1.3 %collective-permute-start = (f32[3,96,256]{2,1,0:T(8,128)S(1)}, f32[3,96,256]{2,1,0:T(8,128)S(1)}, u32[]{:S(2)}, u32[]{:S(2)}) collective-permute-start(f32[3,96,256]{2,1,0:T(8,128)S(1)} %shard_map.121.after), channel_id=1, source_target_pairs={{0,2},{2,0},{4,6},{6,4},{8,10},{10,8},{12,14},{14,12},{1,3},{3,1},... | collective-permute-start | bytes 884744 | tf_op jit(solution)/shard_map/ppermute | solution.py:548
  3.8 0.0 copy-done.4
  3.8 0.0 copy-done.5
  3.8 3.8 %shard_map.122 = (f32[768,512]{1,0:T(8,128)S(1)}, f32[3,96,256]{2,1,0:T(8,128)S(1)}) custom-call(s32[1]{0:T(128)S(6)} %copy.54.off, s32[1,6400]{1,0:T(1,128)S(1)} %copy-done.5, f32[1,2,6400]{2,1,0:T(2,128)S(1)} %copy-done.4, f32[1,2,8,96,256]{4,3,2,1,0:T(8,128)} %ckpt.19, f32[1,2,8,96,256]{4,3,2,1,0:T(8,128)} %adj.15, f32[8,128,256]{2,1,0:T(8,128)} %k_full.1, ...), custom_call_target="tpu_custom_call" | custom-call | flops 40000000000 | bytes 1024 | tf_op jit(solution)/shard_map/pallas_call | solution.py:550
  7.6 1.9 %collective-permute-start.2 = (f32[3,96,256]{2,1,0:T(8,128)S(1)}, f32[3,96,256]{2,1,0:T(8,128)S(1)}, u32[]{:S(2)}, u32[]{:S(2)}) collective-permute-start(f32[3,96,256]{2,1,0:T(8,128)S(1)} %get-tuple-element.45.after), channel_id=1, source_target_pairs={{2,4},{4,2},{6,8},{8,6},{10,12},{12,10},{3,5},{5,3},{7,9},{9,7},{1... | collective-permute-start | bytes 884744 | tf_op jit(solution)/shard_map/ppermute | solution.py:567
  10.8 0.0 copy-done
  10.8 0.0 copy-done.1
  10.8 0.0 copy-done.2
  10.8 0.0 copy-done.3
  10.8 1.2 %shard_map.123 = (f32[8,96,256]{2,1,0:T(8,128)S(1)}, f32[8,96,256]{2,1,0:T(8,128)S(1)}, f32[8,96,256]{2,1,0:T(8,128)S(1)}, f32[8,96,256]{2,1,0:T(8,128)S(1)}, f3...) custom-call(s32[1]{0:T(128)S(6)} %copy.54.off, ...), custom_call_target="tpu_custom_call" | custom-call | flops 40000000000 | bytes 1024 | tf_op jit(solution)/shard_map/pallas_call | solution.py:569
  12.0 0.0 collective-permute-done.recv
  12.0 0.1 shard_map.124
  12.2 2.5 %collective-permute-start.1 = (f32[2,96,256]{2,1,0:T(8,128)S(1)}, f32[2,96,256]{2,1,0:T(8,128)S(1)}, u32[]{:S(2)}, u32[]{:S(2)}) collective-permute-start(f32[2,96,256]{2,1,0:T(8,128)S(1)} %get-tuple-element.53.send), channel_id=1, source_target_pairs={{0,2},{2,0},{4,6},{6,4},{8,10},{10,8},{12,14},{14,12},{1,3},{3,1},... | collective-permute-start | bytes 589832 | tf_op jit(solution)/shard_map/ppermute | solution.py:595
  14.7 1.7 %shard_map.125 = (f32[8,96,256]{2,1,0:T(8,128)S(1)}, f32[8,96,256]{2,1,0:T(8,128)S(1)}, f32[8,96,256]{2,1,0:T(8,128)S(1)}, f32[8,96,256]{2,1,0:T(8,128)S(1)}, f3...) custom-call(s32[1]{0:T(128)S(6)} %copy.55.step, ...), custom_call_target="tpu_custom_call", output_to_operand_aliasing={{0}: (9, {}), {1}: (10, {}), {2}: (11, {}), {3}: (12, {}), ... | custom-call | flops 40000000000 | bytes 1024 | tf_op jit(solution)/shard_map/pallas_call | solution.py:596
  16.4 2.0 %shard_map.127 = (f32[8,96,256]{2,1,0:T(8,128)S(1)}, f32[2,8,96,256]{3,2,1,0:T(8,128)S(1)}) custom-call(f32[1,2,8,96,256]{4,3,2,1,0:T(8,128)S(1)} %copy-done, f32[1,2,8,96,256]{4,3,2,1,0:T(8,128)S(1)} %copy-done.1, f32[8,96,256]{2,1,0:T(8,128)S(1)} %get-tuple-element.46.kq, f32[8,96,256]{2,1,0:T(8,128)S(1)} %get-tuple-element.48.hb, ...), custom_call_target="tpu_custom_call" | custom-call | flops 40000000000 | bytes 1024 | tf_op jit(solution)/shard_map/pallas_call | solution.py:611
  18.4 0.0 collective-permute-done.2.recv
  18.5 0.1 shard_map.126
  18.6 1.9 %collective-permute-start.4 = (f32[2,96,256]{2,1,0:T(8,128)S(1)}, f32[2,96,256]{2,1,0:T(8,128)S(1)}, u32[]{:S(2)}, u32[]{:S(2)}) collective-permute-start(f32[2,96,256]{2,1,0:T(8,128)S(1)} %get-tuple-element.76.send), channel_id=1, source_target_pairs={{2,4},{4,2},{6,8},{8,6},{10,12},{12,10},{3,5},{5,3},{7,9},{9,7},{1... | collective-permute-start | bytes 589832 | tf_op jit(solution)/shard_map/ppermute | solution.py:624
  20.5 0.7 %shard_map.128 = (f32[8,96,256]{2,1,0:T(8,128)S(1)}, f32[2,8,96,256]{3,2,1,0:T(8,128)S(1)}) custom-call(f32[1,2,8,96,256]{4,3,2,1,0:T(8,128)S(1)} %copy-done, f32[1,2,8,96,256]{4,3,2,1,0:T(8,128)S(1)} %copy-done.1, f32[8,96,256]{2,1,0:T(8,128)S(1)} %get-tuple-element.46.kq, ...), custom_call_target="tpu_custom_call", output_to_operand_aliasing={{0}: (11, {}), {1}: (12, {})} | custom-call | flops 2000000000 | bytes 1024 | tf_op jit(solution)/shard_map/pallas_call | solution.py:611
  21.2 2.3 %collective-permute-done.1.recv2 = f32[2,96,256]{2,1,0:T(8,128)S(1)} collective-permute-done((f32[2,96,256]{2,1,0:T(8,128)S(1)}, f32[2,96,256]{2,1,0:T(8,128)S(1)}, u32[]{:S(2)}, u32[]{:S(2)}) %collective-permute-start.1) | collective-permute-done | bytes 196640 | tf_op jit(solution)/shard_map/ppermute | solution.py:595
  23.5 1.2 %shard_map.129 = (f32[1,2,8,96,256]{4,3,2,1,0:T(8,128)}, f32[8,96,256]{2,1,0:T(8,128)S(1)}, f32[2,8,64,256]{3,2,1,0:T(8,128)S(1)}, f32[2,8,64,256]{3,2,1,0:T(8,128)S(1)}) custom-call(s32[1]{0:T(128)S(6)} %copy.54.off, f32[3,96,256]{2,1,0:T(8,128)S(1)} %collective-permute-done.recv, ...), custom_call_target="tpu_custom_call", output_to_operand_aliasing={{1}: (8, {})} | custom-call | flops 2000000000 | bytes 1024 | tf_op jit(solution)/shard_map/pallas_call | solution.py:627
  24.7 0.6 %collective-permute-start.3 = (f32[2,8,64,256]{3,2,1,0:T(8,128)S(1)}, f32[2,8,64,256]{3,2,1,0:T(8,128)S(1)}, u32[]{:S(2)}, u32[]{:S(2)}) collective-permute-start(f32[2,8,64,256]{3,2,1,0:T(8,128)S(1)} %get-tuple-element.75), channel_id=1, source_target_pairs={{0,1},{1,0},{2,3},{3,2},{4,5},{5,4},{6,7},{7,6},{8,9},{9,8},{10,11... | collective-permute-start | bytes 3145736 | tf_op jit(solution)/shard_map/ppermute | solution.py:640
  25.2 1.0 %collective-permute-done.4.recv2 = f32[2,96,256]{2,1,0:T(8,128)S(1)} collective-permute-done((f32[2,96,256]{2,1,0:T(8,128)S(1)}, f32[2,96,256]{2,1,0:T(8,128)S(1)}, u32[]{:S(2)}, u32[]{:S(2)}) %collective-permute-start.4) | collective-permute-done | bytes 196640 | tf_op jit(solution)/shard_map/ppermute | solution.py:624
  26.3 0.1 shard_map.130
  26.4 2.5 %collective-permute-start.5 = (f32[2,64,256]{2,1,0:T(8,128)S(1)}, f32[2,64,256]{2,1,0:T(8,128)S(1)}, u32[]{:S(2)}, u32[]{:S(2)}) collective-permute-start(f32[2,64,256]{2,1,0:T(8,128)S(1)} %get-tuple-element.80), channel_id=1, source_target_pairs={{0,1},{1,0},{2,3},{3,2},{4,5},{5,4},{6,7},{7,6},{8,9},{9,8},{10,11... | collective-permute-start | bytes 393224 | tf_op jit(solution)/shard_map/ppermute | solution.py:649
  28.9 0.0 collective-permute-done.3.recv
  28.9 1.0 %shard_map.131 = (f32[8,64,256]{2,1,0:T(8,128)}, f32[8,64,256]{2,1,0:T(8,128)}, f32[2,64,256]{2,1,0:T(8,128)S(1)}) custom-call(f32[2,8,64,256]{3,2,1,0:T(8,128)S(1)} %get-tuple-element.74.mine, f32[2,8,64,256]{3,2,1,0:T(8,128)S(1)} %collective-permute-done.3.recv, f32[2,64,256]{2,1,0:T(8,128)S(1)} %get-tuple-element.78.mine_e), custom_call_target="tpu_custom_call" | custom-call | flops 40000000000 | bytes 1024 | tf_op jit(solution)/shard_map/pallas_call | solution.py:650
  29.9 0.0 collective-permute-done.5.recv_e
  29.9 0.7 %shard_map.132 = (f32[8,64,256]{2,1,0:T(8,128)}, f32[8,64,256]{2,1,0:T(8,128)}, f32[1,2,8,96,256]{4,3,2,1,0:T(8,128)}) custom-call(f32[2,64,256]{2,1,0:T(8,128)S(1)} %get-tuple-element.79.sums_e, f32[2,64,256]{2,1,0:T(8,128)S(1)} %collective-permute-done.5.recv_e, ...), custom_call_target="tpu_custom_call", output_to_operand_aliasing={{0}: (3, {}), {1}: (4, {}), {2}: (5, {})} | custom-call | tf_op jit(solution)/shard_map/pallas_call | solution.py:659
Async XLA Ops:
  1.3 2.5 %copy-start.4 = (f32[1,2,6400]{2,1,0:T(2,128)S(1)}, f32[1,2,6400]{2,1,0:T(2,128)}, u32[]{:S(2)}) copy-start(f32[1,2,6400]{2,1,0:T(2,128)} %res.1) | copy-start | bytes 153604
  1.3 2.5 %copy-start.5 = (s32[1,6400]{1,0:T(1,128)S(1)}, s32[1,6400]{1,0:T(1,128)}, u32[]{:S(2)}) copy-start(s32[1,6400]{1,0:T(1,128)} %rec.1) | copy-start | bytes 76804
  2.5 8.3 %copy-start = (f32[1,2,8,96,256]{4,3,2,1,0:T(8,128)S(1)}, f32[1,2,8,96,256]{4,3,2,1,0:T(8,128)}, u32[]{:S(2)}) copy-start(f32[1,2,8,96,256]{4,3,2,1,0:T(8,128)} %ckpt.19) | copy-start | bytes 4718596
  2.5 8.3 %copy-start.1 = (f32[1,2,8,96,256]{4,3,2,1,0:T(8,128)S(1)}, f32[1,2,8,96,256]{4,3,2,1,0:T(8,128)}, u32[]{:S(2)}) copy-start(f32[1,2,8,96,256]{4,3,2,1,0:T(8,128)} %adj.15) | copy-start | bytes 4718596
  2.5 8.3 %copy-start.2 = (f32[8,128,256]{2,1,0:T(8,128)S(1)}, f32[8,128,256]{2,1,0:T(8,128)}, u32[]{:S(2)}) copy-start(f32[8,128,256]{2,1,0:T(8,128)} %k_full.1) | copy-start | bytes 3145732
  2.5 8.3 %copy-start.3 = (f32[8,128,256]{2,1,0:T(8,128)S(1)}, f32[8,128,256]{2,1,0:T(8,128)}, u32[]{:S(2)}) copy-start(f32[8,128,256]{2,1,0:T(8,128)} %b_full.1) | copy-start | bytes 3145732
  2.5 9.5 %collective-permute-start = (f32[3,96,256]{2,1,0:T(8,128)S(1)}, f32[3,96,256]{2,1,0:T(8,128)S(1)}, u32[]{:S(2)}, u32[]{:S(2)}) collective-permute-start(f32[3,96,256]{2,1,0:T(8,128)S(1)} %shard_map.121.after), channel_id=1, source_target_pairs={{0,2},{2,0},{4,6},{6,4},{8,10},{10,8},{12,14},{14,12},{1,3},{3,1},... | collective-permute-start | bytes 884744 | tf_op jit(solution)/shard_map/ppermute | solution.py:548
  7.6 10.9 %collective-permute-start.2 = (f32[3,96,256]{2,1,0:T(8,128)S(1)}, f32[3,96,256]{2,1,0:T(8,128)S(1)}, u32[]{:S(2)}, u32[]{:S(2)}) collective-permute-start(f32[3,96,256]{2,1,0:T(8,128)S(1)} %get-tuple-element.45.after), channel_id=1, source_target_pairs={{2,4},{4,2},{6,8},{8,6},{10,12},{12,10},{3,5},{5,3},{7,9},{9,7},{1... | collective-permute-start | bytes 884744 | tf_op jit(solution)/shard_map/ppermute | solution.py:567
  12.2 11.3 %collective-permute-start.1 = (f32[2,96,256]{2,1,0:T(8,128)S(1)}, f32[2,96,256]{2,1,0:T(8,128)S(1)}, u32[]{:S(2)}, u32[]{:S(2)}) collective-permute-start(f32[2,96,256]{2,1,0:T(8,128)S(1)} %get-tuple-element.53.send), channel_id=1, source_target_pairs={{0,2},{2,0},{4,6},{6,4},{8,10},{10,8},{12,14},{14,12},{1,3},{3,1},... | collective-permute-start | bytes 589832 | tf_op jit(solution)/shard_map/ppermute | solution.py:595
  18.6 7.7 %collective-permute-start.4 = (f32[2,96,256]{2,1,0:T(8,128)S(1)}, f32[2,96,256]{2,1,0:T(8,128)S(1)}, u32[]{:S(2)}, u32[]{:S(2)}) collective-permute-start(f32[2,96,256]{2,1,0:T(8,128)S(1)} %get-tuple-element.76.send), channel_id=1, source_target_pairs={{2,4},{4,2},{6,8},{8,6},{10,12},{12,10},{3,5},{5,3},{7,9},{9,7},{1... | collective-permute-start | bytes 589832 | tf_op jit(solution)/shard_map/ppermute | solution.py:624
  24.7 4.2 %collective-permute-start.3 = (f32[2,8,64,256]{3,2,1,0:T(8,128)S(1)}, f32[2,8,64,256]{3,2,1,0:T(8,128)S(1)}, u32[]{:S(2)}, u32[]{:S(2)}) collective-permute-start(f32[2,8,64,256]{3,2,1,0:T(8,128)S(1)} %get-tuple-element.75), channel_id=1, source_target_pairs={{0,1},{1,0},{2,3},{3,2},{4,5},{5,4},{6,7},{7,6},{8,9},{9,8},{10,11... | collective-permute-start | bytes 3145736 | tf_op jit(solution)/shard_map/ppermute | solution.py:640
  26.4 3.5 %collective-permute-start.5 = (f32[2,64,256]{2,1,0:T(8,128)S(1)}, f32[2,64,256]{2,1,0:T(8,128)S(1)}, u32[]{:S(2)}, u32[]{:S(2)}) collective-permute-start(f32[2,64,256]{2,1,0:T(8,128)S(1)} %get-tuple-element.80), channel_id=1, source_target_pairs={{0,1},{1,0},{2,3},{3,2},{4,5},{5,4},{6,7},{7,6},{8,9},{9,8},{10,11... | collective-permute-start | bytes 393224 | tf_op jit(solution)/shard_map/ppermute | solution.py:649

commit v4 on v3

--- a/solution.py
+++ b/solution.py
@@ -54,9 +54,15 @@
     return ends[LEAD], ends[1 - LEAD]
 
 
-def window(block, off, ny):
-    rows = block.shape[0]
-    return pltpu.roll(block, lax.rem(rows - off, rows), 0)[:ny]
+def window(ref, lead, off, ny):
+    rows, nz = ref.shape[-2:]
+    base = jnp.minimum(off - lax.rem(off, TILE), rows - ny - TILE)
+    skip = off - base
+    block = ref[(*lead, pl.ds(pl.multiple_of(base, TILE), ny + TILE), slice(None))]
+    tiles = block.reshape(ny // TILE + 1, TILE, nz)
+    tiles = pltpu.roll(tiles, lax.rem(TILE - skip, TILE), 1)
+    row = lax.broadcasted_iota(jnp.int32, (ny // TILE, TILE, nz), 1)
+    return jnp.where(row < TILE - skip, tiles[:-1], tiles[1:]).reshape(ny, nz)
 
 
 def placed(plane, off, rows):
@@ -75,8 +81,8 @@
 
 def edge_fill(off, send, q_e, k_e, b_e):
     ny = q_e.shape[0]
-    send[1] = window(k_e[...], off, ny) * q_e[...]
-    send[2] = window(b_e[...], off, ny)
+    send[1] = window(k_e, (), off, ny) * q_e[...]
+    send[2] = window(b_e, (), off, ny)
 
 
 def first_send(off, ckpt, adj, kappa, buoy, send, q_e, k_e, b_e, sem):
@@ -313,10 +319,10 @@
     p_old, p, q_late, q = ckpt.at[0, 0], ckpt.at[0, 1], adj.at[0, 0], adj.at[0, 1]
 
     def windows(x, carry):
-        k = window(k_full[x], off[0], ny)
+        k = window(k_full, (x,), off[0], ny)
         kw[x] = k
         kq[x] = k * q[x]
-        hb[x] = 0.5 * window(b_full[x], off[0], ny)
+        hb[x] = 0.5 * window(b_full, (x,), off[0], ny)
         return carry
 
     lax.fori_loop(0, width, windows, 0)

time: 30.9 us -> 30.6 us (level)
  starting transfers between devices: 10.7 us -> 11.2 us
  waiting for transfers between devices: 3.32 us -> 2.91 us
    ppermute x1, waiting for transfers between devices: 1.03 us -> 0.4 us  [shards(): recv2_2 = lax.ppermute(send2_2, 'dom', swaps[1])]
    ppermute x1, starting transfers between devices: 2.5 us -> 2.91 us  [shards(): recv_e = lax.ppermute(other_e, 'shot', swap)]
  transfers between devices with their start and end apart: 6 -> 6, of which waited for: 2 -> 2; matrix products, arithmetic and copies ran while one was open for 0% -> 0% of each run, Pallas kernels for 39% -> 38%
where the time goes in v4:
time: 30.6 us; the launch traced here: 30.4 us
  Pallas kernels  13.5 us (44%)
  starting transfers between devices  11.2 us (37%)
  waiting for transfers between devices  2.91 us (10%)
  between operations  2.77 us (9%)
    pallas_call x1, Pallas kernels, shards(): pl.pallas_call(receivers, in_specs=[SM, VM, VM] + [ANY] * 4 + [VM], out_s...  3.72 us
    ppermute x1, starting transfers between devices, shards(): recv_e = lax.ppermute(other_e, 'shot', swap)  2.91 us
    pallas_call x2, Pallas kernels, second_step(): pl.pallas_call(functools.partial(step_two, part), in_specs=[VM] * (11 + l...  2.74 us
    ppermute x1, starting transfers between devices, shards(): recv2_1 = lax.ppermute(send2_1, 'dom', swaps[0])  2.53 us
    ppermute x1, waiting for transfers between devices, shards(): recv2_1 = lax.ppermute(send2_1, 'dom', swaps[0])  2.5 us
    ppermute x1, starting transfers between devices, shards(): recv2_2 = lax.ppermute(send2_2, 'dom', swaps[1])  1.96 us
    ppermute x1, starting transfers between devices, shards(): recv_2 = lax.ppermute(send_2, 'dom', swaps[1])  1.92 us
    pallas_call x1, Pallas kernels, shards(): pl.pallas_call(step_one_middle, in_specs=[SM] * 2 + [ANY] + [VM] * 12, ou...  1.69 us
  transfers between devices with their start and end apart: 6, of which 2 were waited for; matrix products, arithmetic and copies ran while one was open for 0% of the time, Pallas kernels for 38%

profile of v4, /device:TPU:9, one launch (start us, length us, event | category | flops | bytes accessed | tf_op | source)
XLA Modules:
  0.0 30.4 jit_solution(17200268039222186077)
XLA Ops:
  1.3 0.0 copy-start.4
  1.3 0.0 copy-start.5
  1.3 1.1 %shard_map.121.after = f32[3,96,256]{2,1,0:T(8,128)S(1)} custom-call(s32[1]{0:T(128)S(6)} %copy.54.off, f32[1,2,8,96,256]{4,3,2,1,0:T(8,128)} %ckpt.19, f32[1,2,8,96,256]{4,3,2,1,0:T(8,128)} %adj.15, f32[8,128,256]{2,1,0:T(8,128)} %k_full.1, f32[8,128,256]{2,1,0:T(8,128)} %b_full.1), custom_call_target="tpu_custom_call" | custom-call | tf_op jit(solution)/shard_map/pallas_call | solution.py:546
  2.5 0.0 copy-start
  2.5 0.0 copy-start.1
  2.5 0.0 copy-start.2
  2.5 0.0 copy-start.3
  2.5 1.3 %collective-permute-start = (f32[3,96,256]{2,1,0:T(8,128)S(1)}, f32[3,96,256]{2,1,0:T(8,128)S(1)}, u32[]{:S(2)}, u32[]{:S(2)}) collective-permute-start(f32[3,96,256]{2,1,0:T(8,128)S(1)} %shard_map.121.after), channel_id=1, source_target_pairs={{0,2},{2,0},{4,6},{6,4},{8,10},{10,8},{12,14},{14,12},{1,3},{3,1},... | collective-permute-start | bytes 884744 | tf_op jit(solution)/shard_map/ppermute | solution.py:554
  3.8 0.0 copy-done.4
  3.8 0.0 copy-done.5
  3.8 3.7 %shard_map.122 = (f32[768,512]{1,0:T(8,128)S(1)}, f32[3,96,256]{2,1,0:T(8,128)S(1)}) custom-call(s32[1]{0:T(128)S(6)} %copy.54.off, s32[1,6400]{1,0:T(1,128)S(1)} %copy-done.5, f32[1,2,6400]{2,1,0:T(2,128)S(1)} %copy-done.4, f32[1,2,8,96,256]{4,3,2,1,0:T(8,128)} %ckpt.19, f32[1,2,8,96,256]{4,3,2,1,0:T(8,128)} %adj.15, f32[8,128,256]{2,1,0:T(8,128)} %k_full.1, ...), custom_call_target="tpu_custom_call" | custom-call | flops 40000000000 | bytes 1024 | tf_op jit(solution)/shard_map/pallas_call | solution.py:556
  7.5 1.9 %collective-permute-start.2 = (f32[3,96,256]{2,1,0:T(8,128)S(1)}, f32[3,96,256]{2,1,0:T(8,128)S(1)}, u32[]{:S(2)}, u32[]{:S(2)}) collective-permute-start(f32[3,96,256]{2,1,0:T(8,128)S(1)} %get-tuple-element.45.after), channel_id=1, source_target_pairs={{2,4},{4,2},{6,8},{8,6},{10,12},{12,10},{3,5},{5,3},{7,9},{9,7},{1... | collective-permute-start | bytes 884744 | tf_op jit(solution)/shard_map/ppermute | solution.py:573
  10.7 0.0 copy-done
  10.7 0.0 copy-done.1
  10.8 0.0 copy-done.2
  10.8 0.0 copy-done.3
  10.8 0.9 %shard_map.123 = (f32[8,96,256]{2,1,0:T(8,128)S(1)}, f32[8,96,256]{2,1,0:T(8,128)S(1)}, f32[8,96,256]{2,1,0:T(8,128)S(1)}, f32[8,96,256]{2,1,0:T(8,128)S(1)}, f3...) custom-call(s32[1]{0:T(128)S(6)} %copy.54.off, ...), custom_call_target="tpu_custom_call" | custom-call | flops 40000000000 | bytes 1024 | tf_op jit(solution)/shard_map/pallas_call | solution.py:575
  11.7 0.0 collective-permute-done.recv
  11.7 0.1 shard_map.124
  11.8 2.5 %collective-permute-start.1 = (f32[2,96,256]{2,1,0:T(8,128)S(1)}, f32[2,96,256]{2,1,0:T(8,128)S(1)}, u32[]{:S(2)}, u32[]{:S(2)}) collective-permute-start(f32[2,96,256]{2,1,0:T(8,128)S(1)} %get-tuple-element.53.send), channel_id=1, source_target_pairs={{0,2},{2,0},{4,6},{6,4},{8,10},{10,8},{12,14},{14,12},{1,3},{3,1},... | collective-permute-start | bytes 589832 | tf_op jit(solution)/shard_map/ppermute | solution.py:601
  14.4 1.7 %shard_map.125 = (f32[8,96,256]{2,1,0:T(8,128)S(1)}, f32[8,96,256]{2,1,0:T(8,128)S(1)}, f32[8,96,256]{2,1,0:T(8,128)S(1)}, f32[8,96,256]{2,1,0:T(8,128)S(1)}, f3...) custom-call(s32[1]{0:T(128)S(6)} %copy.55.step, ...), custom_call_target="tpu_custom_call", output_to_operand_aliasing={{0}: (9, {}), {1}: (10, {}), {2}: (11, {}), {3}: (12, {}), ... | custom-call | flops 40000000000 | bytes 1024 | tf_op jit(solution)/shard_map/pallas_call | solution.py:602
  16.1 2.0 %shard_map.127 = (f32[8,96,256]{2,1,0:T(8,128)S(1)}, f32[2,8,96,256]{3,2,1,0:T(8,128)S(1)}) custom-call(f32[1,2,8,96,256]{4,3,2,1,0:T(8,128)S(1)} %copy-done, f32[1,2,8,96,256]{4,3,2,1,0:T(8,128)S(1)} %copy-done.1, f32[8,96,256]{2,1,0:T(8,128)S(1)} %get-tuple-element.46.kq, f32[8,96,256]{2,1,0:T(8,128)S(1)} %get-tuple-element.48.hb, ...), custom_call_target="tpu_custom_call" | custom-call | flops 40000000000 | bytes 1024 | tf_op jit(solution)/shard_map/pallas_call | solution.py:617
  18.1 0.0 collective-permute-done.2.recv
  18.1 0.1 shard_map.126
  18.3 2.0 %collective-permute-start.4 = (f32[2,96,256]{2,1,0:T(8,128)S(1)}, f32[2,96,256]{2,1,0:T(8,128)S(1)}, u32[]{:S(2)}, u32[]{:S(2)}) collective-permute-start(f32[2,96,256]{2,1,0:T(8,128)S(1)} %get-tuple-element.76.send), channel_id=1, source_target_pairs={{2,4},{4,2},{6,8},{8,6},{10,12},{12,10},{3,5},{5,3},{7,9},{9,7},{1... | collective-permute-start | bytes 589832 | tf_op jit(solution)/shard_map/ppermute | solution.py:630
  20.2 0.7 %shard_map.128 = (f32[8,96,256]{2,1,0:T(8,128)S(1)}, f32[2,8,96,256]{3,2,1,0:T(8,128)S(1)}) custom-call(f32[1,2,8,96,256]{4,3,2,1,0:T(8,128)S(1)} %copy-done, f32[1,2,8,96,256]{4,3,2,1,0:T(8,128)S(1)} %copy-done.1, f32[8,96,256]{2,1,0:T(8,128)S(1)} %get-tuple-element.46.kq, ...), custom_call_target="tpu_custom_call", output_to_operand_aliasing={{0}: (11, {}), {1}: (12, {})} | custom-call | flops 2000000000 | bytes 1024 | tf_op jit(solution)/shard_map/pallas_call | solution.py:617
  20.9 2.5 %collective-permute-done.1.recv2 = f32[2,96,256]{2,1,0:T(8,128)S(1)} collective-permute-done((f32[2,96,256]{2,1,0:T(8,128)S(1)}, f32[2,96,256]{2,1,0:T(8,128)S(1)}, u32[]{:S(2)}, u32[]{:S(2)}) %collective-permute-start.1) | collective-permute-done | bytes 196640 | tf_op jit(solution)/shard_map/ppermute | solution.py:601
  23.4 1.2 %shard_map.129 = (f32[1,2,8,96,256]{4,3,2,1,0:T(8,128)}, f32[8,96,256]{2,1,0:T(8,128)S(1)}, f32[2,8,64,256]{3,2,1,0:T(8,128)S(1)}, f32[2,8,64,256]{3,2,1,0:T(8,128)S(1)}) custom-call(s32[1]{0:T(128)S(6)} %copy.54.off, f32[3,96,256]{2,1,0:T(8,128)S(1)} %collective-permute-done.recv, ...), custom_call_target="tpu_custom_call", output_to_operand_aliasing={{1}: (8, {})} | custom-call | flops 2000000000 | bytes 1024 | tf_op jit(solution)/shard_map/pallas_call | solution.py:633
  24.6 0.6 %collective-permute-start.3 = (f32[2,8,64,256]{3,2,1,0:T(8,128)S(1)}, f32[2,8,64,256]{3,2,1,0:T(8,128)S(1)}, u32[]{:S(2)}, u32[]{:S(2)}) collective-permute-start(f32[2,8,64,256]{3,2,1,0:T(8,128)S(1)} %get-tuple-element.75), channel_id=1, source_target_pairs={{0,1},{1,0},{2,3},{3,2},{4,5},{5,4},{6,7},{7,6},{8,9},{9,8},{10,11... | collective-permute-start | bytes 3145736 | tf_op jit(solution)/shard_map/ppermute | solution.py:646
  25.2 0.4 %collective-permute-done.4.recv2 = f32[2,96,256]{2,1,0:T(8,128)S(1)} collective-permute-done((f32[2,96,256]{2,1,0:T(8,128)S(1)}, f32[2,96,256]{2,1,0:T(8,128)S(1)}, u32[]{:S(2)}, u32[]{:S(2)}) %collective-permute-start.4) | collective-permute-done | bytes 196640 | tf_op jit(solution)/shard_map/ppermute | solution.py:630
  25.6 0.1 shard_map.130
  25.7 2.9 %collective-permute-start.5 = (f32[2,64,256]{2,1,0:T(8,128)S(1)}, f32[2,64,256]{2,1,0:T(8,128)S(1)}, u32[]{:S(2)}, u32[]{:S(2)}) collective-permute-start(f32[2,64,256]{2,1,0:T(8,128)S(1)} %get-tuple-element.80), channel_id=1, source_target_pairs={{0,1},{1,0},{2,3},{3,2},{4,5},{5,4},{6,7},{7,6},{8,9},{9,8},{10,11... | collective-permute-start | bytes 393224 | tf_op jit(solution)/shard_map/ppermute | solution.py:655
  28.6 0.0 collective-permute-done.3.recv
  28.6 1.0 %shard_map.131 = (f32[8,64,256]{2,1,0:T(8,128)}, f32[8,64,256]{2,1,0:T(8,128)}, f32[2,64,256]{2,1,0:T(8,128)S(1)}) custom-call(f32[2,8,64,256]{3,2,1,0:T(8,128)S(1)} %get-tuple-element.74.mine, f32[2,8,64,256]{3,2,1,0:T(8,128)S(1)} %collective-permute-done.3.recv, f32[2,64,256]{2,1,0:T(8,128)S(1)} %get-tuple-element.78.mine_e), custom_call_target="tpu_custom_call" | custom-call | flops 40000000000 | bytes 1024 | tf_op jit(solution)/shard_map/pallas_call | solution.py:656
  29.7 0.0 collective-permute-done.5.recv_e
  29.7 0.7 %shard_map.132 = (f32[8,64,256]{2,1,0:T(8,128)}, f32[8,64,256]{2,1,0:T(8,128)}, f32[1,2,8,96,256]{4,3,2,1,0:T(8,128)}) custom-call(f32[2,64,256]{2,1,0:T(8,128)S(1)} %get-tuple-element.79.sums_e, f32[2,64,256]{2,1,0:T(8,128)S(1)} %collective-permute-done.5.recv_e, ...), custom_call_target="tpu_custom_call", output_to_operand_aliasing={{0}: (3, {}), {1}: (4, {}), {2}: (5, {})} | custom-call | tf_op jit(solution)/shard_map/pallas_call | solution.py:665
Async XLA Ops:
  1.3 2.5 %copy-start.4 = (f32[1,2,6400]{2,1,0:T(2,128)S(1)}, f32[1,2,6400]{2,1,0:T(2,128)}, u32[]{:S(2)}) copy-start(f32[1,2,6400]{2,1,0:T(2,128)} %res.1) | copy-start | bytes 153604
  1.3 2.5 %copy-start.5 = (s32[1,6400]{1,0:T(1,128)S(1)}, s32[1,6400]{1,0:T(1,128)}, u32[]{:S(2)}) copy-start(s32[1,6400]{1,0:T(1,128)} %rec.1) | copy-start | bytes 76804
  2.5 8.3 %copy-start = (f32[1,2,8,96,256]{4,3,2,1,0:T(8,128)S(1)}, f32[1,2,8,96,256]{4,3,2,1,0:T(8,128)}, u32[]{:S(2)}) copy-start(f32[1,2,8,96,256]{4,3,2,1,0:T(8,128)} %ckpt.19) | copy-start | bytes 4718596
  2.5 8.3 %copy-start.1 = (f32[1,2,8,96,256]{4,3,2,1,0:T(8,128)S(1)}, f32[1,2,8,96,256]{4,3,2,1,0:T(8,128)}, u32[]{:S(2)}) copy-start(f32[1,2,8,96,256]{4,3,2,1,0:T(8,128)} %adj.15) | copy-start | bytes 4718596
  2.5 8.3 %copy-start.2 = (f32[8,128,256]{2,1,0:T(8,128)S(1)}, f32[8,128,256]{2,1,0:T(8,128)}, u32[]{:S(2)}) copy-start(f32[8,128,256]{2,1,0:T(8,128)} %k_full.1) | copy-start | bytes 3145732
  2.5 8.3 %copy-start.3 = (f32[8,128,256]{2,1,0:T(8,128)S(1)}, f32[8,128,256]{2,1,0:T(8,128)}, u32[]{:S(2)}) copy-start(f32[8,128,256]{2,1,0:T(8,128)} %b_full.1) | copy-start | bytes 3145732
  2.5 9.2 %collective-permute-start = (f32[3,96,256]{2,1,0:T(8,128)S(1)}, f32[3,96,256]{2,1,0:T(8,128)S(1)}, u32[]{:S(2)}, u32[]{:S(2)}) collective-permute-start(f32[3,96,256]{2,1,0:T(8,128)S(1)} %shard_map.121.after), channel_id=1, source_target_pairs={{0,2},{2,0},{4,6},{6,4},{8,10},{10,8},{12,14},{14,12},{1,3},{3,1},... | collective-permute-start | bytes 884744 | tf_op jit(solution)/shard_map/ppermute | solution.py:554
  7.5 10.6 %collective-permute-start.2 = (f32[3,96,256]{2,1,0:T(8,128)S(1)}, f32[3,96,256]{2,1,0:T(8,128)S(1)}, u32[]{:S(2)}, u32[]{:S(2)}) collective-permute-start(f32[3,96,256]{2,1,0:T(8,128)S(1)} %get-tuple-element.45.after), channel_id=1, source_target_pairs={{2,4},{4,2},{6,8},{8,6},{10,12},{12,10},{3,5},{5,3},{7,9},{9,7},{1... | collective-permute-start | bytes 884744 | tf_op jit(solution)/shard_map/ppermute | solution.py:573
  11.8 11.6 %collective-permute-start.1 = (f32[2,96,256]{2,1,0:T(8,128)S(1)}, f32[2,96,256]{2,1,0:T(8,128)S(1)}, u32[]{:S(2)}, u32[]{:S(2)}) collective-permute-start(f32[2,96,256]{2,1,0:T(8,128)S(1)} %get-tuple-element.53.send), channel_id=1, source_target_pairs={{0,2},{2,0},{4,6},{6,4},{8,10},{10,8},{12,14},{14,12},{1,3},{3,1},... | collective-permute-start | bytes 589832 | tf_op jit(solution)/shard_map/ppermute | solution.py:601
  18.3 7.3 %collective-permute-start.4 = (f32[2,96,256]{2,1,0:T(8,128)S(1)}, f32[2,96,256]{2,1,0:T(8,128)S(1)}, u32[]{:S(2)}, u32[]{:S(2)}) collective-permute-start(f32[2,96,256]{2,1,0:T(8,128)S(1)} %get-tuple-element.76.send), channel_id=1, source_target_pairs={{2,4},{4,2},{6,8},{8,6},{10,12},{12,10},{3,5},{5,3},{7,9},{9,7},{1... | collective-permute-start | bytes 589832 | tf_op jit(solution)/shard_map/ppermute | solution.py:630
  24.6 4.0 %collective-permute-start.3 = (f32[2,8,64,256]{3,2,1,0:T(8,128)S(1)}, f32[2,8,64,256]{3,2,1,0:T(8,128)S(1)}, u32[]{:S(2)}, u32[]{:S(2)}) collective-permute-start(f32[2,8,64,256]{3,2,1,0:T(8,128)S(1)} %get-tuple-element.75), channel_id=1, source_target_pairs={{0,1},{1,0},{2,3},{3,2},{4,5},{5,4},{6,7},{7,6},{8,9},{9,8},{10,11... | collective-permute-start | bytes 3145736 | tf_op jit(solution)/shard_map/ppermute | solution.py:646
  25.7 4.0 %collective-permute-start.5 = (f32[2,64,256]{2,1,0:T(8,128)S(1)}, f32[2,64,256]{2,1,0:T(8,128)S(1)}, u32[]{:S(2)}, u32[]{:S(2)}) collective-permute-start(f32[2,64,256]{2,1,0:T(8,128)S(1)} %get-tuple-element.80), channel_id=1, source_target_pairs={{0,1},{1,0},{2,3},{3,2},{4,5},{5,4},{6,7},{7,6},{8,9},{9,8},{10,11... | collective-permute-start | bytes 393224 | tf_op jit(solution)/shard_map/ppermute | solution.py:655

commit v5 on v4

--- a/solution.py
+++ b/solution.py
@@ -95,11 +95,18 @@
     edge_fill(off[0], send, q_e, k_e, b_e)
 
 
+def receiver_sums(left, right_hi, right_lo, step, nz):
+    cols = pl.ds(step * nz, nz)
+    return jnp.dot(left[...], right_hi[:, cols], preferred_element_type=F32) + jnp.dot(
+        left[...], right_lo[:, cols], preferred_element_type=F32
+    )
+
+
 def receivers(
-    off, rec, res, ckpt, adj, kappa, buoy, after, total, send,
-    q_e, k_e, b_e, cell_s, rank_s, row_a_s, row_b_s, z_s, val_s, left, right_hi, right_lo, sem,
+    off, rec, res, ckpt, adj, kappa, buoy, after, total_1, total_2, send, left, right_hi, right_lo, later,
+    q_e, k_e, b_e, cell_s, rank_s, row_a_s, row_b_s, z_s, val_s, sem,
 ):
-    nz = total.shape[1] // 2
+    nz = total_1.shape[1]
     edge = edges(ckpt.shape[2])[1]
     copies = edge_copies(edge, ckpt, adj, kappa, buoy, send, q_e, k_e, b_e, sem)
     for copy in copies:
@@ -110,7 +117,7 @@
         cell_s[r : r + 1, :] = rec[:, at]
         for step in range(2):
             val_s[2 * step, r : r + 1, :] = res[0, step : step + 1, at]
-    cells = total.shape[0] * nz
+    cells = total_1.shape[0] * nz
     shift = nz.bit_length() - 1
     local = cell_s[...] - lax.axis_index("dom") * cells
     inside = (local >= 0) & (local < cells)
@@ -138,6 +145,8 @@
     rank = jnp.where(inside, in_row + row_start, -1.0)
     rank_s[...] = rank
     passes = lax.shift_right_logical(jnp.max(rank).astype(jnp.int32), jnp.int32(7)) + 1
+    leave = (lax.rem(lax.axis_index("dom"), 2) == 0) & (passes <= 1)
+    later[0] = jnp.where(leave, 1, 0)
     groups = rows // GROUP_ROWS
     slot = lax.broadcasted_iota(jnp.int32, (LANES, lanes), 0).astype(F32)
     sub8 = lax.broadcasted_iota(jnp.int32, (TILE, lanes), 0)
@@ -172,13 +181,16 @@
                 low = by_slot[:, 4 + 2 * step : 5 + 2 * step]
                 right_hi[here, cols] = jnp.where(same, high, 0.0).astype(BF16)
                 right_lo[here, cols] = jnp.where(same, low, 0.0).astype(BF16)
-        out = jnp.dot(left[...], right_hi[...], preferred_element_type=F32) + jnp.dot(
-            left[...], right_lo[...], preferred_element_type=F32
-        )
         if first:
-            total[...] = out
+            total_1[...] = receiver_sums(left, right_hi, right_lo, 0, nz)
+
+            @pl.when(jnp.logical_not(leave))
+            def _():
+                total_2[...] = receiver_sums(left, right_hi, right_lo, 1, nz)
+
         else:
-            total[...] += out
+            total_1[...] += receiver_sums(left, right_hi, right_lo, 0, nz)
+            total_2[...] += receiver_sums(left, right_hi, right_lo, 1, nz)
 
     one_pass(0.0, True)
 
@@ -309,14 +321,18 @@
 
 
 def step_one_ends(
-    off, step, src, wav_in, ckpt, adj, k_full, b_full, total, after,
-    kq, kw, hb, fy, fz, lap, pn, qm, kqm,
+    off, step, src, later, wav_in, ckpt, adj, k_full, b_full, total, after, left, right_hi, right_lo, total_2_in,
+    kq, kw, hb, fy, fz, lap, pn, qm, kqm, total_2,
     gx_s, wav, sem,
 ):
     width, ny, nz = kq.shape
     copy = pltpu.make_async_copy(wav_in, wav, sem.at[0])
     copy.start()
     p_old, p, q_late, q = ckpt.at[0, 0], ckpt.at[0, 1], adj.at[0, 0], adj.at[0, 1]
+
+    @pl.when(later[0] == 1)
+    def _():
+        total_2[...] = receiver_sums(left, right_hi, right_lo, 1, nz)
 
     def windows(x, carry):
         k = window(k_full, (x,), off[0], ny)
@@ -418,7 +434,7 @@
             dqm = ch.diffs(kqm, x, xn, y)
             lap_q, tail_q = ch.lap(dqm, faces, h, gx_s, 1, y, tail_q)
             add = [
-                total[pl.ds(pl.multiple_of(x * ny + y, TILE), CHUNK), pl.ds(nz + n * LANES, LANES)]
+                total[pl.ds(pl.multiple_of(x * ny + y, TILE), CHUNK), pl.ds(n * LANES, LANES)]
                 for n in range(ch.blocks)
             ]
             ch.store(last, (x,), y, [2.0 * a - b + c + e for a, b, c, e in zip(mid, now, lap_q, add)])
@@ -553,18 +569,17 @@
     )(offsets, *inputs)
     recv_1 = lax.ppermute(send_1, "dom", swaps[0])
 
-    total, send_2 = pl.pallas_call(
+    sums_shape = vmem(width * ny, nz)
+    hot_shapes = [pltpu.VMEM(shape, BF16) for shape in ((width * ny, slots), (slots, 2 * nz), (slots, 2 * nz))]
+    total_1, total_2, send_2, *hot, later = pl.pallas_call(
         receivers,
         in_specs=[SM, VM, VM] + [ANY] * 4 + [VM],
-        out_specs=[VM, VM],
-        out_shape=[vmem(width * ny, 2 * nz), vmem(3, *layer)],
+        out_specs=[VM] * 6 + [SM],
+        out_shape=[sums_shape, sums_shape, vmem(3, *layer)] + hot_shapes + [pltpu.SMEM((1,), jnp.int32)],
         scratch_shapes=edge_scratch + [
             pltpu.VMEM((rrows, LANES), jnp.int32),
             vmem(rrows, LANES), vmem(rrows, LANES), vmem(rrows, LANES), vmem(rrows, LANES),
             vmem(4, rrows, LANES),
-            pltpu.VMEM((width * ny, slots), BF16),
-            pltpu.VMEM((slots, 2 * nz), BF16),
-            pltpu.VMEM((slots, 2 * nz), BF16),
             dma((4,)),
         ],
         compiler_params=params(),
@@ -572,17 +587,18 @@
     )(offsets, near(rec_cell), near(residuals), *inputs, near(send_1))
     recv_2 = lax.ppermute(send_2, "dom", swaps[1])
 
-    kq, kw, hb, *state = pl.pallas_call(
+    kq, kw, hb, *state, total_2 = pl.pallas_call(
         step_one_ends,
-        in_specs=[SM] * 3 + [ANY] + [VM] * 6,
-        out_specs=[VM] * 9,
-        out_shape=[vmem(*field)] * 9,
+        in_specs=[SM] * 4 + [ANY] + [VM] * 10,
+        out_specs=[VM] * 10,
+        out_shape=[vmem(*field)] * 9 + [sums_shape],
         scratch_shapes=[vmem(2, *layer), pltpu.SMEM(wavelet.shape, F32), dma((1,))],
         compiler_params=params(),
+        input_output_aliases={14: 9},
         cost_estimate=cost(ENDS_COST),
     )(
-        offsets, ckpt_step, src_cell, far(wavelet),
-        *[near(v) for v in (checkpoint, adjoint, kappa, buoyancy, total, send_2)],
+        offsets, ckpt_step, src_cell, later, far(wavelet),
+        *[near(v) for v in (checkpoint, adjoint, kappa, buoyancy, total_1, send_2, *hot, total_2)],
     )
 
     def first_edge(which, recv, state):
@@ -597,8 +613,6 @@
         )(*[near(v) for v in (recv, checkpoint, kq, kw, hb, *state[2:])])
         return send, list(state[:2]) + list(new)
 
-    send2_1, state = first_edge(0, recv_1, state)
-    recv2_1 = lax.ppermute(send2_1, "dom", swaps[0])
     state = pl.pallas_call(
         step_one_middle,
         in_specs=[SM] * 2 + [ANY] + [VM] * 12,
@@ -610,8 +624,11 @@
         cost_estimate=cost(MIDDLE_COST),
     )(
         ckpt_step, src_cell, far(wavelet),
-        *[near(v) for v in (checkpoint, adjoint, kq, kw, hb, total, *state)],
+        *[near(v) for v in (checkpoint, adjoint, kq, kw, hb, total_1, *state)],
     )
+    send2_1, state = first_edge(0, recv_1, state)
+    recv2_1 = lax.ppermute(send2_1, "dom", swaps[0])
+
     def second_step(part, state, *partial):
         out_shape = [vmem(*field), vmem(2, *field)]
         return pl.pallas_call(
@@ -623,7 +640,7 @@
             input_output_aliases={11 + n: n for n in range(len(partial))},
             compiler_params=params(),
             cost_estimate=cost(TWO_COST[part]),
-        )(*[near(v) for v in (checkpoint, adjoint, kq, hb, *state, total, *partial)])
+        )(*[near(v) for v in (checkpoint, adjoint, kq, hb, *state, total_2, *partial)])
 
     partial = second_step(0, state)
     send2_2, state = first_edge(1, recv_2, state)

time: 30.6 us -> 29.9 us (0.977)
  waiting for transfers between devices: 2.91 us -> 1.21 us
  starting transfers between devices: 11.2 us -> 11.7 us
    ppermute x1, starting transfers between devices: 2.53 us -> 0.3 us  [shards(): recv2_1 = lax.ppermute(send2_1, 'dom', swaps[0])]
    ppermute x1, waiting for transfers between devices: 2.5 us -> 0.82 us  [shards(): recv2_1 = lax.ppermute(send2_1, 'dom', swaps[0])]
    pallas_call x1, Pallas kernels: 0.92 us -> 2.1 us  [shards(): pl.pallas_call(step_one_ends, in_specs=[SM] * 4 + [ANY] + [VM] * 10, out_...]
    ppermute x1, starting transfers between devices: 1.96 us -> 3.03 us  [shards(): recv2_2 = lax.ppermute(send2_2, 'dom', swaps[1])]
    ppermute x1, starting transfers between devices: 1.92 us -> 2.99 us  [shards(): recv_2 = lax.ppermute(send_2, 'dom', swaps[1])]
    pallas_call x1, Pallas kernels: 3.72 us -> 2.78 us  [shards(): pl.pallas_call(receivers, in_specs=[SM, VM, VM] + [ANY] * 4 + [VM], out_s...]
    ppermute x1, starting transfers between devices: 0.56 us -> 1.19 us  [shards(): recv_g = lax.ppermute(other, 'shot', swap)]
  transfers between devices with their start and end apart: 6 -> 6, of which waited for: 2 -> 2; matrix products, arithmetic and copies ran while one was open for 0% -> 0% of each run, Pallas kernels for 38% -> 40%
where the time goes in v5:
time: 29.9 us; the launch traced here: 29.4 us
  Pallas kernels  13.8 us (46%)
  starting transfers between devices  11.7 us (39%)
  between operations  2.77 us (9%)
  waiting for transfers between devices  1.21 us (4%)
    ppermute x1, starting transfers between devices, shards(): recv2_2 = lax.ppermute(send2_2, 'dom', swaps[1])  3.03 us
    ppermute x1, starting transfers between devices, shards(): recv_2 = lax.ppermute(send_2, 'dom', swaps[1])  2.99 us
    ppermute x1, starting transfers between devices, shards(): recv_e = lax.ppermute(other_e, 'shot', swap)  2.89 us
    pallas_call x1, Pallas kernels, shards(): pl.pallas_call(receivers, in_specs=[SM, VM, VM] + [ANY] * 4 + [VM], out_s...  2.78 us
    pallas_call x2, Pallas kernels, second_step(): pl.pallas_call(functools.partial(step_two, part), in_specs=[VM] * (11 + l...  2.72 us
    pallas_call x1, Pallas kernels, shards(): pl.pallas_call(step_one_ends, in_specs=[SM] * 4 + [ANY] + [VM] * 10, out_...  2.1 us
    pallas_call x1, Pallas kernels, shards(): pl.pallas_call(step_one_middle, in_specs=[SM] * 2 + [ANY] + [VM] * 12, ou...  1.7 us
    ppermute x1, starting transfers between devices, shards(): recv_1 = lax.ppermute(send_1, 'dom', swaps[0])  1.28 us
  transfers between devices with their start and end apart: 6, of which 2 were waited for; matrix products, arithmetic and copies ran while one was open for 0% of the time, Pallas kernels for 40%

profile of v5, /device:TPU:9, one launch (start us, length us, event | category | flops | bytes accessed | tf_op | source)
XLA Modules:
  0.0 29.4 jit_solution(13216527830090238534)
XLA Ops:
  1.3 0.0 copy-start.4
  1.3 0.0 copy-start.5
  1.3 1.1 %shard_map.121.after = f32[3,96,256]{2,1,0:T(8,128)S(1)} custom-call(s32[1]{0:T(128)S(6)} %copy.56.off, f32[1,2,8,96,256]{4,3,2,1,0:T(8,128)} %ckpt.19, f32[1,2,8,96,256]{4,3,2,1,0:T(8,128)} %adj.15, f32[8,128,256]{2,1,0:T(8,128)} %k_full.1, f32[8,128,256]{2,1,0:T(8,128)} %b_full.1), custom_call_target="tpu_custom_call" | custom-call | tf_op jit(solution)/shard_map/pallas_call | solution.py:562
  2.5 0.0 copy-start
  2.5 0.0 copy-start.1
  2.5 0.0 copy-start.2
  2.5 0.0 copy-start.3
  2.5 1.3 %collective-permute-start = (f32[3,96,256]{2,1,0:T(8,128)S(1)}, f32[3,96,256]{2,1,0:T(8,128)S(1)}, u32[]{:S(2)}, u32[]{:S(2)}) collective-permute-start(f32[3,96,256]{2,1,0:T(8,128)S(1)} %shard_map.121.after), channel_id=1, source_target_pairs={{0,2},{2,0},{4,6},{6,4},{8,10},{10,8},{12,14},{14,12},{1,3},{3,1},... | collective-permute-start | bytes 884744 | tf_op jit(solution)/shard_map/ppermute | solution.py:570
  3.8 0.0 copy-done.4
  3.8 0.0 copy-done.5
  3.8 2.8 %shard_map.122 = (f32[768,256]{1,0:T(8,128)S(1)}, f32[768,256]{1,0:T(8,128)S(1)}, f32[3,96,256]{2,1,0:T(8,128)S(1)}, bf16[768,1280]{1,0:T(8,128)(2,1)S(1)}, bf16...) custom-call(s32[1]{0:T(128)S(6)} %copy.56.off, s32[1,6400]{1,0:T(1,128)S(1)} %copy-done.5, ...), custom_call_target="tpu_custom_call" | custom-call | flops 40000000000 | bytes 1024 | tf_op jit(solution)/shard_map/pallas_call | solution.py:574
  6.6 3.0 %collective-permute-start.2 = (f32[3,96,256]{2,1,0:T(8,128)S(1)}, f32[3,96,256]{2,1,0:T(8,128)S(1)}, u32[]{:S(2)}, u32[]{:S(2)}) collective-permute-start(f32[3,96,256]{2,1,0:T(8,128)S(1)} %get-tuple-element.52.after), channel_id=1, source_target_pairs={{2,4},{4,2},{6,8},{8,6},{10,12},{12,10},{3,5},{5,3},{7,9},{9,7},{1... | collective-permute-start | bytes 884744 | tf_op jit(solution)/shard_map/ppermute | solution.py:588
  10.9 0.0 copy-done
  10.9 0.0 copy-done.1
  10.9 0.0 copy-done.2
  10.9 0.0 copy-done.3
  10.9 2.1 %shard_map.123 = (f32[8,96,256]{2,1,0:T(8,128)S(1)}, f32[8,96,256]{2,1,0:T(8,128)S(1)}, f32[8,96,256]{2,1,0:T(8,128)S(1)}, f32[8,96,256]{2,1,0:T(8,128)S(1)}, f3...) custom-call(s32[1]{0:T(128)S(6)} %copy.56.off, ...), custom_call_target="tpu_custom_call", output_to_operand_aliasing={{9}: (14, {})} | custom-call | flops 40000000000 | bytes 1024 | tf_op jit(solution)/shard_map/pallas_call | solution.py:590
  13.0 1.7 %shard_map.124 = (f32[8,96,256]{2,1,0:T(8,128)S(1)}, f32[8,96,256]{2,1,0:T(8,128)S(1)}, f32[8,96,256]{2,1,0:T(8,128)S(1)}, f32[8,96,256]{2,1,0:T(8,128)S(1)}, f3...) custom-call(s32[1]{0:T(128)S(6)} %copy.57.step, ...), custom_call_target="tpu_custom_call", output_to_operand_aliasing={{0}: (9, {}), {1}: (10, {}), {2}: (11, {}), {3}: (12, {}), ... | custom-call | flops 40000000000 | bytes 1024 | tf_op jit(solution)/shard_map/pallas_call | solution.py:616
  14.7 0.0 collective-permute-done.recv
  14.7 0.1 shard_map.125
  14.9 0.3 %collective-permute-start.1 = (f32[2,96,256]{2,1,0:T(8,128)S(1)}, f32[2,96,256]{2,1,0:T(8,128)S(1)}, u32[]{:S(2)}, u32[]{:S(2)}) collective-permute-start(f32[2,96,256]{2,1,0:T(8,128)S(1)} %get-tuple-element.70.send), channel_id=1, source_target_pairs={{0,2},{2,0},{4,6},{6,4},{8,10},{10,8},{12,14},{14,12},{1,3},{3,1},... | collective-permute-start | bytes 589832 | tf_op jit(solution)/shard_map/ppermute | solution.py:630
  15.2 2.0 %shard_map.127 = (f32[8,96,256]{2,1,0:T(8,128)S(1)}, f32[2,8,96,256]{3,2,1,0:T(8,128)S(1)}) custom-call(f32[1,2,8,96,256]{4,3,2,1,0:T(8,128)S(1)} %copy-done, f32[1,2,8,96,256]{4,3,2,1,0:T(8,128)S(1)} %copy-done.1, f32[8,96,256]{2,1,0:T(8,128)S(1)} %get-tuple-element.57.kq, f32[8,96,256]{2,1,0:T(8,128)S(1)} %get-tuple-element.59.hb, ...), custom_call_target="tpu_custom_call" | custom-call | flops 40000000000 | bytes 1024 | tf_op jit(solution)/shard_map/pallas_call | solution.py:634
  17.2 0.0 collective-permute-done.2.recv
  17.2 0.1 shard_map.126
  17.3 3.0 %collective-permute-start.4 = (f32[2,96,256]{2,1,0:T(8,128)S(1)}, f32[2,96,256]{2,1,0:T(8,128)S(1)}, u32[]{:S(2)}, u32[]{:S(2)}) collective-permute-start(f32[2,96,256]{2,1,0:T(8,128)S(1)} %get-tuple-element.88.send), channel_id=1, source_target_pairs={{2,4},{4,2},{6,8},{8,6},{10,12},{12,10},{3,5},{5,3},{7,9},{9,7},{1... | collective-permute-start | bytes 589832 | tf_op jit(solution)/shard_map/ppermute | solution.py:647
  20.4 0.7 %shard_map.128 = (f32[8,96,256]{2,1,0:T(8,128)S(1)}, f32[2,8,96,256]{3,2,1,0:T(8,128)S(1)}) custom-call(f32[1,2,8,96,256]{4,3,2,1,0:T(8,128)S(1)} %copy-done, f32[1,2,8,96,256]{4,3,2,1,0:T(8,128)S(1)} %copy-done.1, f32[8,96,256]{2,1,0:T(8,128)S(1)} %get-tuple-element.57.kq, ...), custom_call_target="tpu_custom_call", output_to_operand_aliasing={{0}: (11, {}), {1}: (12, {})} | custom-call | flops 2000000000 | bytes 1024 | tf_op jit(solution)/shard_map/pallas_call | solution.py:634
  21.1 0.8 %collective-permute-done.1.recv2 = f32[2,96,256]{2,1,0:T(8,128)S(1)} collective-permute-done((f32[2,96,256]{2,1,0:T(8,128)S(1)}, f32[2,96,256]{2,1,0:T(8,128)S(1)}, u32[]{:S(2)}, u32[]{:S(2)}) %collective-permute-start.1) | collective-permute-done | bytes 196640 | tf_op jit(solution)/shard_map/ppermute | solution.py:630
  21.9 1.2 %shard_map.129 = (f32[1,2,8,96,256]{4,3,2,1,0:T(8,128)}, f32[8,96,256]{2,1,0:T(8,128)S(1)}, f32[2,8,64,256]{3,2,1,0:T(8,128)S(1)}, f32[2,8,64,256]{3,2,1,0:T(8,128)S(1)}) custom-call(s32[1]{0:T(128)S(6)} %copy.56.off, f32[3,96,256]{2,1,0:T(8,128)S(1)} %collective-permute-done.recv, ...), custom_call_target="tpu_custom_call", output_to_operand_aliasing={{1}: (8, {})} | custom-call | flops 2000000000 | bytes 1024 | tf_op jit(solution)/shard_map/pallas_call | solution.py:650
  23.1 1.2 %collective-permute-start.3 = (f32[2,8,64,256]{3,2,1,0:T(8,128)S(1)}, f32[2,8,64,256]{3,2,1,0:T(8,128)S(1)}, u32[]{:S(2)}, u32[]{:S(2)}) collective-permute-start(f32[2,8,64,256]{3,2,1,0:T(8,128)S(1)} %get-tuple-element.87), channel_id=1, source_target_pairs={{0,1},{1,0},{2,3},{3,2},{4,5},{5,4},{6,7},{7,6},{8,9},{9,8},{10,11... | collective-permute-start | bytes 3145736 | tf_op jit(solution)/shard_map/ppermute | solution.py:663
  24.3 0.4 %collective-permute-done.4.recv2 = f32[2,96,256]{2,1,0:T(8,128)S(1)} collective-permute-done((f32[2,96,256]{2,1,0:T(8,128)S(1)}, f32[2,96,256]{2,1,0:T(8,128)S(1)}, u32[]{:S(2)}, u32[]{:S(2)}) %collective-permute-start.4) | collective-permute-done | bytes 196640 | tf_op jit(solution)/shard_map/ppermute | solution.py:647
  24.6 0.1 shard_map.130
  24.8 2.9 %collective-permute-start.5 = (f32[2,64,256]{2,1,0:T(8,128)S(1)}, f32[2,64,256]{2,1,0:T(8,128)S(1)}, u32[]{:S(2)}, u32[]{:S(2)}) collective-permute-start(f32[2,64,256]{2,1,0:T(8,128)S(1)} %get-tuple-element.92), channel_id=1, source_target_pairs={{0,1},{1,0},{2,3},{3,2},{4,5},{5,4},{6,7},{7,6},{8,9},{9,8},{10,11... | collective-permute-start | bytes 393224 | tf_op jit(solution)/shard_map/ppermute | solution.py:672
  27.6 0.0 collective-permute-done.3.recv
  27.6 1.0 %shard_map.131 = (f32[8,64,256]{2,1,0:T(8,128)}, f32[8,64,256]{2,1,0:T(8,128)}, f32[2,64,256]{2,1,0:T(8,128)S(1)}) custom-call(f32[2,8,64,256]{3,2,1,0:T(8,128)S(1)} %get-tuple-element.86.mine, f32[2,8,64,256]{3,2,1,0:T(8,128)S(1)} %collective-permute-done.3.recv, f32[2,64,256]{2,1,0:T(8,128)S(1)} %get-tuple-element.90.mine_e), custom_call_target="tpu_custom_call" | custom-call | flops 40000000000 | bytes 1024 | tf_op jit(solution)/shard_map/pallas_call | solution.py:673
  28.7 0.0 collective-permute-done.5.recv_e
  28.7 0.7 %shard_map.132 = (f32[8,64,256]{2,1,0:T(8,128)}, f32[8,64,256]{2,1,0:T(8,128)}, f32[1,2,8,96,256]{4,3,2,1,0:T(8,128)}) custom-call(f32[2,64,256]{2,1,0:T(8,128)S(1)} %get-tuple-element.91.sums_e, f32[2,64,256]{2,1,0:T(8,128)S(1)} %collective-permute-done.5.recv_e, ...), custom_call_target="tpu_custom_call", output_to_operand_aliasing={{0}: (3, {}), {1}: (4, {}), {2}: (5, {})} | custom-call | tf_op jit(solution)/shard_map/pallas_call | solution.py:682
Async XLA Ops:
  1.3 2.5 %copy-start.4 = (f32[1,2,6400]{2,1,0:T(2,128)S(1)}, f32[1,2,6400]{2,1,0:T(2,128)}, u32[]{:S(2)}) copy-start(f32[1,2,6400]{2,1,0:T(2,128)} %res.1) | copy-start | bytes 153604
  1.3 2.5 %copy-start.5 = (s32[1,6400]{1,0:T(1,128)S(1)}, s32[1,6400]{1,0:T(1,128)}, u32[]{:S(2)}) copy-start(s32[1,6400]{1,0:T(1,128)} %rec.1) | copy-start | bytes 76804
  2.5 8.4 %copy-start = (f32[1,2,8,96,256]{4,3,2,1,0:T(8,128)S(1)}, f32[1,2,8,96,256]{4,3,2,1,0:T(8,128)}, u32[]{:S(2)}) copy-start(f32[1,2,8,96,256]{4,3,2,1,0:T(8,128)} %ckpt.19) | copy-start | bytes 4718596
  2.5 8.4 %copy-start.1 = (f32[1,2,8,96,256]{4,3,2,1,0:T(8,128)S(1)}, f32[1,2,8,96,256]{4,3,2,1,0:T(8,128)}, u32[]{:S(2)}) copy-start(f32[1,2,8,96,256]{4,3,2,1,0:T(8,128)} %adj.15) | copy-start | bytes 4718596
  2.5 8.4 %copy-start.2 = (f32[8,128,256]{2,1,0:T(8,128)S(1)}, f32[8,128,256]{2,1,0:T(8,128)}, u32[]{:S(2)}) copy-start(f32[8,128,256]{2,1,0:T(8,128)} %k_full.1) | copy-start | bytes 3145732
  2.5 8.4 %copy-start.3 = (f32[8,128,256]{2,1,0:T(8,128)S(1)}, f32[8,128,256]{2,1,0:T(8,128)}, u32[]{:S(2)}) copy-start(f32[8,128,256]{2,1,0:T(8,128)} %b_full.1) | copy-start | bytes 3145732
  2.5 12.2 %collective-permute-start = (f32[3,96,256]{2,1,0:T(8,128)S(1)}, f32[3,96,256]{2,1,0:T(8,128)S(1)}, u32[]{:S(2)}, u32[]{:S(2)}) collective-permute-start(f32[3,96,256]{2,1,0:T(8,128)S(1)} %shard_map.121.after), channel_id=1, source_target_pairs={{0,2},{2,0},{4,6},{6,4},{8,10},{10,8},{12,14},{14,12},{1,3},{3,1},... | collective-permute-start | bytes 884744 | tf_op jit(solution)/shard_map/ppermute | solution.py:570
  6.6 10.6 %collective-permute-start.2 = (f32[3,96,256]{2,1,0:T(8,128)S(1)}, f32[3,96,256]{2,1,0:T(8,128)S(1)}, u32[]{:S(2)}, u32[]{:S(2)}) collective-permute-start(f32[3,96,256]{2,1,0:T(8,128)S(1)} %get-tuple-element.52.after), channel_id=1, source_target_pairs={{2,4},{4,2},{6,8},{8,6},{10,12},{12,10},{3,5},{5,3},{7,9},{9,7},{1... | collective-permute-start | bytes 884744 | tf_op jit(solution)/shard_map/ppermute | solution.py:588
  14.9 7.0 %collective-permute-start.1 = (f32[2,96,256]{2,1,0:T(8,128)S(1)}, f32[2,96,256]{2,1,0:T(8,128)S(1)}, u32[]{:S(2)}, u32[]{:S(2)}) collective-permute-start(f32[2,96,256]{2,1,0:T(8,128)S(1)} %get-tuple-element.70.send), channel_id=1, source_target_pairs={{0,2},{2,0},{4,6},{6,4},{8,10},{10,8},{12,14},{14,12},{1,3},{3,1},... | collective-permute-start | bytes 589832 | tf_op jit(solution)/shard_map/ppermute | solution.py:630
  17.3 7.3 %collective-permute-start.4 = (f32[2,96,256]{2,1,0:T(8,128)S(1)}, f32[2,96,256]{2,1,0:T(8,128)S(1)}, u32[]{:S(2)}, u32[]{:S(2)}) collective-permute-start(f32[2,96,256]{2,1,0:T(8,128)S(1)} %get-tuple-element.88.send), channel_id=1, source_target_pairs={{2,4},{4,2},{6,8},{8,6},{10,12},{12,10},{3,5},{5,3},{7,9},{9,7},{1... | collective-permute-start | bytes 589832 | tf_op jit(solution)/shard_map/ppermute | solution.py:647
  23.1 4.6 %collective-permute-start.3 = (f32[2,8,64,256]{3,2,1,0:T(8,128)S(1)}, f32[2,8,64,256]{3,2,1,0:T(8,128)S(1)}, u32[]{:S(2)}, u32[]{:S(2)}) collective-permute-start(f32[2,8,64,256]{3,2,1,0:T(8,128)S(1)} %get-tuple-element.87), channel_id=1, source_target_pairs={{0,1},{1,0},{2,3},{3,2},{4,5},{5,4},{6,7},{7,6},{8,9},{9,8},{10,11... | collective-permute-start | bytes 3145736 | tf_op jit(solution)/shard_map/ppermute | solution.py:663
  24.8 3.9 %collective-permute-start.5 = (f32[2,64,256]{2,1,0:T(8,128)S(1)}, f32[2,64,256]{2,1,0:T(8,128)S(1)}, u32[]{:S(2)}, u32[]{:S(2)}) collective-permute-start(f32[2,64,256]{2,1,0:T(8,128)S(1)} %get-tuple-element.92), channel_id=1, source_target_pairs={{0,1},{1,0},{2,3},{3,2},{4,5},{5,4},{6,7},{7,6},{8,9},{9,8},{10,11... | collective-permute-start | bytes 393224 | tf_op jit(solution)/shard_map/ppermute | solution.py:672

commit v6 on v5

--- a/solution.py
+++ b/solution.py
@@ -507,9 +507,10 @@
     mine[1], other[1] = split(add_b, off[0], half)
 
 
-def combine(mine, recv, mine_e, grad_k, grad_b, sums_e, sums, sem):
+def combine(mine, recv, mine_e, last_e, adj_in, grad_k, grad_b, sums_e, adj_out, sums, sem):
     edge = edges(sums.shape[1])[1]
-    copies = []
+    copies = [pltpu.make_async_copy(last_e, adj_out.at[0, 1, edge], sem.at[2])]
+    copies[0].start()
     for g, grad in enumerate((grad_k, grad_b)):
         sums[g] = mine[g] + recv[g]
         copy = pltpu.make_async_copy(sums.at[g], grad, sem.at[g])
@@ -521,10 +522,9 @@
         copy.wait()
 
 
-def finish(sums_e, recv_e, last_e, grad_k_in, grad_b_in, adj_in, grad_k, grad_b, adj_out, sums, sem):
+def finish(sums_e, recv_e, grad_k_in, grad_b_in, grad_k, grad_b, sums, sem):
     edge = edges(grad_k.shape[0])[1]
-    copies = [pltpu.make_async_copy(last_e, adj_out.at[0, 1, edge], sem.at[2])]
-    copies[0].start()
+    copies = []
     for g, grad in enumerate((grad_k, grad_b)):
         sums[g] = sums_e[g] + recv_e[g]
         copy = pltpu.make_async_copy(sums.at[g], grad.at[edge], sem.at[g])
@@ -670,24 +670,26 @@
         cost_estimate=cost(40),
     )(offsets, *[near(v) for v in (recv_2, recv2_2, send2_2, checkpoint, adjoint, kq, hb, last)])
     recv_e = lax.ppermute(other_e, "shot", swap)
-    grad_k, grad_b, sums_e = pl.pallas_call(
+    grad_k, grad_b, sums_e, adj_next = pl.pallas_call(
         combine,
-        in_specs=[VM] * 3,
-        out_specs=[ANY, ANY, VM],
-        out_shape=[grad_shape, grad_shape, vmem(2, half, nz)],
-        scratch_shapes=[vmem(2, width, half, nz), dma((2,))],
+        in_specs=[VM] * 4 + [ANY],
+        out_specs=[ANY, ANY, VM, ANY],
+        out_shape=[grad_shape, grad_shape, vmem(2, half, nz), adj_shape],
+        scratch_shapes=[vmem(2, width, half, nz), dma((3,))],
+        input_output_aliases={4: 3},
         compiler_params=params(),
         cost_estimate=cost(40),
-    )(near(mine), near(recv_g), near(mine_e))
-    return pl.pallas_call(
+    )(near(mine), near(recv_g), near(mine_e), near(last_e), far(adj_part))
+    grad_k, grad_b = pl.pallas_call(
         finish,
-        in_specs=[VM] * 3 + [ANY] * 3,
-        out_specs=[ANY] * 3,
-        out_shape=[grad_shape, grad_shape, adj_shape],
-        scratch_shapes=[vmem(2, half, nz), dma((3,))],
-        input_output_aliases={3: 0, 4: 1, 5: 2},
+        in_specs=[VM] * 2 + [ANY] * 2,
+        out_specs=[ANY] * 2,
+        out_shape=[grad_shape, grad_shape],
+        scratch_shapes=[vmem(2, half, nz), dma((2,))],
+        input_output_aliases={2: 0, 3: 1},
         compiler_params=params(),
-    )(near(sums_e), near(recv_e), near(last_e), far(grad_k), far(grad_b), far(adj_part))
+    )(near(sums_e), near(recv_e), far(grad_k), far(grad_b))
+    return grad_k, grad_b, adj_next
 
 
 def solution(mesh):

time: 29.9 us -> 29.8 us (level)
  no operation moved by 1% of the time
where the time goes in v6:
time: 29.8 us; the launch traced here: 29.4 us
  Pallas kernels  13.7 us (46%)
  starting transfers between devices  11.7 us (39%)
  between operations  2.77 us (9%)
  waiting for transfers between devices  1.21 us (4%)
    ppermute x1, starting transfers between devices, shards(): recv2_2 = lax.ppermute(send2_2, 'dom', swaps[1])  3.03 us
    ppermute x1, starting transfers between devices, shards(): recv_2 = lax.ppermute(send_2, 'dom', swaps[1])  2.99 us
    ppermute x1, starting transfers between devices, shards(): recv_e = lax.ppermute(other_e, 'shot', swap)  2.89 us
    pallas_call x1, Pallas kernels, shards(): pl.pallas_call(receivers, in_specs=[SM, VM, VM] + [ANY] * 4 + [VM], out_s...  2.78 us
    pallas_call x2, Pallas kernels, second_step(): pl.pallas_call(functools.partial(step_two, part), in_specs=[VM] * (11 + l...  2.72 us
    pallas_call x1, Pallas kernels, shards(): pl.pallas_call(step_one_ends, in_specs=[SM] * 4 + [ANY] + [VM] * 10, out_...  2.1 us
    pallas_call x1, Pallas kernels, shards(): pl.pallas_call(step_one_middle, in_specs=[SM] * 2 + [ANY] + [VM] * 12, ou...  1.7 us
    ppermute x1, starting transfers between devices, shards(): recv_1 = lax.ppermute(send_1, 'dom', swaps[0])  1.28 us
  transfers between devices with their start and end apart: 6, of which 2 were waited for; matrix products, arithmetic and copies ran while one was open for 0% of the time, Pallas kernels for 40%

profile of v6, /device:TPU:9, one launch (start us, length us, event | category | flops | bytes accessed | tf_op | source)
XLA Modules:
  0.0 29.4 jit_solution(6490198476810478461)
XLA Ops:
  1.3 0.0 copy-start.4
  1.3 0.0 copy-start.5
  1.3 1.1 %shard_map.121.after = f32[3,96,256]{2,1,0:T(8,128)S(1)} custom-call(s32[1]{0:T(128)S(6)} %copy.56.off, f32[1,2,8,96,256]{4,3,2,1,0:T(8,128)} %ckpt.19, f32[1,2,8,96,256]{4,3,2,1,0:T(8,128)} %adj.15, f32[8,128,256]{2,1,0:T(8,128)} %k_full.1, f32[8,128,256]{2,1,0:T(8,128)} %b_full.1), custom_call_target="tpu_custom_call" | custom-call | tf_op jit(solution)/shard_map/pallas_call | solution.py:562
  2.5 0.0 copy-start
  2.5 0.0 copy-start.1
  2.5 0.0 copy-start.2
  2.5 0.0 copy-start.3
  2.5 1.3 %collective-permute-start = (f32[3,96,256]{2,1,0:T(8,128)S(1)}, f32[3,96,256]{2,1,0:T(8,128)S(1)}, u32[]{:S(2)}, u32[]{:S(2)}) collective-permute-start(f32[3,96,256]{2,1,0:T(8,128)S(1)} %shard_map.121.after), channel_id=1, source_target_pairs={{0,2},{2,0},{4,6},{6,4},{8,10},{10,8},{12,14},{14,12},{1,3},{3,1},... | collective-permute-start | bytes 884744 | tf_op jit(solution)/shard_map/ppermute | solution.py:570
  3.8 0.0 copy-done.4
  3.8 0.0 copy-done.5
  3.8 2.8 %shard_map.122 = (f32[768,256]{1,0:T(8,128)S(1)}, f32[768,256]{1,0:T(8,128)S(1)}, f32[3,96,256]{2,1,0:T(8,128)S(1)}, bf16[768,1280]{1,0:T(8,128)(2,1)S(1)}, bf16...) custom-call(s32[1]{0:T(128)S(6)} %copy.56.off, s32[1,6400]{1,0:T(1,128)S(1)} %copy-done.5, ...), custom_call_target="tpu_custom_call" | custom-call | flops 40000000000 | bytes 1024 | tf_op jit(solution)/shard_map/pallas_call | solution.py:574
  6.6 3.0 %collective-permute-start.2 = (f32[3,96,256]{2,1,0:T(8,128)S(1)}, f32[3,96,256]{2,1,0:T(8,128)S(1)}, u32[]{:S(2)}, u32[]{:S(2)}) collective-permute-start(f32[3,96,256]{2,1,0:T(8,128)S(1)} %get-tuple-element.55.after), channel_id=1, source_target_pairs={{2,4},{4,2},{6,8},{8,6},{10,12},{12,10},{3,5},{5,3},{7,9},{9,7},{1... | collective-permute-start | bytes 884744 | tf_op jit(solution)/shard_map/ppermute | solution.py:588
  10.9 0.0 copy-done
  10.9 0.0 copy-done.1
  10.9 0.0 copy-done.2
  10.9 0.0 copy-done.3
  10.9 2.1 %shard_map.123 = (f32[8,96,256]{2,1,0:T(8,128)S(1)}, f32[8,96,256]{2,1,0:T(8,128)S(1)}, f32[8,96,256]{2,1,0:T(8,128)S(1)}, f32[8,96,256]{2,1,0:T(8,128)S(1)}, f3...) custom-call(s32[1]{0:T(128)S(6)} %copy.56.off, ...), custom_call_target="tpu_custom_call", output_to_operand_aliasing={{9}: (14, {})} | custom-call | flops 40000000000 | bytes 1024 | tf_op jit(solution)/shard_map/pallas_call | solution.py:590
  13.0 1.7 %shard_map.124 = (f32[8,96,256]{2,1,0:T(8,128)S(1)}, f32[8,96,256]{2,1,0:T(8,128)S(1)}, f32[8,96,256]{2,1,0:T(8,128)S(1)}, f32[8,96,256]{2,1,0:T(8,128)S(1)}, f3...) custom-call(s32[1]{0:T(128)S(6)} %copy.57.step, ...), custom_call_target="tpu_custom_call", output_to_operand_aliasing={{0}: (9, {}), {1}: (10, {}), {2}: (11, {}), {3}: (12, {}), ... | custom-call | flops 40000000000 | bytes 1024 | tf_op jit(solution)/shard_map/pallas_call | solution.py:616
  14.7 0.0 collective-permute-done.recv
  14.7 0.1 shard_map.125
  14.9 0.3 %collective-permute-start.1 = (f32[2,96,256]{2,1,0:T(8,128)S(1)}, f32[2,96,256]{2,1,0:T(8,128)S(1)}, u32[]{:S(2)}, u32[]{:S(2)}) collective-permute-start(f32[2,96,256]{2,1,0:T(8,128)S(1)} %get-tuple-element.73.send), channel_id=1, source_target_pairs={{0,2},{2,0},{4,6},{6,4},{8,10},{10,8},{12,14},{14,12},{1,3},{3,1},... | collective-permute-start | bytes 589832 | tf_op jit(solution)/shard_map/ppermute | solution.py:630
  15.2 2.0 %shard_map.127 = (f32[8,96,256]{2,1,0:T(8,128)S(1)}, f32[2,8,96,256]{3,2,1,0:T(8,128)S(1)}) custom-call(f32[1,2,8,96,256]{4,3,2,1,0:T(8,128)S(1)} %copy-done, f32[1,2,8,96,256]{4,3,2,1,0:T(8,128)S(1)} %copy-done.1, f32[8,96,256]{2,1,0:T(8,128)S(1)} %get-tuple-element.60.kq, f32[8,96,256]{2,1,0:T(8,128)S(1)} %get-tuple-element.62.hb, ...), custom_call_target="tpu_custom_call" | custom-call | flops 40000000000 | bytes 1024 | tf_op jit(solution)/shard_map/pallas_call | solution.py:634
  17.2 0.0 collective-permute-done.2.recv
  17.2 0.1 shard_map.126
  17.3 3.0 %collective-permute-start.4 = (f32[2,96,256]{2,1,0:T(8,128)S(1)}, f32[2,96,256]{2,1,0:T(8,128)S(1)}, u32[]{:S(2)}, u32[]{:S(2)}) collective-permute-start(f32[2,96,256]{2,1,0:T(8,128)S(1)} %get-tuple-element.91.send), channel_id=1, source_target_pairs={{2,4},{4,2},{6,8},{8,6},{10,12},{12,10},{3,5},{5,3},{7,9},{9,7},{1... | collective-permute-start | bytes 589832 | tf_op jit(solution)/shard_map/ppermute | solution.py:647
  20.4 0.7 %shard_map.128 = (f32[8,96,256]{2,1,0:T(8,128)S(1)}, f32[2,8,96,256]{3,2,1,0:T(8,128)S(1)}) custom-call(f32[1,2,8,96,256]{4,3,2,1,0:T(8,128)S(1)} %copy-done, f32[1,2,8,96,256]{4,3,2,1,0:T(8,128)S(1)} %copy-done.1, f32[8,96,256]{2,1,0:T(8,128)S(1)} %get-tuple-element.60.kq, ...), custom_call_target="tpu_custom_call", output_to_operand_aliasing={{0}: (11, {}), {1}: (12, {})} | custom-call | flops 2000000000 | bytes 1024 | tf_op jit(solution)/shard_map/pallas_call | solution.py:634
  21.1 0.8 %collective-permute-done.1.recv2 = f32[2,96,256]{2,1,0:T(8,128)S(1)} collective-permute-done((f32[2,96,256]{2,1,0:T(8,128)S(1)}, f32[2,96,256]{2,1,0:T(8,128)S(1)}, u32[]{:S(2)}, u32[]{:S(2)}) %collective-permute-start.1) | collective-permute-done | bytes 196640 | tf_op jit(solution)/shard_map/ppermute | solution.py:630
  21.9 1.2 %shard_map.129 = (f32[1,2,8,96,256]{4,3,2,1,0:T(8,128)}, f32[8,96,256]{2,1,0:T(8,128)S(1)}, f32[2,8,64,256]{3,2,1,0:T(8,128)S(1)}, f32[2,8,64,256]{3,2,1,0:T(8,128)S(1)}) custom-call(s32[1]{0:T(128)S(6)} %copy.56.off, f32[3,96,256]{2,1,0:T(8,128)S(1)} %collective-permute-done.recv, ...), custom_call_target="tpu_custom_call", output_to_operand_aliasing={{1}: (8, {})} | custom-call | flops 2000000000 | bytes 1024 | tf_op jit(solution)/shard_map/pallas_call | solution.py:650
  23.1 1.2 %collective-permute-start.3 = (f32[2,8,64,256]{3,2,1,0:T(8,128)S(1)}, f32[2,8,64,256]{3,2,1,0:T(8,128)S(1)}, u32[]{:S(2)}, u32[]{:S(2)}) collective-permute-start(f32[2,8,64,256]{3,2,1,0:T(8,128)S(1)} %get-tuple-element.90), channel_id=1, source_target_pairs={{0,1},{1,0},{2,3},{3,2},{4,5},{5,4},{6,7},{7,6},{8,9},{9,8},{10,11... | collective-permute-start | bytes 3145736 | tf_op jit(solution)/shard_map/ppermute | solution.py:663
  24.3 0.4 %collective-permute-done.4.recv2 = f32[2,96,256]{2,1,0:T(8,128)S(1)} collective-permute-done((f32[2,96,256]{2,1,0:T(8,128)S(1)}, f32[2,96,256]{2,1,0:T(8,128)S(1)}, u32[]{:S(2)}, u32[]{:S(2)}) %collective-permute-start.4) | collective-permute-done | bytes 196640 | tf_op jit(solution)/shard_map/ppermute | solution.py:647
  24.6 0.1 shard_map.130
  24.8 2.9 %collective-permute-start.5 = (f32[2,64,256]{2,1,0:T(8,128)S(1)}, f32[2,64,256]{2,1,0:T(8,128)S(1)}, u32[]{:S(2)}, u32[]{:S(2)}) collective-permute-start(f32[2,64,256]{2,1,0:T(8,128)S(1)} %get-tuple-element.97), channel_id=1, source_target_pairs={{0,1},{1,0},{2,3},{3,2},{4,5},{5,4},{6,7},{7,6},{8,9},{9,8},{10,11... | collective-permute-start | bytes 393224 | tf_op jit(solution)/shard_map/ppermute | solution.py:672
  27.6 0.0 collective-permute-done.3.recv
  27.6 1.0 %shard_map.131 = (f32[8,64,256]{2,1,0:T(8,128)}, f32[8,64,256]{2,1,0:T(8,128)}, f32[2,64,256]{2,1,0:T(8,128)S(1)}, f32[1,2,8,96,256]{4,3,2,1,0:T(8,128)}) custom-call(f32[2,8,64,256]{3,2,1,0:T(8,128)S(1)} %get-tuple-element.89.mine, f32[2,8,64,256]{3,2,1,0:T(8,128)S(1)} %collective-permute-done.3.recv, ...), custom_call_target="tpu_custom_call", output_to_operand_aliasing={{3}: (4, {})} | custom-call | flops 40000000000 | bytes 1024 | tf_op jit(solution)/shard_map/pallas_call | solution.py:673
  28.7 0.0 collective-permute-done.5.recv_e
  28.7 0.7 %shard_map.132 = (f32[8,64,256]{2,1,0:T(8,128)}, f32[8,64,256]{2,1,0:T(8,128)}) custom-call(f32[2,64,256]{2,1,0:T(8,128)S(1)} %get-tuple-element.96.sums_e, f32[2,64,256]{2,1,0:T(8,128)S(1)} %collective-permute-done.5.recv_e, f32[8,64,256]{2,1,0:T(8,128)} %get-tuple-element.98.grad_k_in, ...), custom_call_target="tpu_custom_call", output_to_operand_aliasing={{0}: (2, {}), {1}: (3, {})} | custom-call | tf_op jit(solution)/shard_map/pallas_call | solution.py:683
Async XLA Ops:
  1.3 2.5 %copy-start.4 = (f32[1,2,6400]{2,1,0:T(2,128)S(1)}, f32[1,2,6400]{2,1,0:T(2,128)}, u32[]{:S(2)}) copy-start(f32[1,2,6400]{2,1,0:T(2,128)} %res.1) | copy-start | bytes 153604
  1.3 2.5 %copy-start.5 = (s32[1,6400]{1,0:T(1,128)S(1)}, s32[1,6400]{1,0:T(1,128)}, u32[]{:S(2)}) copy-start(s32[1,6400]{1,0:T(1,128)} %rec.1) | copy-start | bytes 76804
  2.5 8.4 %copy-start = (f32[1,2,8,96,256]{4,3,2,1,0:T(8,128)S(1)}, f32[1,2,8,96,256]{4,3,2,1,0:T(8,128)}, u32[]{:S(2)}) copy-start(f32[1,2,8,96,256]{4,3,2,1,0:T(8,128)} %ckpt.19) | copy-start | bytes 4718596
  2.5 8.4 %copy-start.1 = (f32[1,2,8,96,256]{4,3,2,1,0:T(8,128)S(1)}, f32[1,2,8,96,256]{4,3,2,1,0:T(8,128)}, u32[]{:S(2)}) copy-start(f32[1,2,8,96,256]{4,3,2,1,0:T(8,128)} %adj.15) | copy-start | bytes 4718596
  2.5 8.4 %copy-start.2 = (f32[8,128,256]{2,1,0:T(8,128)S(1)}, f32[8,128,256]{2,1,0:T(8,128)}, u32[]{:S(2)}) copy-start(f32[8,128,256]{2,1,0:T(8,128)} %k_full.1) | copy-start | bytes 3145732
  2.5 8.4 %copy-start.3 = (f32[8,128,256]{2,1,0:T(8,128)S(1)}, f32[8,128,256]{2,1,0:T(8,128)}, u32[]{:S(2)}) copy-start(f32[8,128,256]{2,1,0:T(8,128)} %b_full.1) | copy-start | bytes 3145732
  2.5 12.2 %collective-permute-start = (f32[3,96,256]{2,1,0:T(8,128)S(1)}, f32[3,96,256]{2,1,0:T(8,128)S(1)}, u32[]{:S(2)}, u32[]{:S(2)}) collective-permute-start(f32[3,96,256]{2,1,0:T(8,128)S(1)} %shard_map.121.after), channel_id=1, source_target_pairs={{0,2},{2,0},{4,6},{6,4},{8,10},{10,8},{12,14},{14,12},{1,3},{3,1},... | collective-permute-start | bytes 884744 | tf_op jit(solution)/shard_map/ppermute | solution.py:570
  6.6 10.6 %collective-permute-start.2 = (f32[3,96,256]{2,1,0:T(8,128)S(1)}, f32[3,96,256]{2,1,0:T(8,128)S(1)}, u32[]{:S(2)}, u32[]{:S(2)}) collective-permute-start(f32[3,96,256]{2,1,0:T(8,128)S(1)} %get-tuple-element.55.after), channel_id=1, source_target_pairs={{2,4},{4,2},{6,8},{8,6},{10,12},{12,10},{3,5},{5,3},{7,9},{9,7},{1... | collective-permute-start | bytes 884744 | tf_op jit(solution)/shard_map/ppermute | solution.py:588
  14.9 7.0 %collective-permute-start.1 = (f32[2,96,256]{2,1,0:T(8,128)S(1)}, f32[2,96,256]{2,1,0:T(8,128)S(1)}, u32[]{:S(2)}, u32[]{:S(2)}) collective-permute-start(f32[2,96,256]{2,1,0:T(8,128)S(1)} %get-tuple-element.73.send), channel_id=1, source_target_pairs={{0,2},{2,0},{4,6},{6,4},{8,10},{10,8},{12,14},{14,12},{1,3},{3,1},... | collective-permute-start | bytes 589832 | tf_op jit(solution)/shard_map/ppermute | solution.py:630
  17.3 7.3 %collective-permute-start.4 = (f32[2,96,256]{2,1,0:T(8,128)S(1)}, f32[2,96,256]{2,1,0:T(8,128)S(1)}, u32[]{:S(2)}, u32[]{:S(2)}) collective-permute-start(f32[2,96,256]{2,1,0:T(8,128)S(1)} %get-tuple-element.91.send), channel_id=1, source_target_pairs={{2,4},{4,2},{6,8},{8,6},{10,12},{12,10},{3,5},{5,3},{7,9},{9,7},{1... | collective-permute-start | bytes 589832 | tf_op jit(solution)/shard_map/ppermute | solution.py:647
  23.1 4.6 %collective-permute-start.3 = (f32[2,8,64,256]{3,2,1,0:T(8,128)S(1)}, f32[2,8,64,256]{3,2,1,0:T(8,128)S(1)}, u32[]{:S(2)}, u32[]{:S(2)}) collective-permute-start(f32[2,8,64,256]{3,2,1,0:T(8,128)S(1)} %get-tuple-element.90), channel_id=1, source_target_pairs={{0,1},{1,0},{2,3},{3,2},{4,5},{5,4},{6,7},{7,6},{8,9},{9,8},{10,11... | collective-permute-start | bytes 3145736 | tf_op jit(solution)/shard_map/ppermute | solution.py:663
  24.8 3.9 %collective-permute-start.5 = (f32[2,64,256]{2,1,0:T(8,128)S(1)}, f32[2,64,256]{2,1,0:T(8,128)S(1)}, u32[]{:S(2)}, u32[]{:S(2)}) collective-permute-start(f32[2,64,256]{2,1,0:T(8,128)S(1)} %get-tuple-element.97), channel_id=1, source_target_pairs={{0,1},{1,0},{2,3},{3,2},{4,5},{5,4},{6,7},{7,6},{8,9},{9,8},{10,11... | collective-permute-start | bytes 393224 | tf_op jit(solution)/shard_map/ppermute | solution.py:672

commit v7 on v6

--- a/solution.py
+++ b/solution.py
@@ -72,9 +72,9 @@
 
 def edge_copies(edge, ckpt, adj, kappa, buoy, send, q_e, k_e, b_e, sem):
     return [
-        pltpu.make_async_copy(adj.at[0, 1, edge], q_e, sem.at[1]),
         pltpu.make_async_copy(kappa.at[edge], k_e, sem.at[2]),
         pltpu.make_async_copy(buoy.at[edge], b_e, sem.at[3]),
+        pltpu.make_async_copy(adj.at[0, 1, edge], q_e, sem.at[1]),
         pltpu.make_async_copy(ckpt.at[0, 1, edge], send.at[0], sem.at[0]),
     ]
 
@@ -90,9 +90,14 @@
     copies = edge_copies(edge, ckpt, adj, kappa, buoy, send, q_e, k_e, b_e, sem)
     for copy in copies:
         copy.start()
-    for copy in copies:
-        copy.wait()
-    edge_fill(off[0], send, q_e, k_e, b_e)
+    ny = q_e.shape[0]
+    copies[0].wait()
+    k = window(k_e, (), off[0], ny)
+    copies[1].wait()
+    send[2] = window(b_e, (), off[0], ny)
+    copies[2].wait()
+    send[1] = k * q_e[...]
+    copies[3].wait()
 
 
 def receiver_sums(left, right_hi, right_lo, step, nz):

time: 29.8 us -> 29.8 us (level)
  no operation moved by 1% of the time
where the time goes in v7:
time: 29.8 us; the launch traced here: 29.4 us
  Pallas kernels  13.7 us (46%)
  starting transfers between devices  11.7 us (39%)
  between operations  2.77 us (9%)
  waiting for transfers between devices  1.2 us (4%)
    ppermute x1, starting transfers between devices, shards(): recv2_2 = lax.ppermute(send2_2, 'dom', swaps[1])  3.03 us
    ppermute x1, starting transfers between devices, shards(): recv_2 = lax.ppermute(send_2, 'dom', swaps[1])  2.99 us
    ppermute x1, starting transfers between devices, shards(): recv_e = lax.ppermute(other_e, 'shot', swap)  2.89 us
    pallas_call x1, Pallas kernels, shards(): pl.pallas_call(receivers, in_specs=[SM, VM, VM] + [ANY] * 4 + [VM], out_s...  2.78 us
    pallas_call x2, Pallas kernels, second_step(): pl.pallas_call(functools.partial(step_two, part), in_specs=[VM] * (11 + l...  2.72 us
    pallas_call x1, Pallas kernels, shards(): pl.pallas_call(step_one_ends, in_specs=[SM] * 4 + [ANY] + [VM] * 10, out_...  2.1 us
    pallas_call x1, Pallas kernels, shards(): pl.pallas_call(step_one_middle, in_specs=[SM] * 2 + [ANY] + [VM] * 12, ou...  1.7 us
    ppermute x1, starting transfers between devices, shards(): recv_1 = lax.ppermute(send_1, 'dom', swaps[0])  1.28 us
  transfers between devices with their start and end apart: 6, of which 2 were waited for; matrix products, arithmetic and copies ran while one was open for 0% of the time, Pallas kernels for 40%

profile of v7, /device:TPU:9, one launch (start us, length us, event | category | flops | bytes accessed | tf_op | source)
XLA Modules:
  0.0 29.4 jit_solution(15864951401754878769)
XLA Ops:
  1.3 0.0 copy-start.4
  1.3 0.0 copy-start.5
  1.3 1.1 %shard_map.121.after = f32[3,96,256]{2,1,0:T(8,128)S(1)} custom-call(s32[1]{0:T(128)S(6)} %copy.56.off, f32[1,2,8,96,256]{4,3,2,1,0:T(8,128)} %ckpt.19, f32[1,2,8,96,256]{4,3,2,1,0:T(8,128)} %adj.15, f32[8,128,256]{2,1,0:T(8,128)} %k_full.1, f32[8,128,256]{2,1,0:T(8,128)} %b_full.1), custom_call_target="tpu_custom_call" | custom-call | tf_op jit(solution)/shard_map/pallas_call | solution.py:567
  2.4 0.0 copy-start
  2.4 0.0 copy-start.1
  2.5 0.0 copy-start.2
  2.5 0.0 copy-start.3
  2.5 1.3 %collective-permute-start = (f32[3,96,256]{2,1,0:T(8,128)S(1)}, f32[3,96,256]{2,1,0:T(8,128)S(1)}, u32[]{:S(2)}, u32[]{:S(2)}) collective-permute-start(f32[3,96,256]{2,1,0:T(8,128)S(1)} %shard_map.121.after), channel_id=1, source_target_pairs={{0,2},{2,0},{4,6},{6,4},{8,10},{10,8},{12,14},{14,12},{1,3},{3,1},... | collective-permute-start | bytes 884744 | tf_op jit(solution)/shard_map/ppermute | solution.py:575
  3.8 0.0 copy-done.4
  3.8 0.0 copy-done.5
  3.8 2.8 %shard_map.122 = (f32[768,256]{1,0:T(8,128)S(1)}, f32[768,256]{1,0:T(8,128)S(1)}, f32[3,96,256]{2,1,0:T(8,128)S(1)}, bf16[768,1280]{1,0:T(8,128)(2,1)S(1)}, bf16...) custom-call(s32[1]{0:T(128)S(6)} %copy.56.off, s32[1,6400]{1,0:T(1,128)S(1)} %copy-done.5, ...), custom_call_target="tpu_custom_call" | custom-call | flops 40000000000 | bytes 1024 | tf_op jit(solution)/shard_map/pallas_call | solution.py:579
  6.5 3.0 %collective-permute-start.2 = (f32[3,96,256]{2,1,0:T(8,128)S(1)}, f32[3,96,256]{2,1,0:T(8,128)S(1)}, u32[]{:S(2)}, u32[]{:S(2)}) collective-permute-start(f32[3,96,256]{2,1,0:T(8,128)S(1)} %get-tuple-element.55.after), channel_id=1, source_target_pairs={{2,4},{4,2},{6,8},{8,6},{10,12},{12,10},{3,5},{5,3},{7,9},{9,7},{1... | collective-permute-start | bytes 884744 | tf_op jit(solution)/shard_map/ppermute | solution.py:593
  10.8 0.0 copy-done
  10.8 0.0 copy-done.1
  10.9 0.0 copy-done.2
  10.9 0.0 copy-done.3
  10.9 2.1 %shard_map.123 = (f32[8,96,256]{2,1,0:T(8,128)S(1)}, f32[8,96,256]{2,1,0:T(8,128)S(1)}, f32[8,96,256]{2,1,0:T(8,128)S(1)}, f32[8,96,256]{2,1,0:T(8,128)S(1)}, f3...) custom-call(s32[1]{0:T(128)S(6)} %copy.56.off, ...), custom_call_target="tpu_custom_call", output_to_operand_aliasing={{9}: (14, {})} | custom-call | flops 40000000000 | bytes 1024 | tf_op jit(solution)/shard_map/pallas_call | solution.py:595
  13.0 1.7 %shard_map.124 = (f32[8,96,256]{2,1,0:T(8,128)S(1)}, f32[8,96,256]{2,1,0:T(8,128)S(1)}, f32[8,96,256]{2,1,0:T(8,128)S(1)}, f32[8,96,256]{2,1,0:T(8,128)S(1)}, f3...) custom-call(s32[1]{0:T(128)S(6)} %copy.57.step, ...), custom_call_target="tpu_custom_call", output_to_operand_aliasing={{0}: (9, {}), {1}: (10, {}), {2}: (11, {}), {3}: (12, {}), ... | custom-call | flops 40000000000 | bytes 1024 | tf_op jit(solution)/shard_map/pallas_call | solution.py:621
  14.7 0.0 collective-permute-done.recv
  14.7 0.1 shard_map.125
  14.8 0.3 %collective-permute-start.1 = (f32[2,96,256]{2,1,0:T(8,128)S(1)}, f32[2,96,256]{2,1,0:T(8,128)S(1)}, u32[]{:S(2)}, u32[]{:S(2)}) collective-permute-start(f32[2,96,256]{2,1,0:T(8,128)S(1)} %get-tuple-element.73.send), channel_id=1, source_target_pairs={{0,2},{2,0},{4,6},{6,4},{8,10},{10,8},{12,14},{14,12},{1,3},{3,1},... | collective-permute-start | bytes 589832 | tf_op jit(solution)/shard_map/ppermute | solution.py:635
  15.1 2.0 %shard_map.127 = (f32[8,96,256]{2,1,0:T(8,128)S(1)}, f32[2,8,96,256]{3,2,1,0:T(8,128)S(1)}) custom-call(f32[1,2,8,96,256]{4,3,2,1,0:T(8,128)S(1)} %copy-done, f32[1,2,8,96,256]{4,3,2,1,0:T(8,128)S(1)} %copy-done.1, f32[8,96,256]{2,1,0:T(8,128)S(1)} %get-tuple-element.60.kq, f32[8,96,256]{2,1,0:T(8,128)S(1)} %get-tuple-element.62.hb, ...), custom_call_target="tpu_custom_call" | custom-call | flops 40000000000 | bytes 1024 | tf_op jit(solution)/shard_map/pallas_call | solution.py:639
  17.1 0.0 collective-permute-done.2.recv
  17.2 0.1 shard_map.126
  17.3 3.0 %collective-permute-start.4 = (f32[2,96,256]{2,1,0:T(8,128)S(1)}, f32[2,96,256]{2,1,0:T(8,128)S(1)}, u32[]{:S(2)}, u32[]{:S(2)}) collective-permute-start(f32[2,96,256]{2,1,0:T(8,128)S(1)} %get-tuple-element.91.send), channel_id=1, source_target_pairs={{2,4},{4,2},{6,8},{8,6},{10,12},{12,10},{3,5},{5,3},{7,9},{9,7},{1... | collective-permute-start | bytes 589832 | tf_op jit(solution)/shard_map/ppermute | solution.py:652
  20.3 0.7 %shard_map.128 = (f32[8,96,256]{2,1,0:T(8,128)S(1)}, f32[2,8,96,256]{3,2,1,0:T(8,128)S(1)}) custom-call(f32[1,2,8,96,256]{4,3,2,1,0:T(8,128)S(1)} %copy-done, f32[1,2,8,96,256]{4,3,2,1,0:T(8,128)S(1)} %copy-done.1, f32[8,96,256]{2,1,0:T(8,128)S(1)} %get-tuple-element.60.kq, ...), custom_call_target="tpu_custom_call", output_to_operand_aliasing={{0}: (11, {}), {1}: (12, {})} | custom-call | flops 2000000000 | bytes 1024 | tf_op jit(solution)/shard_map/pallas_call | solution.py:639
  21.0 0.8 %collective-permute-done.1.recv2 = f32[2,96,256]{2,1,0:T(8,128)S(1)} collective-permute-done((f32[2,96,256]{2,1,0:T(8,128)S(1)}, f32[2,96,256]{2,1,0:T(8,128)S(1)}, u32[]{:S(2)}, u32[]{:S(2)}) %collective-permute-start.1) | collective-permute-done | bytes 196640 | tf_op jit(solution)/shard_map/ppermute | solution.py:635
  21.9 1.2 %shard_map.129 = (f32[1,2,8,96,256]{4,3,2,1,0:T(8,128)}, f32[8,96,256]{2,1,0:T(8,128)S(1)}, f32[2,8,64,256]{3,2,1,0:T(8,128)S(1)}, f32[2,8,64,256]{3,2,1,0:T(8,128)S(1)}) custom-call(s32[1]{0:T(128)S(6)} %copy.56.off, f32[3,96,256]{2,1,0:T(8,128)S(1)} %collective-permute-done.recv, ...), custom_call_target="tpu_custom_call", output_to_operand_aliasing={{1}: (8, {})} | custom-call | flops 2000000000 | bytes 1024 | tf_op jit(solution)/shard_map/pallas_call | solution.py:655
  23.0 1.2 %collective-permute-start.3 = (f32[2,8,64,256]{3,2,1,0:T(8,128)S(1)}, f32[2,8,64,256]{3,2,1,0:T(8,128)S(1)}, u32[]{:S(2)}, u32[]{:S(2)}) collective-permute-start(f32[2,8,64,256]{3,2,1,0:T(8,128)S(1)} %get-tuple-element.90), channel_id=1, source_target_pairs={{0,1},{1,0},{2,3},{3,2},{4,5},{5,4},{6,7},{7,6},{8,9},{9,8},{10,11... | collective-permute-start | bytes 3145736 | tf_op jit(solution)/shard_map/ppermute | solution.py:668
  24.2 0.4 %collective-permute-done.4.recv2 = f32[2,96,256]{2,1,0:T(8,128)S(1)} collective-permute-done((f32[2,96,256]{2,1,0:T(8,128)S(1)}, f32[2,96,256]{2,1,0:T(8,128)S(1)}, u32[]{:S(2)}, u32[]{:S(2)}) %collective-permute-start.4) | collective-permute-done | bytes 196640 | tf_op jit(solution)/shard_map/ppermute | solution.py:652
  24.6 0.1 shard_map.130
  24.7 2.9 %collective-permute-start.5 = (f32[2,64,256]{2,1,0:T(8,128)S(1)}, f32[2,64,256]{2,1,0:T(8,128)S(1)}, u32[]{:S(2)}, u32[]{:S(2)}) collective-permute-start(f32[2,64,256]{2,1,0:T(8,128)S(1)} %get-tuple-element.97), channel_id=1, source_target_pairs={{0,1},{1,0},{2,3},{3,2},{4,5},{5,4},{6,7},{7,6},{8,9},{9,8},{10,11... | collective-permute-start | bytes 393224 | tf_op jit(solution)/shard_map/ppermute | solution.py:677
  27.6 0.0 collective-permute-done.3.recv
  27.6 1.0 %shard_map.131 = (f32[8,64,256]{2,1,0:T(8,128)}, f32[8,64,256]{2,1,0:T(8,128)}, f32[2,64,256]{2,1,0:T(8,128)S(1)}, f32[1,2,8,96,256]{4,3,2,1,0:T(8,128)}) custom-call(f32[2,8,64,256]{3,2,1,0:T(8,128)S(1)} %get-tuple-element.89.mine, f32[2,8,64,256]{3,2,1,0:T(8,128)S(1)} %collective-permute-done.3.recv, ...), custom_call_target="tpu_custom_call", output_to_operand_aliasing={{3}: (4, {})} | custom-call | flops 40000000000 | bytes 1024 | tf_op jit(solution)/shard_map/pallas_call | solution.py:678
  28.7 0.0 collective-permute-done.5.recv_e
  28.7 0.7 %shard_map.132 = (f32[8,64,256]{2,1,0:T(8,128)}, f32[8,64,256]{2,1,0:T(8,128)}) custom-call(f32[2,64,256]{2,1,0:T(8,128)S(1)} %get-tuple-element.96.sums_e, f32[2,64,256]{2,1,0:T(8,128)S(1)} %collective-permute-done.5.recv_e, f32[8,64,256]{2,1,0:T(8,128)} %get-tuple-element.98.grad_k_in, ...), custom_call_target="tpu_custom_call", output_to_operand_aliasing={{0}: (2, {}), {1}: (3, {})} | custom-call | tf_op jit(solution)/shard_map/pallas_call | solution.py:688
Async XLA Ops:
  1.3 2.5 %copy-start.4 = (f32[1,2,6400]{2,1,0:T(2,128)S(1)}, f32[1,2,6400]{2,1,0:T(2,128)}, u32[]{:S(2)}) copy-start(f32[1,2,6400]{2,1,0:T(2,128)} %res.1) | copy-start | bytes 153604
  1.3 2.5 %copy-start.5 = (s32[1,6400]{1,0:T(1,128)S(1)}, s32[1,6400]{1,0:T(1,128)}, u32[]{:S(2)}) copy-start(s32[1,6400]{1,0:T(1,128)} %rec.1) | copy-start | bytes 76804
  2.4 8.4 %copy-start = (f32[1,2,8,96,256]{4,3,2,1,0:T(8,128)S(1)}, f32[1,2,8,96,256]{4,3,2,1,0:T(8,128)}, u32[]{:S(2)}) copy-start(f32[1,2,8,96,256]{4,3,2,1,0:T(8,128)} %ckpt.19) | copy-start | bytes 4718596
  2.4 8.4 %copy-start.1 = (f32[1,2,8,96,256]{4,3,2,1,0:T(8,128)S(1)}, f32[1,2,8,96,256]{4,3,2,1,0:T(8,128)}, u32[]{:S(2)}) copy-start(f32[1,2,8,96,256]{4,3,2,1,0:T(8,128)} %adj.15) | copy-start | bytes 4718596
  2.5 8.4 %copy-start.2 = (f32[8,128,256]{2,1,0:T(8,128)S(1)}, f32[8,128,256]{2,1,0:T(8,128)}, u32[]{:S(2)}) copy-start(f32[8,128,256]{2,1,0:T(8,128)} %k_full.1) | copy-start | bytes 3145732
  2.5 8.4 %copy-start.3 = (f32[8,128,256]{2,1,0:T(8,128)S(1)}, f32[8,128,256]{2,1,0:T(8,128)}, u32[]{:S(2)}) copy-start(f32[8,128,256]{2,1,0:T(8,128)} %b_full.1) | copy-start | bytes 3145732
  2.5 12.2 %collective-permute-start = (f32[3,96,256]{2,1,0:T(8,128)S(1)}, f32[3,96,256]{2,1,0:T(8,128)S(1)}, u32[]{:S(2)}, u32[]{:S(2)}) collective-permute-start(f32[3,96,256]{2,1,0:T(8,128)S(1)} %shard_map.121.after), channel_id=1, source_target_pairs={{0,2},{2,0},{4,6},{6,4},{8,10},{10,8},{12,14},{14,12},{1,3},{3,1},... | collective-permute-start | bytes 884744 | tf_op jit(solution)/shard_map/ppermute | solution.py:575
  6.5 10.6 %collective-permute-start.2 = (f32[3,96,256]{2,1,0:T(8,128)S(1)}, f32[3,96,256]{2,1,0:T(8,128)S(1)}, u32[]{:S(2)}, u32[]{:S(2)}) collective-permute-start(f32[3,96,256]{2,1,0:T(8,128)S(1)} %get-tuple-element.55.after), channel_id=1, source_target_pairs={{2,4},{4,2},{6,8},{8,6},{10,12},{12,10},{3,5},{5,3},{7,9},{9,7},{1... | collective-permute-start | bytes 884744 | tf_op jit(solution)/shard_map/ppermute | solution.py:593
  14.8 7.0 %collective-permute-start.1 = (f32[2,96,256]{2,1,0:T(8,128)S(1)}, f32[2,96,256]{2,1,0:T(8,128)S(1)}, u32[]{:S(2)}, u32[]{:S(2)}) collective-permute-start(f32[2,96,256]{2,1,0:T(8,128)S(1)} %get-tuple-element.73.send), channel_id=1, source_target_pairs={{0,2},{2,0},{4,6},{6,4},{8,10},{10,8},{12,14},{14,12},{1,3},{3,1},... | collective-permute-start | bytes 589832 | tf_op jit(solution)/shard_map/ppermute | solution.py:635
  17.3 7.3 %collective-permute-start.4 = (f32[2,96,256]{2,1,0:T(8,128)S(1)}, f32[2,96,256]{2,1,0:T(8,128)S(1)}, u32[]{:S(2)}, u32[]{:S(2)}) collective-permute-start(f32[2,96,256]{2,1,0:T(8,128)S(1)} %get-tuple-element.91.send), channel_id=1, source_target_pairs={{2,4},{4,2},{6,8},{8,6},{10,12},{12,10},{3,5},{5,3},{7,9},{9,7},{1... | collective-permute-start | bytes 589832 | tf_op jit(solution)/shard_map/ppermute | solution.py:652
  23.0 4.6 %collective-permute-start.3 = (f32[2,8,64,256]{3,2,1,0:T(8,128)S(1)}, f32[2,8,64,256]{3,2,1,0:T(8,128)S(1)}, u32[]{:S(2)}, u32[]{:S(2)}) collective-permute-start(f32[2,8,64,256]{3,2,1,0:T(8,128)S(1)} %get-tuple-element.90), channel_id=1, source_target_pairs={{0,1},{1,0},{2,3},{3,2},{4,5},{5,4},{6,7},{7,6},{8,9},{9,8},{10,11... | collective-permute-start | bytes 3145736 | tf_op jit(solution)/shard_map/ppermute | solution.py:668
  24.7 3.9 %collective-permute-start.5 = (f32[2,64,256]{2,1,0:T(8,128)S(1)}, f32[2,64,256]{2,1,0:T(8,128)S(1)}, u32[]{:S(2)}, u32[]{:S(2)}) collective-permute-start(f32[2,64,256]{2,1,0:T(8,128)S(1)} %get-tuple-element.97), channel_id=1, source_target_pairs={{0,1},{1,0},{2,3},{3,2},{4,5},{5,4},{6,7},{7,6},{8,9},{9,8},{10,11... | collective-permute-start | bytes 393224 | tf_op jit(solution)/shard_map/ppermute | solution.py:677
